TPU v7x, 32 devices: a whole 2x2x4 slice. The times are simulated.
32 devices in a mesh: dir: 2 (over x), group: 4 (over y, core), dp: 4 (over z).
Axes of the slice: x: 2, y: 2, z: 4, core: 2. Of those that a mesh axis runs over, the one named last changes fastest.
Arguments:
- chars: int32 [2, 384, 24], P('dir', ('group', 'dp')), may hold values from 0 to 274
- targets: int32 [2, 384, 24], P('dir', ('group', 'dp')), may hold values from 0 to 274
- resets: int32 [2, 384, 24], P('dir', ('group', 'dp')), may hold values 0 or 1
- word_pos: int32 [2, 384, 8], P('dir', ('group', 'dp')), may hold values from -1 to 23, as said below
- h_init: float32 [2, 384, 2048], P('dir', ('group', 'dp')), may hold values from -0.9 to 0.9
- c_init: float32 [2, 384, 2048], P('dir', ('group', 'dp')), may hold values from -5 to 5
- word_grad: bfloat16 [384, 8, 4096], P(('group', 'dp'), None, 'dir'), may hold values from -0.119628906 to 0.119628906
- w_emb: float32 [2, 275, 100], P('dir'), may hold values from -5 to 5
- w_in: float32 [2, 100, 8192], P('dir', None, 'group'), may hold values from -0.625 to 0.625
- w_rec: float32 [2, 2048, 8192], P('dir', 'group'), may hold values from -0.125 to 0.125
- b_rec: float32 [2, 8192], P('dir', 'group'), may hold values from -3 to 3
- w_dec: float32 [2, 2048, 275], P('dir', 'group'), may hold values from -0.5 to 0.5
- b_dec: float32 [2, 275], P('dir'), may hold values from -4 to 4
- mom_emb: float32 [2, 275, 100], P('dir'), may hold values from -0.00048828125 to 0.00048828125
- mom_in: float32 [2, 100, 8192], P('dir', None, 'group'), may hold values from -0.00048828125 to 0.00048828125
- mom_rec: float32 [2, 2048, 8192], P('dir', 'group'), may hold values from -0.00048828125 to 0.00048828125
- mom_bias: float32 [2, 8192], P('dir', 'group'), may hold values from -0.00048828125 to 0.00048828125
- mom_dec: float32 [2, 2048, 275], P('dir', 'group'), may hold values from -0.00048828125 to 0.00048828125
- mom_dbias: float32 [2, 275], P('dir'), may hold values from -0.00048828125 to 0.00048828125
Outputs:
- losses: float32 [2], P('dir')
- word_vectors: bfloat16 [384, 8, 4096], P(('group', 'dp'), 'dir')
- grad_h: float32 [2, 384, 2048], P('dir', ('group', 'dp'))
- grad_c: float32 [2, 384, 2048], P('dir', ('group', 'dp'))
- grad_emb: float32 [2, 275, 100], P('dir')
- grad_in: float32 [2, 100, 8192], P('dir', None, 'group')
- grad_rec: float32 [2, 2048, 8192], P('dir', 'group')
- grad_bias: float32 [2, 8192], P('dir', 'group')
- grad_dec: float32 [2, 2048, 275], P('dir', 'group')
- grad_dbias: float32 [2, 275], P('dir')
- next_mom_emb: float32 [2, 275, 100], P('dir')
- next_mom_in: float32 [2, 100, 8192], P('dir', None, 'group')
- next_mom_rec: float32 [2, 2048, 8192], P('dir', 'group')
- next_mom_bias: float32 [2, 8192], P('dir', 'group')
- next_mom_dec: float32 [2, 2048, 275], P('dir', 'group')
- next_mom_dbias: float32 [2, 275], P('dir')
Inputs may be any that keep to these rules, and one draw needn't show every extreme that they name: `word_pos`: for each model and segment the used slots come first and name distinct positions in increasing order; the other slots hold -1. Both models use the same number of slots in a segment; the first segment of each aligned block of 24 segments uses all 8.
All inputs are finite; a program needn't handle non-finite values. No bound on the sum of `resets` on one device may be relied on, other than what follows from the above.
Results may differ from a plain program's by a relative error of at most 0.012.
Values may be sent and summed in bfloat16 or wider, within the bound.
A program may use at most 256 MiB of HBM per device.

v0:
```python
import jax
import jax.numpy as jnp
from jax import lax
from jax.sharding import PartitionSpec as P


def partner(value, axis, bit):
    mask = 2**bit
    pairs = [(source, source ^ mask) for source in range(lax.axis_size(axis))]
    return lax.ppermute(value, axis, pairs)


def momentum_step(moment, gradient, clip_scale):
    return 0.9 * moment + clip_scale * gradient


def squares_of(arrays):
    total_sq = jnp.zeros((), jnp.float32)
    for array in arrays:
        total_sq = total_sq + jnp.sum(array * array)
    return total_sq


def shards(
    chars,
    targets,
    resets,
    word_pos,
    h_init,
    c_init,
    word_grad,
    w_emb,
    w_in,
    w_rec,
    b_rec,
    w_dec,
    b_dec,
    mom_emb,
    mom_in,
    mom_rec,
    mom_bias,
    mom_dec,
    mom_dbias,
):
    vocab_size = w_emb.shape[1]
    seg_len = chars.shape[2]
    batch_size = chars.shape[1]
    hidden_size = w_rec.shape[2] // 4
    in_full, rec_full, bias_full, dec_full = (
        lax.all_gather(w_in[0].astype(jnp.bfloat16), "group", axis=1, tiled=True),
        lax.all_gather(w_rec[0].astype(jnp.bfloat16), "group", axis=0, tiled=True),
        lax.all_gather(b_rec[0].astype(jnp.bfloat16), "group", axis=0, tiled=True),
        lax.all_gather(w_dec[0].astype(jnp.bfloat16), "group", axis=0, tiled=True),
    )
    char_major = jnp.transpose(chars[0])
    char_onehot = (char_major[:, :, None] == jnp.arange(vocab_size, dtype=jnp.int32)).astype(
        jnp.bfloat16
    )
    embedded = jnp.einsum(
        "tbv,ve->tbe",
        char_onehot,
        w_emb[0].astype(jnp.bfloat16),
        preferred_element_type=jnp.float32,
    ).astype(jnp.bfloat16)
    projected = jnp.einsum(
        "tbe,eg->tbg", embedded, in_full, preferred_element_type=jnp.float32
    ) + bias_full.astype(jnp.float32)
    keep_major = (1 - jnp.transpose(resets[0])).astype(jnp.float32)

    def advance(state_pair, step_feed):
        hidden_prev, cell_prev = state_pair
        proj_step, keep_step = step_feed
        hidden_kept = hidden_prev * keep_step[:, None].astype(jnp.bfloat16)
        cell_kept = cell_prev * keep_step[:, None]
        preact = proj_step + jnp.dot(hidden_kept, rec_full, preferred_element_type=jnp.float32)
        gate_in = jax.nn.sigmoid(preact[:, :hidden_size])
        gate_forget = jax.nn.sigmoid(preact[:, hidden_size : 2 * hidden_size])
        gate_cell = jnp.tanh(preact[:, 2 * hidden_size : 3 * hidden_size])
        gate_out = jax.nn.sigmoid(preact[:, 3 * hidden_size :])
        cell_next = gate_forget * cell_kept + gate_in * gate_cell
        hidden_next = (gate_out * jnp.tanh(cell_next)).astype(jnp.bfloat16)
        gate_acts = jnp.concatenate([gate_in, gate_forget, gate_cell, gate_out], axis=-1)
        return (
            (hidden_next, cell_next),
            (hidden_kept, cell_kept, gate_acts, cell_next, hidden_next),
        )

    start_pair = (h_init[0].astype(jnp.bfloat16), c_init[0])
    final_pair, stored = lax.scan(advance, start_pair, (projected, keep_major))
    kept_all, cellkept_all, gate_all, cell_all, hidden_all = stored
    logits = (
        jnp.einsum("tbh,hv->tbv", hidden_all, dec_full, preferred_element_type=jnp.float32)
        + b_dec[0]
    )
    log_probs = jax.nn.log_softmax(logits, axis=-1)
    target_onehot = (
        jnp.transpose(targets[0])[:, :, None] == jnp.arange(vocab_size, dtype=jnp.int32)
    ).astype(jnp.float32)
    loss_part = -jnp.sum(log_probs * target_onehot)
    logit_grad = ((jnp.exp(log_probs) - target_onehot) / seg_len).astype(jnp.bfloat16)
    from_output = jnp.einsum(
        "tbv,hv->tbh", logit_grad, dec_full, preferred_element_type=jnp.float32
    )
    pos_onehot = (word_pos[0][:, :, None] == jnp.arange(seg_len, dtype=jnp.int32)).astype(
        jnp.bfloat16
    )
    picked = jnp.einsum(
        "bkt,tbh->bkh", pos_onehot, hidden_all, preferred_element_type=jnp.float32
    ).astype(jnp.bfloat16)
    from_words = jnp.einsum(
        "bkt,bkh->tbh", pos_onehot, word_grad, preferred_element_type=jnp.float32
    )
    half_slots = picked.shape[1] // 2
    model_index = lax.axis_index("dir")
    own_slots = lax.dynamic_slice_in_dim(picked, model_index * half_slots, half_slots, 1)
    other_slots = lax.dynamic_slice_in_dim(picked, (1 - model_index) * half_slots, half_slots, 1)
    partner_half = partner(other_slots, "dir", 0)
    leading = model_index == 0
    word_vectors = jnp.where(
        leading,
        jnp.concatenate([own_slots, partner_half], axis=-1),
        jnp.concatenate([partner_half, own_slots], axis=-1),
    )

    def retreat(state_pair, step_feed):
        grad_hidden, grad_cell = state_pair
        out_grad, gate_acts, cell_now, cell_kept, keep_step = step_feed
        gate_in = gate_acts[:, :hidden_size]
        gate_forget = gate_acts[:, hidden_size : 2 * hidden_size]
        gate_cell = gate_acts[:, 2 * hidden_size : 3 * hidden_size]
        gate_out = gate_acts[:, 3 * hidden_size :]
        total_hidden = grad_hidden + out_grad
        tanh_cell = jnp.tanh(cell_now)
        total_cell = grad_cell + total_hidden * gate_out * (1.0 - tanh_cell * tanh_cell)
        pre_grad = jnp.concatenate(
            [
                total_cell * gate_cell * gate_in * (1.0 - gate_in),
                total_cell * cell_kept * gate_forget * (1.0 - gate_forget),
                total_cell * gate_in * (1.0 - gate_cell * gate_cell),
                total_hidden * tanh_cell * gate_out * (1.0 - gate_out),
            ],
            axis=-1,
        ).astype(jnp.bfloat16)
        back_hidden = lax.dot_general(
            pre_grad, rec_full, (((1,), (1,)), ((), ())), preferred_element_type=jnp.float32
        )
        keep_col = keep_step[:, None]
        return ((back_hidden * keep_col, total_cell * gate_forget * keep_col), pre_grad)

    zero_state = jnp.zeros((batch_size, hidden_size), jnp.float32)
    start_grads, pre_all = lax.scan(
        retreat,
        (zero_state, zero_state),
        (from_output + from_words, gate_all, cell_all, cellkept_all, keep_major),
        reverse=True,
    )
    grad_hidden0, grad_cell0 = start_grads
    rec_grad = jnp.einsum("tbh,tbg->hg", kept_all, pre_all, preferred_element_type=jnp.float32)
    in_grad = jnp.einsum("tbe,tbg->eg", embedded, pre_all, preferred_element_type=jnp.float32)
    bias_grad = jnp.sum(pre_all, axis=(0, 1), dtype=jnp.float32)
    dec_grad = jnp.einsum("tbh,tbv->hv", hidden_all, logit_grad, preferred_element_type=jnp.float32)
    dbias_grad = jnp.sum(logit_grad, axis=(0, 1), dtype=jnp.float32)
    embed_in = jnp.einsum("tbg,eg->tbe", pre_all, in_full, preferred_element_type=jnp.float32)
    emb_grad = jnp.einsum(
        "tbv,tbe->ve", char_onehot.astype(jnp.float32), embed_in, precision=lax.Precision.HIGHEST
    )
    loss_part = jnp.reshape(loss_part, (1,))
    in_sum, rec_sum, bias_sum, dec_sum = (
        lax.psum_scatter(
            in_grad.astype(jnp.bfloat16), "group", scatter_dimension=1, tiled=True
        ).astype(jnp.float32),
        lax.psum_scatter(
            rec_grad.astype(jnp.bfloat16), "group", scatter_dimension=0, tiled=True
        ).astype(jnp.float32),
        lax.psum_scatter(
            bias_grad.astype(jnp.bfloat16), "group", scatter_dimension=0, tiled=True
        ).astype(jnp.float32),
        lax.psum_scatter(
            dec_grad.astype(jnp.bfloat16), "group", scatter_dimension=0, tiled=True
        ).astype(jnp.float32),
    )
    in_sum, rec_sum, bias_sum, dec_sum, emb_sum, dbias_sum, loss_sum = (
        lax.psum(in_sum.astype(jnp.bfloat16), "dp").astype(jnp.float32),
        lax.psum(rec_sum.astype(jnp.bfloat16), "dp").astype(jnp.float32),
        lax.psum(bias_sum.astype(jnp.bfloat16), "dp").astype(jnp.float32),
        lax.psum(dec_sum.astype(jnp.bfloat16), "dp").astype(jnp.float32),
        lax.psum(emb_grad.astype(jnp.bfloat16), "dp").astype(jnp.float32),
        lax.psum(dbias_grad.astype(jnp.bfloat16), "dp").astype(jnp.float32),
        lax.psum(loss_part.astype(jnp.bfloat16), "dp").astype(jnp.float32),
    )
    shard_sq = squares_of((in_sum, rec_sum, bias_sum, dec_sum))
    shard_sq, emb_sum, dbias_sum, loss_sum = (
        lax.psum(shard_sq.astype(jnp.bfloat16), "group").astype(jnp.float32),
        lax.psum(emb_sum.astype(jnp.bfloat16), "group").astype(jnp.float32),
        lax.psum(dbias_sum.astype(jnp.bfloat16), "group").astype(jnp.float32),
        lax.psum(loss_sum.astype(jnp.bfloat16), "group").astype(jnp.float32),
    )
    total_sq = shard_sq + squares_of((emb_sum, dbias_sum))
    clip_scale = 0.25 / jnp.maximum(jnp.sqrt(total_sq), 0.25)
    mom_in_next = momentum_step(mom_in[0], in_sum, clip_scale)
    mom_rec_next = momentum_step(mom_rec[0], rec_sum, clip_scale)
    mom_bias_next = momentum_step(mom_bias[0], bias_sum, clip_scale)
    mom_dec_next = momentum_step(mom_dec[0], dec_sum, clip_scale)
    mom_emb_next = momentum_step(mom_emb[0], emb_sum, clip_scale)
    mom_dbias_next = momentum_step(mom_dbias[0], dbias_sum, clip_scale)
    token_count = seg_len * batch_size * lax.axis_size("group") * lax.axis_size("dp")
    losses = loss_sum / token_count
    return (
        losses,
        word_vectors,
        grad_hidden0[None],
        grad_cell0[None],
        emb_sum[None],
        in_sum[None],
        rec_sum[None],
        bias_sum[None],
        dec_sum[None],
        dbias_sum[None],
        mom_emb_next[None],
        mom_in_next[None],
        mom_rec_next[None],
        mom_bias_next[None],
        mom_dec_next[None],
        mom_dbias_next[None],
    )


def solution(mesh):
    return jax.shard_map(
        shards,
        mesh=mesh,
        in_specs=(
            P("dir", ("group", "dp"), None),
            P("dir", ("group", "dp"), None),
            P("dir", ("group", "dp"), None),
            P("dir", ("group", "dp"), None),
            P("dir", ("group", "dp"), None),
            P("dir", ("group", "dp"), None),
            P(("group", "dp"), None, "dir"),
            P("dir", None, None),
            P("dir", None, "group"),
            P("dir", "group", None),
            P("dir", "group"),
            P("dir", "group", None),
            P("dir", None),
            P("dir", None, None),
            P("dir", None, "group"),
            P("dir", "group", None),
            P("dir", "group"),
            P("dir", "group", None),
            P("dir", None),
        ),
        out_specs=(
            P("dir"),
            P(("group", "dp"), "dir", None),
            P("dir", ("group", "dp"), None),
            P("dir", ("group", "dp"), None),
            P("dir", None, None),
            P("dir", None, "group"),
            P("dir", "group", None),
            P("dir", "group"),
            P("dir", "group", None),
            P("dir", None),
            P("dir", None, None),
            P("dir", None, "group"),
            P("dir", "group", None),
            P("dir", "group"),
            P("dir", "group", None),
            P("dir", None),
        ),
        check_vma=False,
    )
```

profile of v0, /device:TPU:0, one launch (start us, length us, event | category | flops | bytes accessed | tf_op | source)
XLA Modules:
  0.0 1784.0 jit_solution(6551655441645200572)
XLA Ops:
  43.9 193.3 %all-gather.10.cloned.1.call-done = bf16[1,2048,8192]{2,1,0:T(8,128)(2,1)} async-done(((bf16[1,512,8192]{2,1,0:T(8,128)(2,1)}), bf16[1,2048,8192]{2,1,0:T(8,128)(2,1)}) %all-gather.10.cloned.1.call-update) | async-done | bytes 33554448 | tf_op jit(solution)/shard_map/all_gather | solution.py:51
  237.2 402.9 %while.41 = (s32[]{:T(128)}, bf16[24,2048]{1,0:T(8,128)(2,1)S(1)}, f32[24,2048]{1,0:T(8,128)S(1)}, bf16[24,24,2048]{2,1,0:T(8,128)(2,1)}, f32[24,24,2048]{2,1,0:...) while((s32[]{:T(128)}, bf16[24,2048]{1,0:T(8,128)(2,1)S(1)}, ...), condition=%wide.region_1.2_spmd, body=%wide.region_0.1_spmd.sunk | while | flops 807567360 | bytes 41126540 | solution.py:89
  664.0 449.7 %while.42 = (s32[]{:T(128)}, f32[24,2048]{1,0:T(8,128)S(1)}, f32[24,2048]{1,0:T(8,128)S(1)}, bf16[24,24,8192]{2,1,0:T(8,128)(2,1)}, f32[24,24,2048]{2,1,0:T(8,12...) while((s32[]{:T(128)}, f32[24,2048]{1,0:T(8,128)S(1)}, ...), condition=%wide.region_8.9_spmd.clone, body=%wide.region_7.8_spmd.clone.sunk | while | flops 809975808 | bytes 39453220 | solution.py:151
  668.2 14.6 convolution_multiply_fusion.2
  687.0 14.5 convolution_multiply_fusion.2
  705.7 14.5 convolution_multiply_fusion.2
  724.5 14.5 convolution_multiply_fusion.2
  743.2 14.5 convolution_multiply_fusion.2
  761.9 14.5 convolution_multiply_fusion.2
  780.7 14.5 convolution_multiply_fusion.2
  799.4 14.5 convolution_multiply_fusion.2
  818.1 14.5 convolution_multiply_fusion.2
  836.9 14.5 convolution_multiply_fusion.2
  855.6 14.5 convolution_multiply_fusion.2
  874.4 14.5 convolution_multiply_fusion.2
  893.1 14.5 convolution_multiply_fusion.2
  911.8 14.5 convolution_multiply_fusion.2
  930.6 14.5 convolution_multiply_fusion.2
  949.3 14.5 convolution_multiply_fusion.2
  968.0 14.5 convolution_multiply_fusion.2
  1121.0 32.6 %bitcast_convert_fusion = bf16[2048,8192]{1,0:T(8,128)(2,1)} fusion(bf16[24,24,2048]{2,1,0:T(8,128)(2,1)} %get-tuple-element.284, bf16[24,24,8192]{2,1,0:T(8,128)(2,1)} %get-tuple-element.283), kind=kOutput, calls=%fused_computation.58 | convolution fusion | flops 19344130048 | bytes 45350912 | tf_op jit(solution)/shard_map/tbh,tbg->hg/dot_general | solution.py:158
  1154.0 234.6 %reduce-scatter.10.cloned.1.call-done = bf16[512,8192]{1,0:T(8,128)(2,1)} async-done(((bf16[2048,8192]{1,0:T(8,128)(2,1)}), bf16[512,8192]{1,0:T(8,128)(2,1)}) %reduce-scatter.10.cloned.1.call-update) | async-done | bytes 8388624
  1419.9 25.6 %all-reduce.2 = (bf16[1]{0:T(256)(128)(2,1)}, bf16[275]{0:T(512)(128)(2,1)S(1)}, bf16[2048]{0:T(1024)(128)(2,1)S(1)}, bf16[275,100]{1,0:T(8,128)(2,1)S(1)}) all-reduce(bf16[1]{0:T(256)(128)(2,1)} %bitcast.21, bf16[275]{0:T(512)(128)(2,1)S(1)} %get-tuple-element.410, ...), channel_id=1, replica_groups=mesh['dir'=2,'group'=4,'dp'=4] {'dp'}, use_global_device_ids=true, to_apply=%region_5.6 | all-reduce | flops 29824 | bytes 119296 | tf_op jit(solution)/shard_map/psum | solution.py:189
  1448.2 261.0 %all-reduce.7.cloned.1.call-done = (bf16[100,2048]{1,0:T(8,128)(2,1)}, bf16[512,8192]{1,0:T(8,128)(2,1)}, bf16[512,275]{0,1:T(8,128)(2,1)}) async-done(((bf16[100,2048]{1,0:T(8,128)(2,1)}, bf16[512,8192]{1,0:T(8,128)(2,1)}, bf16[512,275]{0,1:T(8,128)(2,1)}), (bf16[100,2048]{1,0:T(8,128)(2,1)}, bf16[512,8192]{1,0:T(8,128)(2,1)}, bf16[512,275]{0,1:T(8,128)(2,1)})) %all-reduce.7.cloned.1.call-update) | async-done | bytes 9079824 | tf_op jit(solution)/shard_map/psum | solution.py:183
  (463 shorter events, 764.7 us)
Async XLA Ops:
  7.2 20.5 %copy-start = (bf16[24,8,2048]{2,1,0:T(8,128)(2,1)S(1)}, bf16[24,8,2048]{2,1,0:T(8,128)(2,1)}, u32[]{:S(2)}) copy-start(bf16[24,8,2048]{2,1,0:T(8,128)(2,1)} %param.29) | copy-start | bytes 2359300
  7.2 26.3 %all-gather.8.cloned.1.call-start = ((), (), s32[]{:S(2)}) async-start(), calls=%async_computation.5 | async-start | bytes 2129920 | tf_op jit(solution)/shard_map/all_gather | solution.py:50
  9.5 227.7 %all-gather.10.cloned.1.call-start = ((), (), s32[]{:S(2)}) async-start(), calls=%async_computation.6 | async-start | bytes 41943040 | tf_op jit(solution)/shard_map/all_gather | solution.py:51
  18.5 8.7 copy-start.21
  18.5 8.8 copy-start.24
  18.5 9.2 copy-start.26
  18.5 621.5 %all-gather.12.cloned.1.call-start = ((), (), s32[]{:S(2)}) async-start(), calls=%async_computation.7 | async-start | bytes 1433600 | tf_op jit(solution)/shard_map/all_gather | solution.py:53
  20.3 1133.7 %reduce-scatter.8.cloned.1.call-start = ((), (), s32[]{:S(2)}) async-start(), calls=%async_computation.4 | async-start | bytes 1433600 | tf_op jit(solution)/shard_map/reduce_scatter | solution.py:178
  33.5 203.7 %copy-start.2 = (f32[1,24,2048]{2,1,0:T(8,128)S(1)}, f32[1,24,2048]{2,1,0:T(8,128)}, u32[]{:S(2)}) copy-start(f32[1,24,2048]{2,1,0:T(8,128)} %param.28) | copy-start | bytes 589828
  651.1 502.9 %reduce-scatter.6.cloned.1.call-start = ((), (), s32[]{:S(2)}) async-start(), calls=%async_computation.3 | async-start | bytes 2129920 | tf_op jit(solution)/shard_map/reduce_scatter | solution.py:169
  1120.7 267.9 %reduce-scatter.10.cloned.1.call-start = ((), (), s32[]{:S(2)}) async-start(), calls=%async_computation.8 | async-start | bytes 41943040
  1153.6 235.0 %copy-start.27 = (u32[32]{0:T(128)S(1)}, u32[32]{0:T(128)}, u32[]{:S(2)}) copy-start(u32[32]{0:T(128)} %constant.137) | copy-start | bytes 388
  1153.6 236.3 %copy-start.25 = (f32[1,275]{1,0:T(1,128)S(1)}, f32[1,275]{1,0:T(1,128)}, u32[]{:S(2)}) copy-start(f32[1,275]{1,0:T(1,128)} %param.41) | copy-start | bytes 3304
  1153.6 236.3 %copy-start.23 = (f32[1,2048]{1,0:T(1,128)S(1)}, f32[1,2048]{1,0:T(1,128)}, u32[]{:S(2)}) copy-start(f32[1,2048]{1,0:T(1,128)} %param.39) | copy-start | bytes 24580
  1153.6 236.3 %copy-start.7 = (bf16[24,24,2048]{2,1,0:T(8,128)(2,1)S(1)}, bf16[24,24,2048]{2,1,0:T(8,128)(2,1)}, u32[]{:S(2)}) copy-start(bf16[24,24,2048]{2,1,0:T(8,128)(2,1)} %get-tuple-element.277) | copy-start | bytes 7077892
  1153.7 236.3 %copy-start.17 = (s32[24,8]{1,0:T(8,128)S(1)}, s32[24,8]{1,0:T(8,128)}, u32[]{:S(2)}) copy-start(s32[24,8]{1,0:T(8,128)} %copy-done.16) | copy-start | bytes 2308
  1153.7 555.6 %all-reduce.7.cloned.1.call-start = ((), (), s32[]{:S(2)}) async-start(), calls=%async_computation.9 | async-start | bytes 18202624 | tf_op jit(solution)/shard_map/psum | solution.py:183
  1393.5 53.2 %collective-permute-start = (bf16[24,4,2048]{2,1,0:T(4,128)(2,1)S(1)}, bf16[24,4,2048]{2,1,0:T(4,128)(2,1)S(1)}, u32[]{:S(2)}, u32[]{:S(2)}) collective-permute-start(bf16[24,4,2048]{2,1,0:T(4,128)(2,1)S(1)} %get-tuple-element.423), channel_id=1, source_target_pairs={{0,16},{16,0},{1,17},{17,1},{2,18},{18,2},{3,19},{19,3},{4,20},{20... | collective-permute-start | bytes 1179656 | tf_op jit(solution)/shard_map/ppermute | solution.py:10
  1401.1 17.7 copy-start.19
  1709.3 9.2 copy-start.6
  1736.9 14.6 copy-start.12
  1753.5 14.4 copy-start.10
  1753.5 16.5 copy-start.15
  1753.6 21.9 %copy-start.1 = (bf16[24,8,2048]{2,1,0:T(8,128)(2,1)S(1)}, bf16[24,8,2048]{2,1,0:T(8,128)(2,1)}, u32[]{:S(2)}) copy-start(bf16[24,8,2048]{2,1,0:T(8,128)(2,1)} %param.29) | copy-start | bytes 2359300
  (12 other events, 62.7 us)
Sparse Core Ops, SparseCore 0:
  10.2 23.2 all-gather.7
  35.6 201.5 all-gather.9
  239.3 17.2 all-gather.11
  651.3 25.4 reduce-scatter.7
  1120.8 28.9 reduce-scatter.5
  1153.7 234.8 reduce-scatter.9
  1391.4 317.8 all-reduce.6
where the time goes:
time: 1790 us; the launch traced here: 1780 us
  matrix products  746 us (42%)
  waiting for transfers between devices  691 us (39%)
  other arithmetic  215 us (12%)
  blocking collectives  56.1 us (3%)
  local copies, waits for them, and re-layouts  48.3 us (3%)
  between operations  22.8 us (1%)
    dot_general x24, matrix products, retreat(): lax.dot_general(pre_grad, rec_full, (((1,), (1,)), ((), ())), preferred_e...  349 us
    dot_general x24, matrix products, advance(): jnp.dot(hidden_kept, rec_full, preferred_element_type=jnp.float32)  318 us
    psum x1, waiting for transfers between devices, shards(): lax.psum(in_sum.astype(jnp.bfloat16), 'dp').astype(jnp.float32)  261 us
    unnamed x8, waiting for transfers between devices  235 us
    all_gather x1, waiting for transfers between devices, shards(): lax.all_gather(w_rec[0].astype(jnp.bfloat16), 'group', axis=0, tiled=True)  193 us
    dynamic_update_slice x96, other arithmetic, shards(): final_pair, stored = lax.scan(advance, start_pair, (projected, keep_major))  78.7 us
  transfers between devices with their start and end apart: 8, of which 4 were waited for; matrix products, arithmetic and copies ran while one was open for 53% of the time, Pallas kernels for 0%

commit v1 on v0

v1 whole, which is shorter than its diff:
```python
import functools

import jax
import jax.numpy as jnp
from jax import lax
from jax.experimental import pallas as pl
from jax.experimental.pallas import tpu as pltpu
from jax.sharding import PartitionSpec as P

MESH = pl.DeviceIdType.MESH
CHUNK = 256


def partner(value, axis, bit):
    mask = 2**bit
    pairs = [(source, source ^ mask) for source in range(lax.axis_size(axis))]
    return lax.ppermute(value, axis, pairs)


def momentum_step(moment, gradient, clip_scale):
    return 0.9 * moment + clip_scale * gradient


def squares_of(arrays):
    total_sq = jnp.zeros((), jnp.float32)
    for array in arrays:
        total_sq = total_sq + jnp.sum(array * array)
    return total_sq


def sigmoid(value):
    return 0.5 * jnp.tanh(0.5 * value) + 0.5


def core_peer():
    group = lax.axis_index("group")
    core = lax.rem(group, 2)
    return core, (lax.axis_index("dir"), group + 1 - 2 * core, lax.axis_index("dp"))


def greet(peers):
    barrier = pltpu.get_barrier_semaphore()
    for peer in peers:
        pl.semaphore_signal(barrier, inc=1, device_id=peer, device_id_type=MESH)
    pl.semaphore_wait(barrier, len(peers))


def forward_kernel(
    steps,
    emb_ref,
    keep_ref,
    h0_ref,
    c0_ref,
    w_hbm,
    hid_ref,
    kept_ref,
    gates_ref,
    cell_ref,
    ckept_ref,
    w_ref,
    hown,
    hpar,
    kown,
    kpar,
    cell,
    acc,
    w_sem,
    send_sem,
    recv_sem,
):
    t = pl.program_id(0)
    slot = lax.rem(t, 2)
    nxt = 1 - slot
    core, peer = core_peer()
    units = cell.shape[1]
    hidden = 2 * units
    chunks = units // CHUNK
    own0 = pl.multiple_of(core * units, units)
    par0 = pl.multiple_of((1 - core) * units, units)

    def exchange(which, u):
        return pltpu.make_async_remote_copy(
            src_ref=hown.at[which, u],
            dst_ref=hpar.at[which, u],
            send_sem=send_sem.at[which, u],
            recv_sem=recv_sem.at[which, u],
            device_id=peer,
            device_id_type=MESH,
        )

    @pl.when(t == 0)
    def _():
        copy = pltpu.make_async_copy(w_hbm, w_ref, w_sem)
        copy.start()
        greet([peer])
        for u in range(chunks):
            hown[0, u] = h0_ref[:, pl.ds(pl.multiple_of(own0 + u * CHUNK, CHUNK), CHUNK)]
            hpar[0, u] = h0_ref[:, pl.ds(pl.multiple_of(par0 + u * CHUNK, CHUNK), CHUNK)]
        cell[...] = c0_ref[...]
        copy.wait()

    keep = keep_ref[0][:, :1]
    keep_b = keep.astype(jnp.bfloat16)

    def early(u):
        for q in range(4):
            cols = pl.ds(q * units + u * CHUNK, CHUNK)
            acc[q, u] = jnp.dot(
                emb_ref[0], w_ref[hidden:, cols], preferred_element_type=jnp.float32
            ) + jnp.dot(kown[...], w_ref[pl.ds(own0, units), cols], preferred_element_type=jnp.float32)

    def late(u):
        pre = []
        for q in range(4):
            cols = pl.ds(q * units + u * CHUNK, CHUNK)
            pre.append(
                acc[q, u]
                + jnp.dot(kpar[...], w_ref[pl.ds(par0, units), cols], preferred_element_type=jnp.float32)
            )
        span = pl.ds(u * CHUNK, CHUNK)
        gate_in, gate_forget, gate_cell, gate_out = (
            sigmoid(pre[0]),
            sigmoid(pre[1]),
            jnp.tanh(pre[2]),
            sigmoid(pre[3]),
        )
        kept_cell = cell[:, span] * keep
        cell_next = gate_forget * kept_cell + gate_in * gate_cell
        hown[nxt, u] = (gate_out * jnp.tanh(cell_next)).astype(jnp.bfloat16)
        cell[:, span] = cell_next
        gates_ref[0, 0, :, span] = gate_in
        gates_ref[0, 1, :, span] = gate_forget
        gates_ref[0, 2, :, span] = gate_cell
        gates_ref[0, 3, :, span] = gate_out
        cell_ref[0, :, span] = cell_next
        ckept_ref[0, :, span] = kept_cell
        exchange(nxt, u).start()

    @pl.when(t < steps)
    def _():
        for u in range(chunks):
            kown[:, pl.ds(u * CHUNK, CHUNK)] = hown[slot, u] * keep_b
        early(0)
        early(1)

    @pl.when(t > 0)
    def _():
        for u in range(chunks):
            exchange(slot, u).wait()

    for u in range(chunks):
        hid_ref[0, :, pl.ds(pl.multiple_of(own0 + u * CHUNK, CHUNK), CHUNK)] = hown[slot, u]
        hid_ref[0, :, pl.ds(pl.multiple_of(par0 + u * CHUNK, CHUNK), CHUNK)] = hpar[slot, u]

    @pl.when(t < steps)
    def _():
        for u in range(chunks):
            kpar[:, pl.ds(u * CHUNK, CHUNK)] = hpar[slot, u] * keep_b
        kept_ref[0, :, pl.ds(own0, units)] = kown[...]
        kept_ref[0, :, pl.ds(par0, units)] = kpar[...]
        for u in range(chunks):
            late(u)
            if u + 2 < chunks:
                early(u + 2)


def run_forward(embedded, keep, h0, c0, weights):
    steps, rows, depth = embedded.shape
    units = c0.shape[1]
    hidden = 2 * units
    chunks = units // CHUNK

    def at(t):
        return jnp.minimum(t, steps - 1)

    whole = pl.BlockSpec(memory_space=pltpu.VMEM)
    return pl.pallas_call(
        functools.partial(forward_kernel, steps),
        grid=(steps + 1,),
        in_specs=[
            pl.BlockSpec((1, rows, depth), lambda t: (at(t), 0, 0)),
            pl.BlockSpec((1, rows, 128), lambda t: (at(t), 0, 0)),
            whole,
            whole,
            pl.BlockSpec(memory_space=pl.ANY),
        ],
        out_specs=[
            pl.BlockSpec((1, rows, hidden), lambda t: (t, 0, 0)),
            pl.BlockSpec((1, rows, hidden), lambda t: (at(t), 0, 0)),
            pl.BlockSpec((1, 4, rows, units), lambda t: (at(t), 0, 0, 0)),
            pl.BlockSpec((1, rows, units), lambda t: (at(t), 0, 0)),
            pl.BlockSpec((1, rows, units), lambda t: (at(t), 0, 0)),
        ],
        out_shape=[
            jax.ShapeDtypeStruct((steps + 1, rows, hidden), jnp.bfloat16),
            jax.ShapeDtypeStruct((steps, rows, hidden), jnp.bfloat16),
            jax.ShapeDtypeStruct((steps, 4, rows, units), jnp.float32),
            jax.ShapeDtypeStruct((steps, rows, units), jnp.float32),
            jax.ShapeDtypeStruct((steps, rows, units), jnp.float32),
        ],
        scratch_shapes=[
            pltpu.VMEM(weights.shape, jnp.bfloat16),
            pltpu.VMEM((2, chunks, rows, CHUNK), jnp.bfloat16),
            pltpu.VMEM((2, chunks, rows, CHUNK), jnp.bfloat16),
            pltpu.VMEM((rows, units), jnp.bfloat16),
            pltpu.VMEM((rows, units), jnp.bfloat16),
            pltpu.VMEM((rows, units), jnp.float32),
            pltpu.VMEM((4, chunks, rows, CHUNK), jnp.float32),
            pltpu.SemaphoreType.DMA,
            pltpu.SemaphoreType.DMA((2, chunks)),
            pltpu.SemaphoreType.DMA((2, chunks)),
        ],
        compiler_params=pltpu.CompilerParams(
            collective_id=1, has_side_effects=True, vmem_limit_bytes=56 << 20
        ),
        cost_estimate=pl.CostEstimate(
            flops=2 * steps * rows * weights.shape[0] * weights.shape[1],
            bytes_accessed=500 << 20,
            transcendentals=0,
        ),
    )(embedded, keep, h0, c0, weights)


def backward_kernel(
    steps,
    outg_ref,
    gates_ref,
    cell_ref,
    ckept_ref,
    keep_ref,
    w_hbm,
    pre_ref,
    gh_ref,
    gc_ref,
    w_ref,
    dh,
    dc,
    pg,
    outbox,
    inbox,
    w_sem,
    send_sem,
    recv_sem,
):
    i = pl.program_id(0)
    slot = lax.rem(i, 2)
    core, peer = core_peer()
    units = dh.shape[1]
    chunks = units // CHUNK
    own0 = pl.multiple_of(core * units, units)
    par0 = pl.multiple_of((1 - core) * units, units)

    def exchange(which, u):
        return pltpu.make_async_remote_copy(
            src_ref=outbox.at[which, u],
            dst_ref=inbox.at[which, u],
            send_sem=send_sem.at[which, u],
            recv_sem=recv_sem.at[which, u],
            device_id=peer,
            device_id_type=MESH,
        )

    @pl.when(i == 0)
    def _():
        copy = pltpu.make_async_copy(w_hbm, w_ref, w_sem)
        copy.start()
        greet([peer])
        dh[...] = jnp.zeros_like(dh)
        dc[...] = jnp.zeros_like(dc)
        copy.wait()

    @pl.when(i > 0)
    def _():
        for u in range(chunks):
            exchange(1 - slot, u).wait()
        for u in range(chunks):
            span = pl.ds(u * CHUNK, CHUNK)
            dh[:, span] = dh[:, span] + inbox[1 - slot, u]

    keep = keep_ref[0][:, :1]
    for u in range(chunks):
        span = pl.ds(u * CHUNK, CHUNK)
        gate_in = gates_ref[0, 0, :, span]
        gate_forget = gates_ref[0, 1, :, span]
        gate_cell = gates_ref[0, 2, :, span]
        gate_out = gates_ref[0, 3, :, span]
        total_hidden = dh[:, span] + outg_ref[0, :, span]
        tanh_cell = jnp.tanh(cell_ref[0, :, span])
        total_cell = dc[:, span] + total_hidden * gate_out * (1.0 - tanh_cell * tanh_cell)
        grads = [
            total_cell * gate_cell * gate_in * (1.0 - gate_in),
            total_cell * ckept_ref[0, :, span] * gate_forget * (1.0 - gate_forget),
            total_cell * gate_in * (1.0 - gate_cell * gate_cell),
            total_hidden * tanh_cell * gate_out * (1.0 - gate_out),
        ]
        for q in range(4):
            grad = grads[q].astype(jnp.bfloat16)
            pg[:, pl.ds(q * units + u * CHUNK, CHUNK)] = grad
            pre_ref[0, :, pl.ds(q * units + u * CHUNK, CHUNK)] = grad
        dc[:, span] = total_cell * gate_forget * keep
    for u in range(chunks):
        cols = pl.ds(pl.multiple_of(par0 + u * CHUNK, CHUNK), CHUNK)
        outbox[slot, u] = (
            jnp.dot(pg[...], w_ref[:, cols], preferred_element_type=jnp.float32) * keep
        )
        exchange(slot, u).start()
    for u in range(chunks):
        cols = pl.ds(pl.multiple_of(own0 + u * CHUNK, CHUNK), CHUNK)
        dh[:, pl.ds(u * CHUNK, CHUNK)] = (
            jnp.dot(pg[...], w_ref[:, cols], preferred_element_type=jnp.float32) * keep
        )

    @pl.when(i == steps - 1)
    def _():
        for u in range(chunks):
            exchange(slot, u).wait()
        for u in range(chunks):
            span = pl.ds(u * CHUNK, CHUNK)
            gh_ref[:, span] = dh[:, span] + inbox[slot, u]
        gc_ref[...] = dc[...]


def run_backward(out_grad, gates, cells, cells_kept, keep, weights_t):
    steps, rows, units = out_grad.shape
    chunks = units // CHUNK

    def back(i):
        return (steps - 1 - i, 0, 0)

    row_block = pl.BlockSpec((1, rows, units), back)
    whole = pl.BlockSpec(memory_space=pltpu.VMEM)
    return pl.pallas_call(
        functools.partial(backward_kernel, steps),
        grid=(steps,),
        in_specs=[
            row_block,
            pl.BlockSpec((1, 4, rows, units), lambda i: (steps - 1 - i, 0, 0, 0)),
            row_block,
            row_block,
            pl.BlockSpec((1, rows, 128), back),
            pl.BlockSpec(memory_space=pl.ANY),
        ],
        out_specs=[pl.BlockSpec((1, rows, 4 * units), back), whole, whole],
        out_shape=[
            jax.ShapeDtypeStruct((steps, rows, 4 * units), jnp.bfloat16),
            jax.ShapeDtypeStruct((rows, units), jnp.float32),
            jax.ShapeDtypeStruct((rows, units), jnp.float32),
        ],
        scratch_shapes=[
            pltpu.VMEM(weights_t.shape, jnp.bfloat16),
            pltpu.VMEM((rows, units), jnp.float32),
            pltpu.VMEM((rows, units), jnp.float32),
            pltpu.VMEM((rows, 4 * units), jnp.bfloat16),
            pltpu.VMEM((2, chunks, rows, CHUNK), jnp.float32),
            pltpu.VMEM((2, chunks, rows, CHUNK), jnp.float32),
            pltpu.SemaphoreType.DMA,
            pltpu.SemaphoreType.DMA((2, chunks)),
            pltpu.SemaphoreType.DMA((2, chunks)),
        ],
        compiler_params=pltpu.CompilerParams(
            collective_id=2, has_side_effects=True, vmem_limit_bytes=56 << 20
        ),
        cost_estimate=pl.CostEstimate(
            flops=2 * steps * rows * weights_t.shape[0] * weights_t.shape[1],
            bytes_accessed=500 << 20,
            transcendentals=0,
        ),
    )(out_grad, gates, cells, cells_kept, keep, weights_t)


def shards(
    chars,
    targets,
    resets,
    word_pos,
    h_init,
    c_init,
    word_grad,
    w_emb,
    w_in,
    w_rec,
    b_rec,
    w_dec,
    b_dec,
    mom_emb,
    mom_in,
    mom_rec,
    mom_bias,
    mom_dec,
    mom_dbias,
):
    vocab_size = w_emb.shape[1]
    embed_size = w_emb.shape[2]
    seg_len = chars.shape[2]
    batch_size = chars.shape[1]
    hidden_size = w_rec.shape[2] // 4
    units = hidden_size // 2
    core = lax.rem(lax.axis_index("group"), 2)
    first = core == 0

    def pair(own):
        other = partner(own, "group", 0)
        return jnp.where(first, jnp.concatenate([own, other]), jnp.concatenate([other, own]))

    def half(value, axis, index):
        return lax.dynamic_slice_in_dim(value, index * units, units, axis)

    def own_columns(value):
        return jnp.concatenate(
            [half(value[:, q * hidden_size : (q + 1) * hidden_size], 1, core) for q in range(4)],
            axis=1,
        )

    def spread(value):
        wide = jnp.zeros((value.shape[0], 4 * hidden_size), value.dtype)
        for q in range(4):
            wide = lax.dynamic_update_slice_in_dim(
                wide, value[:, q * units : (q + 1) * units], q * hidden_size + core * units, 1
            )
        return wide

    in_full, rec_full, bias_full, dec_full = (
        lax.all_gather(w_in[0].astype(jnp.bfloat16), "group", axis=1, tiled=True),
        lax.all_gather(w_rec[0].astype(jnp.bfloat16), "group", axis=0, tiled=True),
        lax.all_gather(b_rec[0].astype(jnp.bfloat16), "group", axis=0, tiled=True),
        lax.all_gather(w_dec[0].astype(jnp.bfloat16), "group", axis=0, tiled=True),
    )
    packed = pair(jnp.concatenate([chars[0], targets[0], resets[0], word_pos[0]], axis=1))
    chars2 = packed[:, :seg_len]
    targets2 = packed[:, seg_len : 2 * seg_len]
    resets2 = packed[:, 2 * seg_len : 3 * seg_len]
    word_pos2 = packed[:, 3 * seg_len :]
    h_pair = pair(h_init[0].astype(jnp.bfloat16))
    c_mine = half(c_init[0], 1, core)
    c_other = partner(half(c_init[0], 1, 1 - core), "group", 0)
    wg_mine = half(word_grad, 2, core)
    wg_other = partner(half(word_grad, 2, 1 - core), "group", 0)

    def ordered(mine, other):
        return jnp.where(first, jnp.concatenate([mine, other]), jnp.concatenate([other, mine]))

    c_pair = ordered(c_mine, c_other)
    wg_pair = ordered(wg_mine, wg_other)
    in_own = own_columns(in_full)
    rec_own = own_columns(rec_full)
    bias_own = own_columns(bias_full[None])
    depth = 128
    weights = jnp.concatenate(
        [
            rec_own,
            in_own,
            bias_own,
            jnp.zeros((depth - embed_size - 1, 4 * units), jnp.bfloat16),
        ]
    )
    char_major = jnp.transpose(chars2)
    char_onehot = (char_major[:, :, None] == jnp.arange(vocab_size, dtype=jnp.int32)).astype(
        jnp.bfloat16
    )
    embedded = jnp.einsum(
        "tbv,ve->tbe",
        char_onehot,
        w_emb[0].astype(jnp.bfloat16),
        preferred_element_type=jnp.float32,
    ).astype(jnp.bfloat16)
    pad_shape = (seg_len, 2 * batch_size, depth - embed_size - 1)
    embedded_one = jnp.concatenate(
        [
            embedded,
            jnp.ones((seg_len, 2 * batch_size, 1), jnp.bfloat16),
            jnp.zeros(pad_shape, jnp.bfloat16),
        ],
        axis=-1,
    )
    keep_major = jnp.broadcast_to(
        (1 - jnp.transpose(resets2)).astype(jnp.float32)[:, :, None],
        (seg_len, 2 * batch_size, 128),
    )
    hidden_all, kept_all, gate_all, cell_all, cellkept_all = run_forward(
        embedded_one, keep_major, h_pair, c_pair, weights
    )
    out_all = hidden_all[1:]
    logits = (
        jnp.einsum("tbh,hv->tbv", out_all, dec_full, preferred_element_type=jnp.float32) + b_dec[0]
    )
    log_probs = jax.nn.log_softmax(logits, axis=-1)
    target_onehot = (
        jnp.transpose(targets2)[:, :, None] == jnp.arange(vocab_size, dtype=jnp.int32)
    ).astype(jnp.float32)
    loss_part = -0.5 * jnp.sum(log_probs * target_onehot)
    logit_grad = ((jnp.exp(log_probs) - target_onehot) / seg_len).astype(jnp.bfloat16)
    from_output = jnp.einsum(
        "tbv,hv->tbh",
        logit_grad,
        lax.dynamic_slice_in_dim(dec_full, core * units, units, 0),
        preferred_element_type=jnp.float32,
    )
    pos_onehot2 = (word_pos2[:, :, None] == jnp.arange(seg_len, dtype=jnp.int32)).astype(
        jnp.bfloat16
    )
    from_words = jnp.einsum(
        "bkt,bkh->tbh", pos_onehot2, wg_pair, preferred_element_type=jnp.float32
    )
    out_own = lax.dynamic_slice_in_dim(out_all, core * batch_size, batch_size, 1)
    pos_onehot = (word_pos[0][:, :, None] == jnp.arange(seg_len, dtype=jnp.int32)).astype(
        jnp.bfloat16
    )
    picked = jnp.einsum(
        "bkt,tbh->bkh", pos_onehot, out_own, preferred_element_type=jnp.float32
    ).astype(jnp.bfloat16)
    half_slots = picked.shape[1] // 2
    model_index = lax.axis_index("dir")
    own_slots = lax.dynamic_slice_in_dim(picked, model_index * half_slots, half_slots, 1)
    other_slots = lax.dynamic_slice_in_dim(picked, (1 - model_index) * half_slots, half_slots, 1)
    partner_half = partner(other_slots, "dir", 0)
    leading = model_index == 0
    word_vectors = jnp.where(
        leading,
        jnp.concatenate([own_slots, partner_half], axis=-1),
        jnp.concatenate([partner_half, own_slots], axis=-1),
    )
    pre_all, gh_pair, gc_pair = run_backward(
        from_output + from_words, gate_all, cell_all, cellkept_all, keep_major, rec_own.T
    )

    def own_rows(value):
        mine = lax.dynamic_slice_in_dim(value, core * batch_size, batch_size, 0)
        theirs = lax.dynamic_slice_in_dim(value, (1 - core) * batch_size, batch_size, 0)
        other = partner(theirs, "group", 0)
        return jnp.where(
            first,
            jnp.concatenate([mine, other], axis=1),
            jnp.concatenate([other, mine], axis=1),
        )

    grad_hidden0 = own_rows(gh_pair)
    grad_cell0 = own_rows(gc_pair)
    rec_grad = spread(
        jnp.einsum("tbh,tbg->hg", kept_all, pre_all, preferred_element_type=jnp.float32).astype(
            jnp.bfloat16
        )
    )
    in_grad = spread(
        jnp.einsum("tbe,tbg->eg", embedded, pre_all, preferred_element_type=jnp.float32).astype(
            jnp.bfloat16
        )
    )
    bias_grad = spread(jnp.sum(pre_all, axis=(0, 1), dtype=jnp.float32).astype(jnp.bfloat16)[None])[0]
    lg_own = lax.dynamic_slice_in_dim(logit_grad, core * batch_size, batch_size, 1)
    dec_grad = jnp.einsum("tbh,tbv->hv", out_own, lg_own, preferred_element_type=jnp.float32)
    dbias_grad = jnp.sum(lg_own, axis=(0, 1), dtype=jnp.float32)
    embed_in = jnp.einsum("tbg,eg->tbe", pre_all, in_own, preferred_element_type=jnp.float32)
    emb_grad = jnp.einsum(
        "tbv,tbe->ve", char_onehot.astype(jnp.float32), embed_in, precision=lax.Precision.HIGHEST
    )
    loss_part = jnp.reshape(loss_part, (1,))
    in_sum, rec_sum, bias_sum, dec_sum = (
        lax.psum_scatter(in_grad, "group", scatter_dimension=1, tiled=True).astype(jnp.float32),
        lax.psum_scatter(rec_grad, "group", scatter_dimension=0, tiled=True).astype(jnp.float32),
        lax.psum_scatter(bias_grad, "group", scatter_dimension=0, tiled=True).astype(jnp.float32),
        lax.psum_scatter(
            dec_grad.astype(jnp.bfloat16), "group", scatter_dimension=0, tiled=True
        ).astype(jnp.float32),
    )
    in_sum, rec_sum, bias_sum, dec_sum, emb_sum, dbias_sum, loss_sum = (
        lax.psum(in_sum.astype(jnp.bfloat16), "dp").astype(jnp.float32),
        lax.psum(rec_sum.astype(jnp.bfloat16), "dp").astype(jnp.float32),
        lax.psum(bias_sum.astype(jnp.bfloat16), "dp").astype(jnp.float32),
        lax.psum(dec_sum.astype(jnp.bfloat16), "dp").astype(jnp.float32),
        lax.psum(emb_grad.astype(jnp.bfloat16), "dp").astype(jnp.float32),
        lax.psum(dbias_grad.astype(jnp.bfloat16), "dp").astype(jnp.float32),
        lax.psum(loss_part.astype(jnp.bfloat16), "dp").astype(jnp.float32),
    )
    shard_sq = squares_of((in_sum, rec_sum, bias_sum, dec_sum))
    shard_sq, emb_sum, dbias_sum, loss_sum = (
        lax.psum(shard_sq.astype(jnp.bfloat16), "group").astype(jnp.float32),
        lax.psum(emb_sum.astype(jnp.bfloat16), "group").astype(jnp.float32),
        lax.psum(dbias_sum.astype(jnp.bfloat16), "group").astype(jnp.float32),
        lax.psum(loss_sum.astype(jnp.bfloat16), "group").astype(jnp.float32),
    )
    total_sq = shard_sq + squares_of((emb_sum, dbias_sum))
    clip_scale = 0.25 / jnp.maximum(jnp.sqrt(total_sq), 0.25)
    mom_in_next = momentum_step(mom_in[0], in_sum, clip_scale)
    mom_rec_next = momentum_step(mom_rec[0], rec_sum, clip_scale)
    mom_bias_next = momentum_step(mom_bias[0], bias_sum, clip_scale)
    mom_dec_next = momentum_step(mom_dec[0], dec_sum, clip_scale)
    mom_emb_next = momentum_step(mom_emb[0], emb_sum, clip_scale)
    mom_dbias_next = momentum_step(mom_dbias[0], dbias_sum, clip_scale)
    token_count = seg_len * batch_size * lax.axis_size("group") * lax.axis_size("dp")
    losses = loss_sum / token_count
    return (
        losses,
        word_vectors,
        grad_hidden0[None],
        grad_cell0[None],
        emb_sum[None],
        in_sum[None],
        rec_sum[None],
        bias_sum[None],
        dec_sum[None],
        dbias_sum[None],
        mom_emb_next[None],
        mom_in_next[None],
        mom_rec_next[None],
        mom_bias_next[None],
        mom_dec_next[None],
        mom_dbias_next[None],
    )


def solution(mesh):
    segments = P("dir", ("group", "dp"), None)
    shared = P("dir", None, None)
    columns = P("dir", None, "group")
    rows = P("dir", "group", None)
    flat = P("dir", "group")
    return jax.shard_map(
        shards,
        mesh=mesh,
        in_specs=(
            segments,
            segments,
            segments,
            segments,
            segments,
            segments,
            P(("group", "dp"), None, "dir"),
            shared,
            columns,
            rows,
            flat,
            rows,
            P("dir", None),
            shared,
            columns,
            rows,
            flat,
            rows,
            P("dir", None),
        ),
        out_specs=(
            P("dir"),
            P(("group", "dp"), "dir", None),
            segments,
            segments,
            shared,
            columns,
            rows,
            flat,
            rows,
            P("dir", None),
            shared,
            columns,
            rows,
            flat,
            rows,
            P("dir", None),
        ),
        check_vma=False,
    )
```

time: 1790 us -> 1280 us (0.72)
  matrix products: 746 us -> 62.7 us
  Pallas kernels: 0 us -> 219 us
  other arithmetic: 215 us -> 75 us
  local copies, waits for them, and re-layouts: 48.3 us -> 147 us
    dot_general x54 -> x5, matrix products: 701 us -> 22.4 us  [the longest x1 7.96 us: shards(): jnp.einsum('tbv,hv->tbh', logit_grad, lax.dynamic_slice_in_dim(dec_full,...]
    pallas_call x0 -> x2, Pallas kernels: none -> 219 us  [the longest x1 113 us: run_backward(): pl.pallas_call(functools.partial(backward_kernel, steps), grid=(steps,),...]
    dynamic_update_slice x120 -> x0, other arithmetic: 97.4 us -> none  [the longest x96 78.7 us: shards(): final_pair, stored = lax.scan(advance, start_pair, (projected, keep_major))]
    concatenate x0 -> x7, local copies, waits for them, and re-layouts: none -> 50.7 us  [the longest x2 50 us: shards(): jnp.concatenate([rec_own, in_own, bias_own, jnp.zeros((depth - embed_size...]
    squeeze x24 -> x2, local copies, waits for them, and re-layouts: 28.5 us -> 0.08 us  [the longest x1 0.07 us: shards(): word_pos[0]]
    slice x0 -> x6, local copies, waits for them, and re-layouts: none -> 28.2 us  [the longest x3 22.9 us: own_columns(): value[:, q * hidden_size:(q + 1) * hidden_size]]
    mul x24 -> x0, other arithmetic: 27.7 us -> none  [retreat(): total_cell * gate_forget * keep_col]
    another operation x28 -> x0, other arithmetic: 24.6 us -> none
  transfers between devices with their start and end apart: 8 -> 14, of which waited for: 4 -> 4; matrix products, arithmetic and copies ran while one was open for 53% -> 17% of each run, Pallas kernels for 0% -> 17%
where the time goes in v1:
time: 1280 us; the launch traced here: 1270 us
  waiting for transfers between devices  684 us (53%)
  Pallas kernels  219 us (17%)
  local copies, waits for them, and re-layouts  147 us (11%)
  other arithmetic  75 us (6%)
  matrix products  62.7 us (5%)
  blocking collectives  55.6 us (4%)
  between operations  23.1 us (2%)
    psum x1, waiting for transfers between devices, shards(): lax.psum(in_sum.astype(jnp.bfloat16), 'dp').astype(jnp.float32)  250 us
    unnamed x8, waiting for transfers between devices  235 us
    all_gather x1, waiting for transfers between devices, shards(): lax.all_gather(w_rec[0].astype(jnp.bfloat16), 'group', axis=0, tiled=True)  191 us
    pallas_call x1, Pallas kernels, run_backward(): pl.pallas_call(functools.partial(backward_kernel, steps), grid=(steps,),...  113 us
    pallas_call x1, Pallas kernels, run_forward(): pl.pallas_call(functools.partial(forward_kernel, steps), grid=(steps + 1,...  106 us
    concatenate x2, local copies, waits for them, and re-layouts, shards(): jnp.concatenate([rec_own, in_own, bias_own, jnp.zeros((depth - embed_size...  50 us
    dot_general x1, matrix products, shards(): jnp.einsum('tbh,tbg->hg', kept_all, pre_all, preferred_element_type=jnp.f...  26 us
  transfers between devices with their start and end apart: 14, of which 4 were waited for; matrix products, arithmetic and copies ran while one was open for 17% of the time, Pallas kernels for 17%

profile of v1, /device:TPU:0, one launch (start us, length us, event | category | flops | bytes accessed | tf_op | source)
XLA Modules:
  0.0 1270.9 jit_solution(2982797455826389550)
XLA Ops:
  9.7 13.9 %copy.81 = bf16[1,512,8192]{1,2,0:T(8,128)(2,1)} copy(f32[1,512,8192]{2,1,0:T(8,128)} %param.28) | data formatting | bytes 25165824 | tf_op args[9]
  27.2 6.5 all-gather.2
  48.3 191.1 %all-gather.8.cloned.1.call-done = bf16[1,2048,8192]{1,2,0:T(8,128)(2,1)} async-done(((bf16[1,512,8192]{1,2,0:T(8,128)(2,1)}), bf16[1,2048,8192]{1,2,0:T(8,128)(2,1)}) %all-gather.8.cloned.1.call-update) | async-done | bytes 33554448 | tf_op jit(solution)/shard_map/all_gather | solution.py:424
  239.4 20.7 %fusion.51 = (bf16[2048,2048]{0,1:T(8,128)(2,1)}, bf16[2048,2048]{0,1:T(8,128)(2,1)S(1)}, bf16[2048,2048]{0,1:T(8,128)(2,1)}, bf16[2048,2048]{0,1:T(8,128)(2,1)}) fusion(bf16[2048,8192]{0,1:T(8,128)(2,1)} %bitcast.94), kind=kLoop, calls=%fused_computation.137 | loop fusion | bytes 67108864 | tf_op jit(solution)/shard_map/slice | solution.py:410
  260.1 6.8 constant_dynamic-slice_fusion.17
  266.9 6.7 constant_dynamic-slice_fusion.15
  273.5 16.0 %fusion.50 = (bf16[4096,2048]{1,0:T(8,128)(2,1)}, bf16[2048,4096]{0,1:T(8,128)(2,1)}) fusion(bf16[2048,1024]{0,1:T(8,128)(2,1)} %get-tuple-element.132, bf16[2048,1024]{0,1:T(8,128)(2,1)} %get-tuple-element.133, bf16[2048,1024]{0,1:T(8,128)(2,1)S(1)} %get-tuple-element.134, bf16[2048,1024]{0,1:T(8,128)(2,1)} %get-tuple-element.135), kind=kLoop, calls=%fused_computation.136 | loop fusion | flops 67108864 | bytes 50331648 | tf_op jit(solution)/shard_map/transpose | solution.py:523
  289.7 25.9 %concatenate.107 = bf16[2176,4096]{0,1:T(8,128)(2,1)} concatenate(bf16[2048,4096]{0,1:T(8,128)(2,1)} %get-tuple-element.100, bf16[100,4096]{0,1:T(8,128)(2,1)} %pad_maximum_fusion.1, bf16[1,4096]{0,1:T(8,128)(2,1)S(1)} %copy.84, bf16[27,4096]{0,1:T(8,128)(2,1)S(1)} %broadcast_in_dim.81), dimensions={0} | concatenate | bytes 35651584 | tf_op jit(solution)/shard_map/concatenate | solution.py:448
  315.6 24.1 %copy.85.w_hbm = bf16[2176,4096]{1,0:T(8,128)(2,1)} copy(bf16[2176,4096]{0,1:T(8,128)(2,1)} %concatenate.107) | data formatting | bytes 35651584 | tf_op jit(solution)/shard_map/concatenate | solution.py:448
  340.7 106.2 %shard_map.306 = (bf16[25,48,2048]{2,1,0:T(8,128)(2,1)}, bf16[24,48,2048]{2,1,0:T(8,128)(2,1)}, f32[24,4,48,1024]{3,2,1,0:T(8,128)}, f32[24,48,1024]{2,1,0:T(8,128)}, f32[24,48,1024]{2,1,0:T(8,128)}) custom-call(bf16[24,48,128]{2,1,0:T(8,128)(2,1)} %maximum_maximum_fusion.emb_ref, f32[24,48,128]{2,1,0:T(8,128)} %broadcast_in_dim.79.keep_ref, ...), custom_call_target="tpu_custom_call" | custom-call | flops 20535312384 | bytes 524288000 | tf_op jit(solution)/shard_map/pallas_call | solution.py:177
  452.1 6.6 fusion.11
  465.8 8.0 bitcast_add_fusion.outg_ref
  473.7 113.1 %shard_map.307 = (bf16[24,48,4096]{2,1,0:T(8,128)(2,1)}, f32[48,1024]{1,0:T(8,128)}, f32[48,1024]{1,0:T(8,128)}) custom-call(f32[24,48,1024]{2,1,0:T(8,128)} %bitcast_add_fusion.outg_ref, f32[24,4,48,1024]{3,2,1,0:T(8,128)} %get-tuple-element.25.gates_ref, f32[24,48,1024]{2,1,0:T(8,128)} %get-tuple-element.26.cell_ref, ...), custom_call_target="tpu_custom_call" | custom-call | flops 19327352832 | bytes 524288000 | tf_op jit(solution)/shard_map/pallas_call | solution.py:332
  593.8 26.0 %bitcast_convert_fusion = bf16[2048,4096]{1,0:T(8,128)(2,1)S(1)} fusion(bf16[24,48,2048]{2,1,0:T(8,128)(2,1)} %get-tuple-element.31, bf16[24,48,4096]{2,1,0:T(8,128)(2,1)} %get-tuple-element.30), kind=kOutput, calls=%fused_computation.2 | convolution fusion | flops 19335741440 | bytes 30932992 | tf_op jit(solution)/shard_map/tbh,tbg->hg/dot_general | solution.py:539
  619.8 11.0 broadcast_in_dim.85
  640.6 234.8 %reduce-scatter.10.cloned.1.call-done = bf16[512,8192]{1,0:T(8,128)(2,1)} async-done(((bf16[2048,8192]{1,0:T(8,128)(2,1)}), bf16[512,8192]{1,0:T(8,128)(2,1)}) %reduce-scatter.10.cloned.1.call-update) | async-done | bytes 8388624
  883.6 11.1 all-reduce.1
  901.9 24.5 %all-reduce.2 = (bf16[1]{0:T(256)(128)(2,1)}, bf16[275]{0:T(512)(128)(2,1)S(1)}, bf16[2048]{0:T(1024)(128)(2,1)S(1)}, bf16[275,100]{1,0:T(8,128)(2,1)S(1)}) all-reduce(bf16[1]{0:T(256)(128)(2,1)} %bitcast.14, bf16[275]{0:T(512)(128)(2,1)S(1)} %dynamic-slice_reduce_fusion, ...), channel_id=1, replica_groups=mesh['dir'=2,'group'=4,'dp'=4] {'dp'}, use_global_device_ids=true, to_apply=%region_3.4 | all-reduce | flops 29824 | bytes 119296 | tf_op jit(solution)/shard_map/psum | solution.py:572
  936.7 7.5 collective-permute-done.3
  945.7 250.5 %all-reduce.7.cloned.1.call-done = (bf16[100,2048]{1,0:T(8,128)(2,1)}, bf16[512,8192]{1,0:T(8,128)(2,1)}, bf16[512,275]{0,1:T(8,128)(2,1)}) async-done(((bf16[100,2048]{1,0:T(8,128)(2,1)}, bf16[512,8192]{1,0:T(8,128)(2,1)}, bf16[512,275]{0,1:T(8,128)(2,1)}), (bf16[100,2048]{1,0:T(8,128)(2,1)}, bf16[512,8192]{1,0:T(8,128)(2,1)}, bf16[512,275]{0,1:T(8,128)(2,1)})) %all-reduce.7.cloned.1.call-update) | async-done | bytes 9079824 | tf_op jit(solution)/shard_map/psum | solution.py:566
  1198.0 8.3 fusion.2
  1209.7 13.5 %all-reduce.4 = (bf16[1]{0:T(256)(128)(2,1)}, bf16[275]{0:T(512)(128)(2,1)S(1)}, bf16[]{:T(256)}, bf16[275,100]{1,0:T(8,128)(2,1)S(1)}) all-reduce(bf16[1]{0:T(256)(128)(2,1)} %get-tuple-element.84, bf16[275]{0:T(512)(128)(2,1)S(1)} %get-tuple-element.85, bf16[]{:T(256)S(6)} %add.170, ...), channel_id=1, replica_groups=mesh['dir'=2,'group'=4,'dp'=4] {'group'}, use_global_device_ids=true, to_apply=%region_4.5 | all-reduce | flops 27777 | bytes 111108 | tf_op jit(solution)/shard_map/psum | solution.py:579
  1226.4 11.8 convert_bitcast_fusion
  1247.8 13.9 %fusion.4 = f32[1,512,8192]{2,1,0:T(8,128)} fusion(bf16[512,8192]{1,0:T(8,128)(2,1)} %get-tuple-element.89, f32[1,512,8192]{2,1,0:T(8,128)} %param.34, f32[]{:T(128)S(6)} %div.15), kind=kLoop, calls=%fused_computation.8 | loop fusion | flops 16777216 | bytes 41943044 | tf_op jit(solution)/shard_map/broadcast_in_dim | solution.py:604
  (196 shorter events, 89.3 us)
Async XLA Ops:
  7.2 36.7 %all-gather.10.cloned.1.call-start = ((), (), s32[]{:S(2)}) async-start(), calls=%async_computation.6 | async-start | bytes 2621440 | tf_op jit(solution)/shard_map/all_gather | solution.py:423
  9.7 229.7 %all-gather.8.cloned.1.call-start = ((), (), s32[]{:S(2)}) async-start(), calls=%async_computation.5 | async-start | bytes 41943040 | tf_op jit(solution)/shard_map/all_gather | solution.py:424
  23.8 428.4 %all-gather.12.cloned.1.call-start = ((), (), s32[]{:S(2)}) async-start(), calls=%async_computation.7 | async-start | bytes 1433600 | tf_op jit(solution)/shard_map/all_gather | solution.py:426
  24.4 19.5 %copy-start.17 = (s32[24,8]{1,0:T(8,128)}, s32[24,8]{1,0:T(8,128)S(1)}, u32[]{:S(2)}) copy-start(s32[24,8]{1,0:T(8,128)S(1)} %copy.77) | copy-start | bytes 2308
  24.5 10.2 collective-permute-start
  24.9 13.3 %collective-permute-start.1 = (bf16[24,2048]{1,0:T(8,128)(2,1)S(1)}, bf16[24,2048]{1,0:T(8,128)(2,1)}, u32[]{:S(2)}, u32[]{:S(2)}) collective-permute-start(bf16[24,2048]{1,0:T(8,128)(2,1)S(1)} %convert_bitcast_fusion.3), channel_id=1, source_target_pairs={{0,4},{4,0},{8,12},{12,8},{1,5},{5,1},{9,13},{13,9},{2,6},{6,2},{1... | collective-permute-start | bytes 294920 | tf_op jit(solution)/shard_map/ppermute | solution.py:17
  25.8 10.7 collective-permute-start.2
  26.2 13.7 %collective-permute-start.4 = (bf16[24,8,1024]{2,1,0:T(8,128)(2,1)S(1)}, bf16[24,8,1024]{2,1,0:T(8,128)(2,1)S(1)}, u32[]{:S(2)}, u32[]{:S(2)}) collective-permute-start(bf16[24,8,1024]{2,1,0:T(8,128)(2,1)S(1)} %get-tuple-element.110), channel_id=1, source_target_pairs={{0,4},{4,0},{8,12},{12,8},{1,5},{5,1},{9,13},{13,9},{2,6},{6,2},{1... | collective-permute-start | bytes 1179656 | tf_op jit(solution)/shard_map/ppermute | solution.py:17
  27.2 613.4 %reduce-scatter.8.cloned.1.call-start = ((), (), s32[]{:S(2)}) async-start(), calls=%async_computation.4 | async-start | bytes 1433600 | tf_op jit(solution)/shard_map/reduce_scatter | solution.py:561
  465.7 174.9 %reduce-scatter.6.cloned.1.call-start = ((), (), s32[]{:S(2)}) async-start(), calls=%async_computation.3 | async-start | bytes 2129920 | tf_op jit(solution)/shard_map/reduce_scatter | solution.py:558
  593.7 281.7 %reduce-scatter.10.cloned.1.call-start = ((), (), s32[]{:S(2)}) async-start(), calls=%async_computation.8 | async-start | bytes 41943040
  640.5 235.0 %copy-start.35 = (u32[32]{0:T(128)S(1)}, u32[32]{0:T(128)}, u32[]{:S(2)}) copy-start(u32[32]{0:T(128)} %constant.108) | copy-start | bytes 388
  640.5 236.2 %copy-start.33 = (f32[1,275]{1,0:T(1,128)S(1)}, f32[1,275]{1,0:T(1,128)}, u32[]{:S(2)}) copy-start(f32[1,275]{1,0:T(1,128)} %param.37) | copy-start | bytes 3304
  640.5 236.3 %copy-start.31 = (f32[1,2048]{1,0:T(1,128)S(1)}, f32[1,2048]{1,0:T(1,128)}, u32[]{:S(2)}) copy-start(f32[1,2048]{1,0:T(1,128)} %param.35) | copy-start | bytes 24580
  640.5 555.6 %all-reduce.7.cloned.1.call-start = ((), (), s32[]{:S(2)}) async-start(), calls=%async_computation.9 | async-start | bytes 18202624 | tf_op jit(solution)/shard_map/psum | solution.py:566
  876.8 18.0 %copy-start.5 = (bf16[100,1024]{0,1:T(8,128)(2,1)S(1)}, bf16[100,1024]{0,1:T(8,128)(2,1)}, u32[]{:S(2)}) copy-start(bf16[100,1024]{0,1:T(8,128)(2,1)} %copy-done.4) | copy-start | bytes 614404
  876.8 18.0 %copy-start.7 = (bf16[100,1024]{0,1:T(8,128)(2,1)S(1)}, bf16[100,1024]{0,1:T(8,128)(2,1)}, u32[]{:S(2)}) copy-start(bf16[100,1024]{0,1:T(8,128)(2,1)} %copy-done.6) | copy-start | bytes 614404
  894.9 32.1 %copy-start.22 = (f32[48,1024]{1,0:T(8,128)S(1)}, f32[48,1024]{1,0:T(8,128)}, u32[]{:S(2)}) copy-start(f32[48,1024]{1,0:T(8,128)} %get-tuple-element.28) | copy-start | bytes 589828
  894.9 32.2 %copy-start.21 = (f32[48,1024]{1,0:T(8,128)S(1)}, f32[48,1024]{1,0:T(8,128)}, u32[]{:S(2)}) copy-start(f32[48,1024]{1,0:T(8,128)} %get-tuple-element.29) | copy-start | bytes 589828
  900.1 29.3 %copy-start.18 = (s32[24,8]{1,0:T(8,128)S(1)}, s32[24,8]{1,0:T(8,128)}, u32[]{:S(2)}) copy-start(s32[24,8]{1,0:T(8,128)} %copy-done.17) | copy-start | bytes 2308
  927.0 8.3 collective-permute-start.5
  927.1 8.9 collective-permute-start.6
  933.0 11.1 collective-permute-start.3
  1196.2 28.8 %copy-start.3 = (bf16[512,275]{0,1:T(8,128)(2,1)S(1)}, bf16[512,275]{0,1:T(8,128)(2,1)}, u32[]{:S(2)}) copy-start(bf16[512,275]{0,1:T(8,128)(2,1)} %get-tuple-element.90) | copy-start | bytes 844804
  (26 other events, 149.2 us)
Sparse Core Ops, SparseCore 0:
  10.1 25.4 all-gather.9
  37.8 201.5 all-gather.7
  241.5 17.2 all-gather.11
  465.8 25.4 reduce-scatter.7
  593.9 28.8 reduce-scatter.5
  640.6 234.7 reduce-scatter.9
  878.3 317.8 all-reduce.6

commit v2 on v1

--- a/solution.py
+++ b/solution.py
@@ -19,13 +19,6 @@
 
 def momentum_step(moment, gradient, clip_scale):
     return 0.9 * moment + clip_scale * gradient
-
-
-def squares_of(arrays):
-    total_sq = jnp.zeros((), jnp.float32)
-    for array in arrays:
-        total_sq = total_sq + jnp.sum(array * array)
-    return total_sq
 
 
 def sigmoid(value):
@@ -368,6 +361,568 @@
     )(out_grad, gates, cells, cells_kept, keep, weights_t)
 
 
+def reduce_kernel(
+    chips,
+    depth,
+    embed,
+    kept_ref,
+    aug_ref,
+    pre_ref,
+    in_ref,
+    chars_ref,
+    extra_ref,
+    decsq_ref,
+    rec_hbm,
+    inout_ref,
+    emb_ref,
+    clip_ref,
+    turned,
+    inbox,
+    outbox,
+    partial,
+    final,
+    in_all,
+    in_box,
+    in_mine,
+    in_part,
+    in_final,
+    in_swap,
+    emb_box,
+    emb_mine,
+    emb_part,
+    emb_final,
+    ssq,
+    norm_box,
+    y_send,
+    y_recv,
+    part_recv,
+    final_recv,
+    part_send,
+    final_send,
+    write_sem,
+    in_send,
+    in_recv,
+    emb_send,
+    emb_recv,
+    misc_recv,
+    misc_send,
+    norm_send,
+    norm_recv,
+):
+    model = lax.axis_index("dir")
+    group = lax.axis_index("group")
+    z = lax.axis_index("dp")
+    core = lax.rem(group, 2)
+    chip = group // 2
+    peers = 2 * chips
+    middle = depth // 2
+    rows_out = kept_ref.shape[1] // peers
+    wide = pre_ref.shape[1]
+    tall = turned.shape[0]
+    lot = tall // 16
+    batches = rows_out // tall
+    groups = rows_out // 16
+    per_pass = lot // peers
+    upper = depth - 1 > middle
+    is_middle = z == middle
+    low = z < middle
+    has_away = jnp.logical_or(jnp.logical_and(low, z > 0), jnp.logical_and(z > middle, z < depth - 1))
+    toward = jnp.where(low, z + 1, jnp.maximum(z - 1, 0))
+    away = jnp.where(low, jnp.maximum(z - 1, 0), jnp.minimum(z + 1, depth - 1))
+
+    def in_group(index):
+        return (model, index, z)
+
+    def in_line(index):
+        return (model, group, index)
+
+    def owner_of(slot):
+        if slot == 0:
+            return group
+        if slot == 1:
+            return group + 1 - 2 * core
+        step = (slot - 2) // 2 + 1
+        side = core if slot % 2 == 0 else 1 - core
+        return 2 * lax.rem(chip + step, chips) + side
+
+    def slot_there(slot):
+        if slot == 1:
+            return 1
+        step = (slot - 2) // 2 + 1
+        return 2 + 2 * (chips - step - 1) + slot % 2
+
+    barrier = pltpu.get_barrier_semaphore()
+    for slot in range(1, peers):
+        pl.semaphore_signal(barrier, inc=1, device_id=in_group(owner_of(slot)), device_id_type=MESH)
+
+    @pl.when(z > 0)
+    def _():
+        pl.semaphore_signal(
+            barrier, inc=1, device_id=in_line(jnp.maximum(z - 1, 0)), device_id_type=MESH
+        )
+
+    @pl.when(z < depth - 1)
+    def _():
+        pl.semaphore_signal(
+            barrier, inc=1, device_id=in_line(jnp.minimum(z + 1, depth - 1)), device_id_type=MESH
+        )
+
+    pl.semaphore_wait(
+        barrier,
+        peers - 1 + jnp.where(z > 0, 1, 0) + jnp.where(z < depth - 1, 1, 0),
+    )
+    ssq[...] = jnp.zeros_like(ssq)
+
+    def remote(src, dst, send, recv, device):
+        return pltpu.make_async_remote_copy(
+            src_ref=src,
+            dst_ref=dst,
+            send_sem=send,
+            recv_sem=recv,
+            device_id=device,
+            device_id_type=MESH,
+        )
+
+    def squares(value):
+        square = value * value
+        total = square[:, :128]
+        for lane in range(128, value.shape[1], 128):
+            total = total + square[:, lane : lane + 128]
+        rows = total[:16]
+        for row in range(16, value.shape[0], 16):
+            rows = rows + total[row : row + 16]
+        ssq[...] = ssq[...] + rows
+
+    def send_partial(mine, part, fin, sems):
+        @pl.when(jnp.logical_not(is_middle))
+        def _():
+            @pl.when(has_away)
+            def _():
+                remote(mine, part, sems["ps"], sems["pr"], in_line(away)).wait_recv()
+                mine[...] = (
+                    mine[...].astype(jnp.float32) + part[...].astype(jnp.float32)
+                ).astype(mine.dtype)
+
+            if upper:
+
+                @pl.when(z == middle + 1)
+                def _():
+                    remote(mine, fin, sems["ps"], sems["fr"], in_line(toward)).start()
+
+            @pl.when(z != middle + 1)
+            def _():
+                remote(mine, part, sems["ps"], sems["pr"], in_line(toward)).start()
+
+        @pl.when(is_middle)
+        def _():
+            remote(mine, part, sems["ps"], sems["pr"], in_line(toward)).wait_recv()
+            total = mine[...].astype(jnp.float32) + part[...].astype(jnp.float32)
+            if upper:
+                remote(mine, fin, sems["ps"], sems["fr"], in_line(toward)).wait_recv()
+                total = total + fin[...].astype(jnp.float32)
+            fin[...] = total.astype(fin.dtype)
+            remote(fin, fin, sems["f0"], sems["fr"], in_line(middle - 1)).start()
+            if upper:
+                remote(fin, fin, sems["f1"], sems["fr"], in_line(middle + 1)).start()
+
+    def pass_final(fin, sems):
+        @pl.when(jnp.logical_not(is_middle))
+        def _():
+            remote(fin, fin, sems["f0"], sems["fr"], in_line(toward)).wait_recv()
+
+            @pl.when(has_away)
+            def _():
+                remote(fin, fin, sems["f0"], sems["fr"], in_line(away)).start()
+
+    def wait_line(mine, fin, sems):
+        @pl.when(is_middle)
+        def _():
+            remote(fin, fin, sems["f0"], sems["fr"], in_line(toward)).wait_send()
+            if upper:
+                remote(fin, fin, sems["f1"], sems["fr"], in_line(toward)).wait_send()
+
+        @pl.when(jnp.logical_not(is_middle))
+        def _():
+            remote(mine, fin, sems["ps"], sems["fr"], in_line(toward)).wait_send()
+
+            @pl.when(has_away)
+            def _():
+                remote(fin, fin, sems["f0"], sems["fr"], in_line(away)).wait_send()
+
+    def line_sems(unit):
+        return {
+            "pr": part_recv.at[unit],
+            "fr": final_recv.at[unit],
+            "ps": part_send.at[unit],
+            "f0": final_send.at[0, unit],
+            "f1": final_send.at[1, unit],
+        }
+
+    units = 2 * groups
+    in_sems, emb_sems = line_sems(units), line_sems(units + 1)
+
+    def send_block(slot, parity, index, row):
+        return remote(
+            outbox.at[slot - 1, parity, index],
+            inbox.at[slot_there(slot), row],
+            y_send.at[slot - 1, parity, index],
+            y_recv.at[slot_there(slot) - 1, row],
+            in_group(owner_of(slot)),
+        )
+
+    span = 1024
+
+    def product(dest):
+        def columns(j, carry):
+            cols = pl.ds(pl.multiple_of(j * span, span), span)
+            dest[:, :, cols] = (
+                jnp.dot(turned[...], pre_ref[:, cols], preferred_element_type=jnp.float32)
+                .astype(jnp.bfloat16)
+                .reshape(lot, 16, span)
+            )
+            return carry
+
+        lax.fori_loop(0, wide // span, columns, 0)
+
+    def block(slot, b, parity):
+        start = owner_of(slot) * rows_out + b * tall
+        turned[...] = jnp.transpose(kept_ref[:, pl.ds(pl.multiple_of(start, tall), tall)])
+        if slot == 0:
+            product(inbox.at[0, pl.ds(b * lot, lot)])
+        else:
+
+            @pl.when(b >= 2)
+            def _():
+                for index in range(lot):
+                    send_block(slot, parity, index, 0).wait_send()
+
+            product(outbox.at[slot - 1, parity])
+
+    def send(row):
+        parity, index = lax.rem(row // lot, 2), lax.rem(row, lot)
+        for slot in list(range(2, peers)) + [1]:
+            send_block(slot, parity, index, row).start()
+
+    def take(row):
+        for slot in range(1, peers):
+            remote(
+                outbox.at[slot - 1, 0, 0],
+                inbox.at[slot, row],
+                y_send.at[slot - 1, 0, 0],
+                y_recv.at[slot - 1, row],
+                in_group(owner_of(slot)),
+            ).wait_recv()
+        for part in range(2):
+            if chips > 1:
+                total = inbox[part, row].astype(jnp.float32)
+                for slot in range(2 + part, peers, 2):
+                    total = total + inbox[slot, row].astype(jnp.float32)
+                inbox[part, row] = total.astype(jnp.bfloat16)
+            send_partial(
+                inbox.at[part, row],
+                partial.at[2 * row + part],
+                final.at[2 * row + part],
+                line_sems(2 * row + part),
+            )
+
+    def write_out(row, part):
+        side = core if part == 0 else 1 - core
+        return pltpu.make_async_copy(
+            final.at[2 * row + part],
+            rec_hbm.at[side, pl.ds(pl.multiple_of(row * 16, 16), 16)],
+            write_sem.at[2 * row + part],
+        )
+
+    def finish(row):
+        for part in range(2):
+            pass_final(final.at[2 * row + part], line_sems(2 * row + part))
+            write_out(row, part).start()
+            squares(final[2 * row + part].astype(jnp.float32))
+
+    in_rows, in_wide = in_mine.shape
+
+    def in_columns(index):
+        return pl.ds(pl.multiple_of(index * in_wide, in_wide), in_wide)
+
+    def in_copy(step):
+        there = lax.rem(chip + step, chips)
+        return remote(
+            in_all.at[:, in_columns(there)],
+            in_box.at[chips - step - 1],
+            in_send.at[step - 1],
+            in_recv.at[chips - step - 1],
+            in_group(2 * there + core),
+        )
+
+    def emb_copy(slot, source):
+        return remote(
+            emb_mine,
+            emb_box.at[source],
+            emb_send.at[slot - 1],
+            emb_recv.at[source],
+            in_group(owner_of(slot)),
+        )
+
+    def small_products():
+        turned[...] = jnp.transpose(aug_ref[...])
+
+        def columns(j, carry):
+            cols = pl.ds(pl.multiple_of(j * span, span), span)
+            in_all[:, cols] = jnp.dot(
+                turned[...], pre_ref[:, cols], preferred_element_type=jnp.float32
+            )[:in_rows].astype(jnp.bfloat16)
+            return carry
+
+        lax.fori_loop(0, wide // span, columns, 0)
+        for step in range(1, chips):
+            in_copy(step).start()
+        into = lax.dot_general(
+            pre_ref[...], in_ref[...], (((1,), (1,)), ((), ())), preferred_element_type=jnp.float32
+        ).astype(jnp.bfloat16)
+        vocab_rows = emb_mine.shape[0]
+        ids = lax.broadcasted_iota(jnp.int32, (vocab_rows, chars_ref.shape[1]), 0)
+        onehot = jnp.where(chars_ref[...] == ids, 1.0, 0.0).astype(jnp.bfloat16)
+        summed = jnp.dot(onehot, into, preferred_element_type=jnp.float32)
+        lanes = lax.broadcasted_iota(jnp.int32, summed.shape, 1)
+        emb_mine[...] = jnp.where(lanes < embed, summed, 0.0) + extra_ref[...]
+        for slot in range(1, peers):
+            emb_copy(slot, group).start()
+
+    def small_partials():
+        for step in range(1, chips):
+            in_copy(step).wait_recv()
+        total = in_all[:, in_columns(chip)].astype(jnp.float32)
+        for step in range(1, chips):
+            total = total + in_box[step - 1].astype(jnp.float32)
+        in_mine[...] = total.astype(jnp.bfloat16)
+        send_partial(in_mine, in_part, in_final, in_sems)
+        for slot in range(1, peers):
+            emb_copy(slot, owner_of(slot)).wait_recv()
+        for slot in range(1, peers):
+            emb_copy(slot, group).wait_send()
+        emb_box[group] = emb_mine[...]
+        total = emb_box[0]
+        for source in range(1, peers):
+            total = total + emb_box[source]
+        emb_mine[...] = total
+        send_partial(emb_mine, emb_part, emb_final, emb_sems)
+
+    def small_finals():
+        pass_final(in_final, in_sems)
+        squares(in_final[...].astype(jnp.float32))
+        pass_final(emb_final, emb_sems)
+
+    order = list(range(2, peers)) + [1, 0]
+    lead = (peers - 2) * per_pass
+    y_lag, hop_lag = 3, 4
+    hops = jnp.where(low, middle - z, z - middle)
+    most_hops = max(middle, depth - 1 - middle)
+    steps = groups + y_lag + hop_lag * most_hops + lead
+    rounds = max(-(-steps // lot), 3 + most_hops)
+
+    def round_of(b, carry):
+        parity = lax.rem(b, 2)
+
+        @pl.when(b == 1)
+        def _():
+            small_products()
+
+        for turn, slot in enumerate(order):
+
+            @pl.when(b < batches)
+            def _():
+                block(slot, b, parity)
+
+            def step(j, inner):
+                row = b * lot + turn * per_pass + j - lead
+                arrived = row - y_lag
+                summed = arrived - hop_lag * hops
+
+                @pl.when(jnp.logical_and(row >= 0, row < groups))
+                def _():
+                    send(row)
+
+                @pl.when(jnp.logical_and(arrived >= 0, arrived < groups))
+                def _():
+                    take(arrived)
+
+                @pl.when(jnp.logical_and(summed >= 0, summed < groups))
+                def _():
+                    finish(summed)
+
+                return inner
+
+            lax.fori_loop(0, per_pass, step, 0)
+
+        @pl.when(b == 2)
+        def _():
+            small_partials()
+
+        @pl.when(b == 2 + hops)
+        def _():
+            small_finals()
+
+        return carry
+
+    lax.fori_loop(0, rounds, round_of, 0)
+
+    keep_cols = in_wide // 2
+    if in_wide > wide // 4:
+        mine = pl.ds(pl.multiple_of(core * keep_cols, keep_cols), keep_cols)
+        theirs = pl.ds(pl.multiple_of((1 - core) * keep_cols, keep_cols), keep_cols)
+        swap = remote(
+            in_final.at[:, theirs], in_swap, misc_send, misc_recv, in_group(owner_of(1))
+        )
+        swap.start()
+        swap.wait()
+        inout_ref[:, mine] = in_final[:, mine]
+        inout_ref[:, theirs] = in_swap[...]
+    else:
+        inout_ref[...] = in_final[...]
+    emb_ref[...] = emb_final[...]
+
+    ssq[...] = ssq[...] + decsq_ref[...]
+    norm_box[group] = ssq[...]
+
+    def norm_copy(slot, source):
+        return remote(
+            ssq,
+            norm_box.at[source],
+            norm_send.at[slot - 1],
+            norm_recv.at[source],
+            in_group(owner_of(slot)),
+        )
+
+    for slot in range(1, peers):
+        norm_copy(slot, group).start()
+    for slot in range(1, peers):
+        norm_copy(slot, owner_of(slot)).wait_recv()
+    for slot in range(1, peers):
+        norm_copy(slot, group).wait_send()
+    total = norm_box[0]
+    for source in range(1, peers):
+        total = total + norm_box[source]
+    lanes = lax.broadcasted_iota(jnp.int32, emb_final.shape, 1)
+    small = jnp.where(lanes <= embed, emb_final[...], 0.0)
+    total_sq = jnp.sum(total) + jnp.sum(small * small)
+    clip_ref[...] = jnp.full(clip_ref.shape, 0.25, jnp.float32) / jnp.maximum(
+        jnp.sqrt(jnp.full(clip_ref.shape, total_sq, jnp.float32)), 0.25
+    )
+
+    for step in range(1, chips):
+        in_copy(step).wait_send()
+    wait_line(in_mine, in_final, in_sems)
+    wait_line(emb_mine, emb_final, emb_sems)
+    for slot in range(1, peers):
+        for parity in range(min(2, batches)):
+            for index in range(lot):
+                send_block(slot, parity, index, 0).wait_send()
+
+    def settle(row, carry):
+        for part in range(2):
+            wait_line(
+                inbox.at[part, row], final.at[2 * row + part], line_sems(2 * row + part)
+            )
+            write_out(row, part).wait()
+        return carry
+
+    lax.fori_loop(0, groups, settle, 0)
+
+
+def run_reduce(chips, depth, embed, kept, aug, pre, in_own, chars, extra, dec_sq):
+    hidden = kept.shape[1]
+    count, wide = pre.shape
+    peers = 2 * chips
+    rows_out = hidden // peers
+    tall = 128
+    lot = tall // 16
+    groups = rows_out // 16
+    units = 2 * groups
+    in_rows = -(-(embed + 1) // 16) * 16
+    in_wide = wide // chips
+    in_cols = 2 * wide // peers
+    vmem = pl.BlockSpec(memory_space=pltpu.VMEM)
+    bf16, f32 = jnp.bfloat16, jnp.float32
+    small = extra.shape
+    dma = pltpu.SemaphoreType.DMA
+    return pl.pallas_call(
+        functools.partial(reduce_kernel, chips, depth, embed),
+        in_specs=[vmem] * 7,
+        out_specs=[pl.BlockSpec(memory_space=pl.ANY), vmem, vmem, vmem],
+        out_shape=[
+            jax.ShapeDtypeStruct((2, rows_out, wide), bf16),
+            jax.ShapeDtypeStruct((in_rows, in_cols), bf16),
+            jax.ShapeDtypeStruct(small, f32),
+            jax.ShapeDtypeStruct((8, 128), f32),
+        ],
+        scratch_shapes=[
+            pltpu.VMEM((tall, count), bf16),
+            pltpu.VMEM((peers, groups, 16, wide), bf16),
+            pltpu.VMEM((peers - 1, 2, lot, 16, wide), bf16),
+            pltpu.VMEM((units, 16, wide), bf16),
+            pltpu.VMEM((units, 16, wide), bf16),
+            pltpu.VMEM((in_rows, wide), bf16),
+            pltpu.VMEM((max(chips - 1, 1), in_rows, in_wide), bf16),
+            pltpu.VMEM((in_rows, in_wide), bf16),
+            pltpu.VMEM((in_rows, in_wide), bf16),
+            pltpu.VMEM((in_rows, in_wide), bf16),
+            pltpu.VMEM((in_rows, in_wide // 2), bf16),
+            pltpu.VMEM((peers,) + small, f32),
+            pltpu.VMEM(small, f32),
+            pltpu.VMEM(small, f32),
+            pltpu.VMEM(small, f32),
+            pltpu.VMEM((16, 128), f32),
+            pltpu.VMEM((peers, 16, 128), f32),
+            dma((peers - 1, 2, lot)),
+            dma((peers - 1, groups)),
+            dma((units + 2,)),
+            dma((units + 2,)),
+            dma((units + 2,)),
+            dma((2, units + 2)),
+            dma((units,)),
+            dma((max(chips - 1, 1),)),
+            dma((max(chips - 1, 1),)),
+            dma((peers - 1,)),
+            dma((peers,)),
+            dma,
+            dma,
+            dma((peers - 1,)),
+            dma((peers,)),
+        ],
+        compiler_params=pltpu.CompilerParams(
+            collective_id=3, has_side_effects=True, vmem_limit_bytes=60 << 20
+        ),
+        cost_estimate=pl.CostEstimate(
+            flops=2 * count * hidden * wide, bytes_accessed=700 << 20, transcendentals=0
+        ),
+    )(kept, aug, pre, in_own, chars, extra, dec_sq)
+
+
+def momentum_kernel(clip_ref, sum_ref, moment_ref, grad_ref, next_ref):
+    gradient = sum_ref[0].astype(jnp.float32)
+    grad_ref[0] = gradient
+    next_ref[0] = momentum_step(moment_ref[0], gradient, clip_ref[0, 0])
+
+
+def run_momentum(clip, sums, moment):
+    halves, rows, wide = sums.shape
+    span = wide // 4
+    block = pl.BlockSpec((1, rows, span), lambda q, s: (0, 0, 2 * q + s))
+    shape = jax.ShapeDtypeStruct(moment.shape, jnp.float32)
+    return pl.pallas_call(
+        momentum_kernel,
+        grid=(4, 2),
+        in_specs=[
+            pl.BlockSpec(memory_space=pltpu.SMEM),
+            pl.BlockSpec((1, rows, span), lambda q, s: (s, 0, q)),
+            block,
+        ],
+        out_specs=[block, block],
+        out_shape=[shape, shape],
+        compiler_params=pltpu.CompilerParams(vmem_limit_bytes=48 << 20),
+    )(clip, sums, moment)
+
+
 def shards(
     chars,
     targets,
@@ -411,14 +966,6 @@
             axis=1,
         )
 
-    def spread(value):
-        wide = jnp.zeros((value.shape[0], 4 * hidden_size), value.dtype)
-        for q in range(4):
-            wide = lax.dynamic_update_slice_in_dim(
-                wide, value[:, q * units : (q + 1) * units], q * hidden_size + core * units, 1
-            )
-        return wide
-
     in_full, rec_full, bias_full, dec_full = (
         lax.all_gather(w_in[0].astype(jnp.bfloat16), "group", axis=1, tiled=True),
         lax.all_gather(w_rec[0].astype(jnp.bfloat16), "group", axis=0, tiled=True),
@@ -535,53 +1082,39 @@
 
     grad_hidden0 = own_rows(gh_pair)
     grad_cell0 = own_rows(gc_pair)
-    rec_grad = spread(
-        jnp.einsum("tbh,tbg->hg", kept_all, pre_all, preferred_element_type=jnp.float32).astype(
-            jnp.bfloat16
-        )
-    )
-    in_grad = spread(
-        jnp.einsum("tbe,tbg->eg", embedded, pre_all, preferred_element_type=jnp.float32).astype(
-            jnp.bfloat16
-        )
-    )
-    bias_grad = spread(jnp.sum(pre_all, axis=(0, 1), dtype=jnp.float32).astype(jnp.bfloat16)[None])[0]
     lg_own = lax.dynamic_slice_in_dim(logit_grad, core * batch_size, batch_size, 1)
     dec_grad = jnp.einsum("tbh,tbv->hv", out_own, lg_own, preferred_element_type=jnp.float32)
     dbias_grad = jnp.sum(lg_own, axis=(0, 1), dtype=jnp.float32)
-    embed_in = jnp.einsum("tbg,eg->tbe", pre_all, in_own, preferred_element_type=jnp.float32)
-    emb_grad = jnp.einsum(
-        "tbv,tbe->ve", char_onehot.astype(jnp.float32), embed_in, precision=lax.Precision.HIGHEST
-    )
-    loss_part = jnp.reshape(loss_part, (1,))
-    in_sum, rec_sum, bias_sum, dec_sum = (
-        lax.psum_scatter(in_grad, "group", scatter_dimension=1, tiled=True).astype(jnp.float32),
-        lax.psum_scatter(rec_grad, "group", scatter_dimension=0, tiled=True).astype(jnp.float32),
-        lax.psum_scatter(bias_grad, "group", scatter_dimension=0, tiled=True).astype(jnp.float32),
-        lax.psum_scatter(
-            dec_grad.astype(jnp.bfloat16), "group", scatter_dimension=0, tiled=True
-        ).astype(jnp.float32),
-    )
-    in_sum, rec_sum, bias_sum, dec_sum, emb_sum, dbias_sum, loss_sum = (
-        lax.psum(in_sum.astype(jnp.bfloat16), "dp").astype(jnp.float32),
-        lax.psum(rec_sum.astype(jnp.bfloat16), "dp").astype(jnp.float32),
-        lax.psum(bias_sum.astype(jnp.bfloat16), "dp").astype(jnp.float32),
-        lax.psum(dec_sum.astype(jnp.bfloat16), "dp").astype(jnp.float32),
-        lax.psum(emb_grad.astype(jnp.bfloat16), "dp").astype(jnp.float32),
-        lax.psum(dbias_grad.astype(jnp.bfloat16), "dp").astype(jnp.float32),
-        lax.psum(loss_part.astype(jnp.bfloat16), "dp").astype(jnp.float32),
-    )
-    shard_sq = squares_of((in_sum, rec_sum, bias_sum, dec_sum))
-    shard_sq, emb_sum, dbias_sum, loss_sum = (
-        lax.psum(shard_sq.astype(jnp.bfloat16), "group").astype(jnp.float32),
-        lax.psum(emb_sum.astype(jnp.bfloat16), "group").astype(jnp.float32),
-        lax.psum(dbias_sum.astype(jnp.bfloat16), "group").astype(jnp.float32),
-        lax.psum(loss_sum.astype(jnp.bfloat16), "group").astype(jnp.float32),
-    )
-    total_sq = shard_sq + squares_of((emb_sum, dbias_sum))
-    clip_scale = 0.25 / jnp.maximum(jnp.sqrt(total_sq), 0.25)
+    dec_sum = lax.psum_scatter(
+        dec_grad.astype(jnp.bfloat16), "group", scatter_dimension=0, tiled=True
+    )
+    dec_sum = lax.psum(dec_sum, "dp").astype(jnp.float32)
+    vocab_rows = -(-vocab_size // 32) * 32
+    extra = jnp.zeros((vocab_rows, depth), jnp.float32)
+    extra = lax.dynamic_update_slice(extra, dbias_grad[:, None], (0, embed_size))
+    extra = lax.dynamic_update_slice(extra, loss_part.reshape(1, 1), (0, embed_size + 1))
+    dec_sq = jnp.zeros((16, 128), jnp.float32).at[0, 0].set(jnp.sum(dec_sum * dec_sum))
+    positions = seg_len * 2 * batch_size
+    rec_sum, in_out, emb_out, clip = run_reduce(
+        lax.axis_size("group") // 2,
+        lax.axis_size("dp"),
+        embed_size,
+        kept_all.reshape(positions, hidden_size),
+        embedded_one.reshape(positions, depth),
+        pre_all.reshape(positions, 4 * units),
+        weights[hidden_size:],
+        char_major.reshape(1, positions),
+        extra,
+        dec_sq,
+    )
+    rec_grad, mom_rec_next = run_momentum(clip, rec_sum, mom_rec)
+    clip_scale = clip[0, 0]
+    in_sum = in_out[:embed_size].astype(jnp.float32)
+    bias_sum = in_out[embed_size].astype(jnp.float32)
+    emb_sum = emb_out[:vocab_size, :embed_size]
+    dbias_sum = emb_out[:vocab_size, embed_size]
+    loss_sum = emb_out[0, embed_size + 1].reshape(1)
     mom_in_next = momentum_step(mom_in[0], in_sum, clip_scale)
-    mom_rec_next = momentum_step(mom_rec[0], rec_sum, clip_scale)
     mom_bias_next = momentum_step(mom_bias[0], bias_sum, clip_scale)
     mom_dec_next = momentum_step(mom_dec[0], dec_sum, clip_scale)
     mom_emb_next = momentum_step(mom_emb[0], emb_sum, clip_scale)
@@ -595,13 +1128,13 @@
         grad_cell0[None],
         emb_sum[None],
         in_sum[None],
-        rec_sum[None],
+        rec_grad,
         bias_sum[None],
         dec_sum[None],
         dbias_sum[None],
         mom_emb_next[None],
         mom_in_next[None],
-        mom_rec_next[None],
+        mom_rec_next,
         mom_bias_next[None],
         mom_dec_next[None],
         mom_dbias_next[None],

time: 1280 us -> 973 us (0.76)
  waiting for transfers between devices: 684 us -> 222 us
  Pallas kernels: 219 us -> 527 us
  blocking collectives: 55.6 us -> 6.37 us
  other arithmetic: 75 us -> 33.4 us
  matrix products: 62.7 us -> 23.7 us
  local copies, waits for them, and re-layouts: 147 us -> 129 us
    pallas_call x0 -> x2, Pallas kernels: none -> 307 us  [the longest x1 287 us: run_reduce(): pl.pallas_call(functools.partial(reduce_kernel, chips, depth, embed), in_...]
    unnamed x8 -> x5, waiting for transfers between devices: 235 us -> 0.08 us
    psum x1, waiting for transfers between devices: 250 us -> 25.9 us  [shards(): dec_sum = lax.psum(dec_sum, 'dp').astype(jnp.float32)]
    dot_general x4 -> x0, matrix products: 38.3 us -> none  [the longest x1 26 us: shards(): jnp.einsum('tbh,tbg->hg', kept_all, pre_all, preferred_element_type=jnp.f...]
    psum x2 -> x0, blocking collectives: 38 us -> none  [the longest x1 24.5 us: shards(): lax.psum(loss_part.astype(jnp.bfloat16), 'dp').astype(jnp.float32)]
    broadcast_in_dim x3 -> x2, other arithmetic: 25.8 us -> 1.15 us  [the longest x1 1.08 us: shards(): mom_in_next[None]]
    reduce_sum x7 -> x1, other arithmetic: 17.9 us -> 1.71 us  [shards(): jnp.sum(dec_sum * dec_sum)]
    broadcast_in_dim x7 -> x1, local copies, waits for them, and re-layouts: 15 us -> 0.09 us  [shards(): dbias_grad[:, None]]
  transfers between devices with their start and end apart: 14 -> 12, of which waited for: 4 -> 3; matrix products, arithmetic and copies ran while one was open for 17% -> 16% of each run, Pallas kernels for 17% -> 23%
where the time goes in v2:
time: 973 us; the launch traced here: 962 us
  Pallas kernels  527 us (54%)
  waiting for transfers between devices  222 us (23%)
  local copies, waits for them, and re-layouts  129 us (13%)
  other arithmetic  33.4 us (3%)
  matrix products  23.7 us (2%)
  between operations  17.2 us (2%)
    pallas_call x1, Pallas kernels, run_reduce(): pl.pallas_call(functools.partial(reduce_kernel, chips, depth, embed), in_...  287 us
    all_gather x1, waiting for transfers between devices, shards(): lax.all_gather(w_rec[0].astype(jnp.bfloat16), 'group', axis=0, tiled=True)  189 us
    pallas_call x1, Pallas kernels, run_backward(): pl.pallas_call(functools.partial(backward_kernel, steps), grid=(steps,),...  114 us
    pallas_call x1, Pallas kernels, run_forward(): pl.pallas_call(functools.partial(forward_kernel, steps), grid=(steps + 1,...  106 us
    concatenate x2, local copies, waits for them, and re-layouts, shards(): jnp.concatenate([rec_own, in_own, bias_own, jnp.zeros((depth - embed_size...  48.8 us
    psum x1, waiting for transfers between devices, shards(): dec_sum = lax.psum(dec_sum, 'dp').astype(jnp.float32)  25.9 us
    unnamed x59, local copies, waits for them, and re-layouts  25.4 us
    slice x3, local copies, waits for them, and re-layouts, own_columns(): value[:, q * hidden_size:(q + 1) * hidden_size]  23.1 us
  transfers between devices with their start and end apart: 12, of which 3 were waited for; matrix products, arithmetic and copies ran while one was open for 16% of the time, Pallas kernels for 23%

profile of v2, /device:TPU:0, one launch (start us, length us, event | category | flops | bytes accessed | tf_op | source)
XLA Modules:
  0.0 962.2 jit_solution(6299680904016881277)
XLA Ops:
  7.2 2.1 copy.109
  9.4 13.8 %copy.64 = bf16[1,512,8192]{1,2,0:T(8,128)(2,1)} copy(f32[1,512,8192]{2,1,0:T(8,128)} %param.30) | data formatting | bytes 25165824 | tf_op args[9]
  26.6 6.4 all-gather.2
  38.8 4.6 fusion.17
  43.4 2.2 fusion.42
  48.3 188.6 %all-gather.8.cloned.1.call-done = bf16[1,2048,8192]{1,2,0:T(8,128)(2,1)} async-done(((bf16[1,512,8192]{1,2,0:T(8,128)(2,1)}), bf16[1,2048,8192]{1,2,0:T(8,128)(2,1)}) %all-gather.8.cloned.1.call-update) | async-done | bytes 33554448 | tf_op jit(solution)/shard_map/all_gather | solution.py:971
  237.0 20.8 %fusion.41 = (bf16[2048,2048]{0,1:T(8,128)(2,1)}, bf16[2048,2048]{0,1:T(8,128)(2,1)S(1)}, bf16[2048,2048]{0,1:T(8,128)(2,1)}, bf16[2048,2048]{0,1:T(8,128)(2,1)}) fusion(bf16[2048,8192]{0,1:T(8,128)(2,1)} %bitcast.77), kind=kLoop, calls=%fused_computation.108 | loop fusion | bytes 67108864 | tf_op jit(solution)/shard_map/slice | solution.py:965
  257.8 6.7 constant_dynamic-slice_fusion.17
  264.5 6.7 constant_dynamic-slice_fusion.15
  271.2 16.0 %fusion.40 = (bf16[4096,2048]{1,0:T(8,128)(2,1)}, bf16[2048,4096]{0,1:T(8,128)(2,1)}) fusion(bf16[2048,1024]{0,1:T(8,128)(2,1)} %get-tuple-element.129, bf16[2048,1024]{0,1:T(8,128)(2,1)} %get-tuple-element.130, bf16[2048,1024]{0,1:T(8,128)(2,1)S(1)} %get-tuple-element.131, bf16[2048,1024]{0,1:T(8,128)(2,1)} %get-tuple-element.132), kind=kLoop, calls=%fused_computation.107 | loop fusion | flops 67108864 | bytes 50331648 | tf_op jit(solution)/shard_map/transpose | solution.py:1070
  287.3 25.9 %concatenate.112 = bf16[2176,4096]{0,1:T(8,128)(2,1)} concatenate(bf16[2048,4096]{0,1:T(8,128)(2,1)} %get-tuple-element.95, bf16[100,4096]{0,1:T(8,128)(2,1)} %copy.66, bf16[1,4096]{0,1:T(8,128)(2,1)S(1)} %copy.67, bf16[27,4096]{0,1:T(8,128)(2,1)S(1)} %broadcast_in_dim.32.clone), dimensions={0} | concatenate | bytes 35651584 | tf_op jit(solution)/shard_map/concatenate | solution.py:995
  313.2 22.9 %copy.69.w_hbm = bf16[2176,4096]{1,0:T(8,128)(2,1)} copy(bf16[2176,4096]{0,1:T(8,128)(2,1)} %concatenate.112) | data formatting | bytes 35651584 | tf_op jit(solution)/shard_map/concatenate | solution.py:995
  337.2 105.9 %shard_map.306 = (bf16[25,48,2048]{2,1,0:T(8,128)(2,1)}, bf16[24,48,2048]{2,1,0:T(8,128)(2,1)}, f32[24,4,48,1024]{3,2,1,0:T(8,128)}, f32[24,48,1024]{2,1,0:T(8,128)}, f32[24,48,1024]{2,1,0:T(8,128)}) custom-call(bf16[24,48,128]{2,1,0:T(8,128)(2,1)} %maximum_maximum_fusion.1.emb_ref, f32[24,48,128]{2,1,0:T(8,128)} %broadcast_in_dim.30.keep_ref, ...), custom_call_target="tpu_custom_call" | custom-call | flops 20535312384 | bytes 524288000 | tf_op jit(solution)/shard_map/pallas_call | solution.py:170
  443.1 5.2 slice.101
  448.3 5.4 fusion.6
  453.7 2.6 select_reduce_fusion
  456.3 2.1 fusion.2
  458.5 8.0 bitcast_add_fusion.outg_ref
  466.5 114.2 %shard_map.307 = (bf16[24,48,4096]{2,1,0:T(8,128)(2,1)}, f32[48,1024]{1,0:T(8,128)}, f32[48,1024]{1,0:T(8,128)}) custom-call(f32[24,48,1024]{2,1,0:T(8,128)} %bitcast_add_fusion.outg_ref, f32[24,4,48,1024]{3,2,1,0:T(8,128)} %get-tuple-element.44.gates_ref, f32[24,48,1024]{2,1,0:T(8,128)} %get-tuple-element.45.cell_ref, ...), custom_call_target="tpu_custom_call" | custom-call | flops 19327352832 | bytes 524288000 | tf_op jit(solution)/shard_map/pallas_call | solution.py:325
  583.6 3.1 convolution_convert_fusion
  591.1 7.5 collective-permute-done.4
  600.1 25.9 %all-reduce.4.cloned.1.call-done = bf16[512,275]{0,1:T(8,128)(2,1)} async-done(((bf16[512,275]{0,1:T(8,128)(2,1)}), bf16[512,275]{0,1:T(8,128)(2,1)}) %all-reduce.4.cloned.1.call-update) | async-done | bytes 281616 | tf_op jit(solution)/shard_map/psum | solution.py:1091
  629.0 287.2 %shard_map.308 = (bf16[2,512,4096]{2,1,0:T(8,128)(2,1)}, bf16[112,2048]{1,0:T(8,128)(2,1)}, f32[288,128]{1,0:T(8,128)}, f32[8,128]{1,0:T(8,128)}) custom-call(bf16[1152,2048]{1,0:T(8,128)(2,1)} %bitcast.92, bf16[1152,128]{1,0:T(8,128)(2,1)} %bitcast.81, bf16[1152,4096]{1,0:T(8,128)(2,1)} %bitcast.91, bf16[128,4096]{1,0:T(8,128)(2,1)} %maximum_maximum_fusion.in_ref, ...), custom_call_target="tpu_custom_call" | custom-call | flops 19327352832 | bytes 734003200 | tf_op jit(solution)/shard_map/pallas_call | solution.py:848
  933.5 19.9 %shard_map.309 = (f32[1,512,8192]{2,1,0:T(8,128)}, f32[1,512,8192]{2,1,0:T(8,128)}) custom-call(f32[8,128]{1,0:T(8,128)S(1)} %copy-done, bf16[2,512,4096]{2,1,0:T(8,128)(2,1)} %get-tuple-element.53.sum_ref, f32[1,512,8192]{2,1,0:T(8,128)} %moment_ref.1), custom_call_target="tpu_custom_call" | custom-call | tf_op jit(solution)/shard_map/pallas_call | solution.py:912
  (142 shorter events, 41.3 us)
Async XLA Ops:
  7.2 36.2 %all-gather.10.cloned.1.call-start = ((), (), s32[]{:S(2)}) async-start(), calls=%async_computation.4 | async-start | bytes 2129920 | tf_op jit(solution)/shard_map/all_gather | solution.py:970
  9.4 227.6 %all-gather.8.cloned.1.call-start = ((), (), s32[]{:S(2)}) async-start(), calls=%async_computation.3 | async-start | bytes 41943040 | tf_op jit(solution)/shard_map/all_gather | solution.py:971
  23.4 424.9 %all-gather.12.cloned.1.call-start = ((), (), s32[]{:S(2)}) async-start(), calls=%async_computation.5 | async-start | bytes 1433600 | tf_op jit(solution)/shard_map/all_gather | solution.py:973
  24.2 9.4 copy-start.13
  24.2 9.7 %copy-start.21 = (f32[1,275]{1,0:T(1,128)S(1)}, f32[1,275]{1,0:T(1,128)}, u32[]{:S(2)}) copy-start(f32[1,275]{1,0:T(1,128)} %param.33) | copy-start | bytes 3304
  24.2 12.1 %collective-permute-start.2 = (f32[24,1024]{1,0:T(8,128)S(1)}, f32[24,1024]{1,0:T(8,128)S(1)}, u32[]{:S(2)}, u32[]{:S(2)}) collective-permute-start(f32[24,1024]{1,0:T(8,128)S(1)} %get-tuple-element.111), channel_id=1, source_target_pairs={{0,4},{4,0},{8,12},{12,8},{1,5},{5,1},{9,13},{13,9},{2,6},{6,2},{1... | collective-permute-start | bytes 294920 | tf_op jit(solution)/shard_map/ppermute | solution.py:17
  24.9 8.9 collective-permute-start
  25.0 12.1 %collective-permute-start.1 = (bf16[24,2048]{1,0:T(8,128)(2,1)S(1)}, bf16[24,2048]{1,0:T(8,128)(2,1)}, u32[]{:S(2)}, u32[]{:S(2)}) collective-permute-start(bf16[24,2048]{1,0:T(8,128)(2,1)S(1)} %convert_bitcast_fusion.2), channel_id=1, source_target_pairs={{0,4},{4,0},{8,12},{12,8},{1,5},{5,1},{9,13},{13,9},{2,6},{6,2},{1... | collective-permute-start | bytes 294920 | tf_op jit(solution)/shard_map/ppermute | solution.py:17
  25.6 13.1 %collective-permute-start.3 = (bf16[24,8,1024]{2,1,0:T(8,128)(2,1)S(1)}, bf16[24,8,1024]{2,1,0:T(8,128)(2,1)S(1)}, u32[]{:S(2)}, u32[]{:S(2)}) collective-permute-start(bf16[24,8,1024]{2,1,0:T(8,128)(2,1)S(1)} %get-tuple-element.105), channel_id=1, source_target_pairs={{0,4},{4,0},{8,12},{12,8},{1,5},{5,1},{9,13},{13,9},{2,6},{6,2},{1... | collective-permute-start | bytes 1179656 | tf_op jit(solution)/shard_map/ppermute | solution.py:17
  26.5 564.5 %reduce-scatter.2.cloned.1.call-start = ((), (), s32[]{:S(2)}) async-start(), calls=%async_computation.1 | async-start | bytes 1433600 | tf_op jit(solution)/shard_map/reduce_scatter | solution.py:1088
  458.4 167.6 %all-reduce.4.cloned.1.call-start = ((), (), s32[]{:S(2)}) async-start(), calls=%async_computation.2 | async-start | bytes 573440 | tf_op jit(solution)/shard_map/psum | solution.py:1091
  466.5 117.0 %slice-start = ((s8[4718592]{0:T(1024)(128)(4,1)}), s8[4194304]{0:T(1024)(128)(4,1)S(1)}, s32[]{:S(2)}) async-start(s8[4718592]{0:T(1024)(128)(4,1)} %bitcast.78), calls=%async_computation.6 | async-start | bytes 8388608
  466.5 117.0 %slice-start.1 = ((s8[4718592]{0:T(1024)(128)(4,1)}), s8[524288]{0:T(1024)(128)(4,1)S(1)}, s32[]{:S(2)}) async-start(s8[4718592]{0:T(1024)(128)(4,1)} %bitcast.78), calls=%async_computation.7 | async-start | bytes 1048576
  581.9 7.7 collective-permute-start.6
  583.2 7.2 collective-permute-start.5
  587.2 11.3 %collective-permute-start.4 = (bf16[24,4,2048]{2,1,0:T(4,128)(2,1)S(1)}, bf16[24,4,2048]{2,1,0:T(4,128)(2,1)S(1)}, u32[]{:S(2)}, u32[]{:S(2)}) collective-permute-start(bf16[24,4,2048]{2,1,0:T(4,128)(2,1)S(1)} %get-tuple-element.103), channel_id=1, source_target_pairs={{0,16},{16,0},{1,17},{17,1},{2,18},{18,2},{3,19},{19,3},{4,20},{20... | collective-permute-start | bytes 1179656 | tf_op jit(solution)/shard_map/ppermute | solution.py:17
  589.6 39.4 %copy-start.12 = (f32[288,128]{1,0:T(8,128)}, f32[288,128]{1,0:T(8,128)S(1)}, u32[]{:S(2)}) copy-start(f32[288,128]{1,0:T(8,128)S(1)} %dynamic_update_slice.7.extra_ref) | copy-start | bytes 442372
  629.0 291.5 %copy-start.22 = (f32[1,275]{1,0:T(1,128)S(1)}, f32[1,275]{1,0:T(1,128)}, u32[]{:S(2)}) copy-start(f32[1,275]{1,0:T(1,128)} %param.39) | copy-start | bytes 3304
  629.0 292.7 %copy-start.2 = (bf16[512,275]{0,1:T(8,128)(2,1)S(1)}, bf16[512,275]{0,1:T(8,128)(2,1)}, u32[]{:S(2)}) copy-start(bf16[512,275]{0,1:T(8,128)(2,1)} %all-reduce.4.cloned.1.call-done) | copy-start | bytes 844804
  629.0 292.7 %copy-start.7 = (f32[1,512,275]{1,0,2:T(1,128)S(1)}, f32[1,512,275]{1,0,2:T(1,128)}, u32[]{:S(2)}) copy-start(f32[1,512,275]{1,0,2:T(1,128)} %param.38) | copy-start | bytes 1689604
  916.2 7.6 copy-start.3
  916.2 7.7 copy-start.4
  923.8 4.2 copy-start.14
  928.0 5.5 copy-start
  (13 other events, 28.7 us)
Sparse Core Ops, SparseCore 0:
  10.2 23.1 all-gather.9
  35.5 201.4 all-gather.7
  239.1 17.2 all-gather.11
  458.6 25.4 reduce-scatter.1
  591.2 34.8 all-reduce.3

commit v3 on v2

--- a/solution.py
+++ b/solution.py
@@ -36,6 +36,408 @@
     for peer in peers:
         pl.semaphore_signal(barrier, inc=1, device_id=peer, device_id_type=MESH)
     pl.semaphore_wait(barrier, len(peers))
+
+
+def gather_kernel(
+    chips,
+    shared,
+    rec_hbm,
+    inb_ref,
+    h_ref,
+    c_ref,
+    wg_ref,
+    ids_ref,
+    w_hbm,
+    wt_hbm,
+    h_out,
+    c_out,
+    wg_out,
+    ids_out,
+    w_ref,
+    wt_ref,
+    stage,
+    loaded,
+    load_sem,
+    core_send,
+    core_recv,
+    y_send,
+    y_recv,
+    z_send,
+    z_recv,
+    in_send,
+    in_recv,
+    inz_send,
+    inz_recv,
+    seg_send,
+    seg_recv,
+    w_out_sem,
+    wt_out_sem,
+):
+    model = lax.axis_index("dir")
+    group = lax.axis_index("group")
+    z = lax.axis_index("dp")
+    core = lax.rem(group, 2)
+    chip = group // 2
+    peers = 2 * chips
+    rows = stage.shape[0]
+    piece = loaded.shape[1]
+    units = w_ref.shape[1] // 4
+    hidden = 2 * units
+    pieces = rows // piece
+    mine = pieces // 2 if shared else pieces
+    part = lax.rem(z, 2) if shared else 0
+    buddy = z + 1 - 2 * lax.rem(z, 2) if shared else z
+    far = list(range(2, peers))
+
+    def owner_of(slot):
+        if slot == 0:
+            return group
+        if slot == 1:
+            return group + 1 - 2 * core
+        side = core if slot % 2 == 0 else 1 - core
+        return 2 * lax.rem(chip + (slot - 2) // 2 + 1, chips) + side
+
+    def slot_there(slot):
+        if slot == 1:
+            return 1
+        return 2 + 2 * (chips - (slot - 2) // 2 - 2) + slot % 2
+
+    def peer(slot):
+        return (model, owner_of(slot), z)
+
+    barrier = pltpu.get_barrier_semaphore()
+    for slot in range(1, peers):
+        pl.semaphore_signal(barrier, inc=1, device_id=peer(slot), device_id_type=MESH)
+    if shared:
+        pl.semaphore_signal(
+            barrier, inc=1, device_id=(model, group, buddy), device_id_type=MESH
+        )
+
+    def remote(src, dst, send, recv, device):
+        return pltpu.make_async_remote_copy(
+            src_ref=src,
+            dst_ref=dst,
+            send_sem=send,
+            recv_sem=recv,
+            device_id=device,
+            device_id_type=MESH,
+        )
+
+    def which(i):
+        return lax.rem(part * mine + i, pieces)
+
+    def load(i):
+        return pltpu.make_async_copy(
+            rec_hbm.at[pl.ds(pl.multiple_of(which(i) * piece, piece), piece)],
+            loaded.at[lax.rem(i, 2)],
+            load_sem.at[lax.rem(i, 2)],
+        )
+
+    load(0).start()
+    pl.semaphore_wait(barrier, peers if shared else peers - 1)
+
+    def rows_of(owner, k):
+        return pl.ds(pl.multiple_of(owner * rows + k * piece, piece), piece)
+
+    def rows_staged(k):
+        return pl.ds(pl.multiple_of(k * piece, piece), piece)
+
+    def to_core(k):
+        return remote(
+            stage.at[rows_staged(k)],
+            w_ref.at[rows_of(group, k)],
+            core_send.at[k],
+            core_recv.at[k],
+            peer(1),
+        )
+
+    def to_chip(slot, k):
+        held = w_ref.at[rows_of(group, k)] if slot % 2 == 0 else stage.at[rows_staged(k)]
+        return remote(
+            held,
+            w_ref.at[rows_of(group, k)],
+            y_send.at[slot - 2, k],
+            y_recv.at[slot_there(slot) - 2, k],
+            peer(slot),
+        )
+
+    def to_buddy(slot, k):
+        return remote(
+            w_ref.at[rows_of(owner_of(slot), k)],
+            w_ref.at[rows_of(owner_of(slot), k)],
+            z_send.at[slot - 2, k],
+            z_recv.at[slot - 2, k],
+            (model, group, buddy),
+        )
+
+    blocks = inb_ref.shape[1] // units
+    deep = inb_ref.shape[0]
+    in_slots = list(range(peers)) if blocks == 2 else [0] + [s for s in far if s % 2 == 0]
+    share_rows = deep // 2 if shared else deep
+
+    def in_place(owner, first, count):
+        gate = owner if blocks == 2 else owner // 2
+        return w_ref.at[
+            pl.ds(pl.multiple_of(hidden + first, 16), count),
+            pl.ds(pl.multiple_of(gate * units, units), units),
+        ]
+
+    def in_block(slot):
+        if blocks == 1:
+            return 0
+        return core if slot == 0 or (slot > 1 and slot % 2 == 0) else 1 - core
+
+    def in_copy(slot):
+        first, count = (0, deep) if slot == 1 else (part * share_rows, share_rows)
+        source = inb_ref.at[
+            pl.ds(pl.multiple_of(first, 16), count),
+            pl.ds(pl.multiple_of(in_block(slot) * units, units), units),
+        ]
+        return remote(
+            source,
+            in_place(group, first, count),
+            in_send.at[slot - 1],
+            in_recv.at[slot_there(slot) - 1],
+            peer(slot),
+        )
+
+    def in_buddy(slot):
+        held = in_place(owner_of(slot), part * share_rows, share_rows)
+        return remote(
+            held, held, inz_send.at[slot - 1], inz_recv.at[slot - 1], (model, group, buddy)
+        )
+
+    for slot in in_slots:
+        if slot > 1:
+            in_copy(slot).start()
+    gate0 = group if blocks == 2 else chip
+    w_ref[hidden:, pl.ds(pl.multiple_of(gate0 * units, units), units)] = inb_ref[
+        :, pl.ds(pl.multiple_of(in_block(0) * units, units), units)
+    ]
+
+    def cast(i, carry):
+        k = which(i)
+
+        @pl.when(i + 1 < pieces)
+        def _():
+            load(i + 1).start()
+
+        load(i).wait()
+        buffer = lax.rem(i, 2)
+        for q in range(4):
+            local = pl.ds(q * units, units)
+            own = pl.ds(pl.multiple_of(q * hidden + core * units, units), units)
+            other = pl.ds(pl.multiple_of(q * hidden + (1 - core) * units, units), units)
+            w_ref[rows_of(group, k), local] = loaded[buffer, :, own].astype(jnp.bfloat16)
+            stage[rows_staged(k), local] = loaded[buffer, :, other].astype(jnp.bfloat16)
+
+        @pl.when(i < mine)
+        def _():
+            for slot in far:
+                to_chip(slot, k).start()
+
+        to_core(k).start()
+        return carry
+
+    lax.fori_loop(0, pieces, cast, 0)
+
+    seg = h_ref.shape[0]
+    words = wg_ref.shape[0]
+    at_h = pl.ds(pl.multiple_of(core * seg, 8), seg)
+    at_w = pl.ds(pl.multiple_of(core * words, 16), words)
+    half_own = pl.ds(pl.multiple_of(core * units, units), units)
+    half_other = pl.ds(pl.multiple_of((1 - core) * units, units), units)
+    segment_copies = [
+        remote(h_ref, h_out.at[at_h], seg_send.at[0], seg_recv.at[0], peer(1)),
+        remote(c_ref.at[:, half_other], c_out.at[at_h], seg_send.at[1], seg_recv.at[1], peer(1)),
+        remote(wg_ref.at[:, half_other], wg_out.at[at_w], seg_send.at[2], seg_recv.at[2], peer(1)),
+        remote(ids_ref, ids_out.at[at_h], seg_send.at[3], seg_recv.at[3], peer(1)),
+    ]
+    if blocks == 2:
+        in_copy(1).start()
+    for copy in segment_copies:
+        copy.start()
+    h_out[at_h] = h_ref[...]
+    c_out[at_h] = c_ref[:, half_own]
+    wg_out[at_w] = wg_ref[:, half_own]
+    ids_out[at_h] = ids_ref[...]
+
+    tall = 128
+
+    def turn(row0):
+        at = pl.ds(pl.multiple_of(row0, tall), tall)
+        for q in range(4):
+            local = pl.ds(q * units, units)
+            wt_ref[local, at] = jnp.transpose(w_ref[at, local])
+
+    def store(row0):
+        at = pl.ds(pl.multiple_of(row0, tall), tall)
+        index = row0 // tall
+        return (
+            pltpu.make_async_copy(w_ref.at[at], w_hbm.at[at], w_out_sem.at[index]),
+            pltpu.make_async_copy(wt_ref.at[:, at], wt_hbm.at[:, at], wt_out_sem.at[index]),
+        )
+
+    def turn_and_store(row0):
+        turn(row0)
+        for copy in store(row0):
+            copy.start()
+
+    chip_rows = 2 * rows
+    chip_tiles = chip_rows // tall
+    per_tile = tall // piece
+
+    def relay(i, carry):
+        k = which(i)
+        for slot in far:
+            to_chip(slot, k).wait_recv()
+            if shared:
+                to_buddy(slot, k).start()
+        return carry
+
+    def wait_core(k, carry):
+        to_core(k).wait_recv()
+        return carry
+
+    if shared:
+        for slot in in_slots:
+            if slot > 1:
+                in_copy(slot).wait_recv()
+                in_buddy(slot).start()
+    relay(0, 0)
+    lax.fori_loop(0, pieces, wait_core, 0)
+
+    def own_tile(j, carry):
+        turn_and_store(chip * chip_rows + j * tall)
+
+        @pl.when(j + 1 < mine)
+        def _():
+            relay(j + 1, 0)
+
+        return carry
+
+    lax.fori_loop(0, chip_tiles, own_tile, 0)
+    if mine > chip_tiles + 1:
+        lax.fori_loop(chip_tiles + 1, mine, relay, 0)
+
+    def far_tile(j, carry):
+        for slot in far:
+            turn_and_store(owner_of(slot) * rows + part * mine * piece + j * tall)
+        return carry
+
+    lax.fori_loop(0, mine // per_tile, far_tile, 0)
+
+    if shared:
+
+        def far_tile_late(j, carry):
+            for slot in far:
+                for p in range(per_tile):
+                    k = (1 - part) * mine + j * per_tile + p
+                    to_buddy(slot, k).wait_recv()
+                turn_and_store(owner_of(slot) * rows + (1 - part) * mine * piece + j * tall)
+            return carry
+
+        lax.fori_loop(0, mine // per_tile, far_tile_late, 0)
+        for slot in in_slots:
+            if slot > 1:
+                in_buddy(slot).wait_recv()
+    else:
+        for slot in in_slots:
+            if slot > 1:
+                in_copy(slot).wait_recv()
+    if blocks == 2:
+        in_copy(1).wait_recv()
+    tail = pltpu.make_async_copy(
+        w_ref.at[pl.ds(hidden, deep)], w_hbm.at[pl.ds(hidden, deep)], load_sem.at[0]
+    )
+    tail.start()
+
+    for copy in segment_copies:
+        copy.wait()
+    for slot in in_slots:
+        if slot > 0:
+            in_copy(slot).wait_send()
+        if slot > 1 and shared:
+            in_buddy(slot).wait_send()
+
+    def settle(i, carry):
+        k = which(i)
+        to_core(k).wait_send()
+
+        @pl.when(i < mine)
+        def _():
+            for slot in far:
+                to_chip(slot, k).wait_send()
+                if shared:
+                    to_buddy(slot, k).wait_send()
+
+        return carry
+
+    lax.fori_loop(0, pieces, settle, 0)
+
+    def stored(j, carry):
+        for copy in store(j * tall):
+            copy.wait()
+        return carry
+
+    lax.fori_loop(0, hidden // tall, stored, 0)
+    tail.wait()
+
+
+def run_gather(chips, depth, w_rec, in_bias, h_init, c_init, word_grad, ids):
+    rows, columns = w_rec.shape
+    wide = columns // 2
+    units = wide // 4
+    hidden = 2 * units
+    deep = in_bias.shape[0]
+    peers = 2 * chips
+    shared = depth % 2 == 0
+    piece = 32
+    pieces = rows // piece
+    seg = h_init.shape[0]
+    vmem = pl.BlockSpec(memory_space=pltpu.VMEM)
+    anywhere = pl.BlockSpec(memory_space=pl.ANY)
+    bf16, f32 = jnp.bfloat16, jnp.float32
+    dma = pltpu.SemaphoreType.DMA
+    far = max(peers - 2, 1)
+    return pl.pallas_call(
+        functools.partial(gather_kernel, chips, shared),
+        in_specs=[anywhere] + [vmem] * 5,
+        out_specs=[anywhere, anywhere] + [vmem] * 4,
+        out_shape=[
+            jax.ShapeDtypeStruct((hidden + deep, wide), bf16),
+            jax.ShapeDtypeStruct((wide, hidden), bf16),
+            jax.ShapeDtypeStruct((2 * seg, hidden), f32),
+            jax.ShapeDtypeStruct((2 * seg, units), f32),
+            jax.ShapeDtypeStruct((2 * word_grad.shape[0], units), bf16),
+            jax.ShapeDtypeStruct((2 * seg, ids.shape[1]), jnp.int32),
+        ],
+        scratch_shapes=[
+            pltpu.VMEM((hidden + deep, wide), bf16),
+            pltpu.VMEM((wide, hidden), bf16),
+            pltpu.VMEM((rows, wide), bf16),
+            pltpu.VMEM((2, piece, columns), f32),
+            dma((2,)),
+            dma((pieces,)),
+            dma((pieces,)),
+            dma((far, pieces)),
+            dma((far, pieces)),
+            dma((far, pieces)),
+            dma((far, pieces)),
+            dma((peers - 1,)),
+            dma((peers - 1,)),
+            dma((peers - 1,)),
+            dma((peers - 1,)),
+            dma((4,)),
+            dma((4,)),
+            dma((hidden // 128,)),
+            dma((hidden // 128,)),
+        ],
+        compiler_params=pltpu.CompilerParams(
+            collective_id=4, has_side_effects=True, vmem_limit_bytes=58 << 20
+        ),
+        cost_estimate=pl.CostEstimate(flops=0, bytes_accessed=400 << 20, transcendentals=0),
+    )(w_rec, in_bias, h_init, c_init, word_grad, ids)
 
 
 def forward_kernel(
@@ -87,8 +489,8 @@
         copy.start()
         greet([peer])
         for u in range(chunks):
-            hown[0, u] = h0_ref[:, pl.ds(pl.multiple_of(own0 + u * CHUNK, CHUNK), CHUNK)]
-            hpar[0, u] = h0_ref[:, pl.ds(pl.multiple_of(par0 + u * CHUNK, CHUNK), CHUNK)]
+            hown[0, u] = h0_ref[:, pl.ds(pl.multiple_of(own0 + u * CHUNK, CHUNK), CHUNK)].astype(jnp.bfloat16)
+            hpar[0, u] = h0_ref[:, pl.ds(pl.multiple_of(par0 + u * CHUNK, CHUNK), CHUNK)].astype(jnp.bfloat16)
         cell[...] = c0_ref[...]
         copy.wait()
 
@@ -953,53 +1355,38 @@
     core = lax.rem(lax.axis_index("group"), 2)
     first = core == 0
 
-    def pair(own):
-        other = partner(own, "group", 0)
-        return jnp.where(first, jnp.concatenate([own, other]), jnp.concatenate([other, own]))
-
-    def half(value, axis, index):
-        return lax.dynamic_slice_in_dim(value, index * units, units, axis)
-
-    def own_columns(value):
-        return jnp.concatenate(
-            [half(value[:, q * hidden_size : (q + 1) * hidden_size], 1, core) for q in range(4)],
-            axis=1,
-        )
-
-    in_full, rec_full, bias_full, dec_full = (
-        lax.all_gather(w_in[0].astype(jnp.bfloat16), "group", axis=1, tiled=True),
-        lax.all_gather(w_rec[0].astype(jnp.bfloat16), "group", axis=0, tiled=True),
-        lax.all_gather(b_rec[0].astype(jnp.bfloat16), "group", axis=0, tiled=True),
-        lax.all_gather(w_dec[0].astype(jnp.bfloat16), "group", axis=0, tiled=True),
-    )
-    packed = pair(jnp.concatenate([chars[0], targets[0], resets[0], word_pos[0]], axis=1))
+    depth = 128
+    dec_full = lax.all_gather(w_dec[0].astype(jnp.bfloat16), "group", axis=0, tiled=True)
+    in_bias = jnp.concatenate(
+        [w_in[0], b_rec, jnp.zeros((depth - embed_size - 1, w_in.shape[2]), jnp.float32)]
+    ).astype(jnp.bfloat16)
+    word_slots = word_pos.shape[2]
+    spare = -(3 * seg_len + word_slots) % 128
+    ids = jnp.concatenate(
+        [
+            chars[0],
+            targets[0],
+            resets[0],
+            word_pos[0],
+            jnp.zeros((batch_size, spare), jnp.int32),
+        ],
+        axis=1,
+    )
+    weights, weights_t, h_pair, c_pair, wg_pair, packed = run_gather(
+        lax.axis_size("group") // 2,
+        lax.axis_size("dp"),
+        w_rec[0],
+        in_bias,
+        h_init[0],
+        c_init[0],
+        word_grad.reshape(batch_size * word_slots, hidden_size),
+        ids,
+    )
+    wg_pair = wg_pair.reshape(2 * batch_size, word_slots, units)
     chars2 = packed[:, :seg_len]
     targets2 = packed[:, seg_len : 2 * seg_len]
     resets2 = packed[:, 2 * seg_len : 3 * seg_len]
-    word_pos2 = packed[:, 3 * seg_len :]
-    h_pair = pair(h_init[0].astype(jnp.bfloat16))
-    c_mine = half(c_init[0], 1, core)
-    c_other = partner(half(c_init[0], 1, 1 - core), "group", 0)
-    wg_mine = half(word_grad, 2, core)
-    wg_other = partner(half(word_grad, 2, 1 - core), "group", 0)
-
-    def ordered(mine, other):
-        return jnp.where(first, jnp.concatenate([mine, other]), jnp.concatenate([other, mine]))
-
-    c_pair = ordered(c_mine, c_other)
-    wg_pair = ordered(wg_mine, wg_other)
-    in_own = own_columns(in_full)
-    rec_own = own_columns(rec_full)
-    bias_own = own_columns(bias_full[None])
-    depth = 128
-    weights = jnp.concatenate(
-        [
-            rec_own,
-            in_own,
-            bias_own,
-            jnp.zeros((depth - embed_size - 1, 4 * units), jnp.bfloat16),
-        ]
-    )
+    word_pos2 = packed[:, 3 * seg_len : 3 * seg_len + word_slots]
     char_major = jnp.transpose(chars2)
     char_onehot = (char_major[:, :, None] == jnp.arange(vocab_size, dtype=jnp.int32)).astype(
         jnp.bfloat16
@@ -1067,7 +1454,7 @@
         jnp.concatenate([partner_half, own_slots], axis=-1),
     )
     pre_all, gh_pair, gc_pair = run_backward(
-        from_output + from_words, gate_all, cell_all, cellkept_all, keep_major, rec_own.T
+        from_output + from_words, gate_all, cell_all, cellkept_all, keep_major, weights_t
     )
 
     def own_rows(value):

time: 973 us -> 785 us (0.81)
  waiting for transfers between devices: 222 us -> 37.4 us
  Pallas kernels: 527 us -> 647 us
  local copies, waits for them, and re-layouts: 129 us -> 31.1 us
  other arithmetic: 33.4 us -> 19.4 us
    all_gather x2 -> x0, waiting for transfers between devices: 189 us -> none  [the longest x1 189 us: shards(): lax.all_gather(w_rec[0].astype(jnp.bfloat16), 'group', axis=0, tiled=True)]
    pallas_call x0 -> x1, Pallas kernels: none -> 121 us  [run_gather(): pl.pallas_call(functools.partial(gather_kernel, chips, shared), in_specs=...]
    concatenate x4 -> x2, local copies, waits for them, and re-layouts: 50.7 us -> 0.76 us  [the longest x1 0.68 us: shards(): jnp.concatenate([chars[0], targets[0], resets[0], word_pos[0], jnp.zeros(...]
    slice x4 -> x2, local copies, waits for them, and re-layouts: 23.1 us -> 2.38 us  [the longest x1 2.31 us: shards(): weights[hidden_size:]]
    transpose x1 -> x0, other arithmetic: 16 us -> none  [shards(): pre_all, gh_pair, gc_pair = run_backward(from_output + from_words, gate_a...]
    unnamed x59 -> x43, local copies, waits for them, and re-layouts: 25.4 us -> 10.8 us
    dynamic_slice x8 -> x0, local copies, waits for them, and re-layouts: 13.6 us -> none  [half(): return lax.dynamic_slice_in_dim(value, index * units, units, axis)]
  transfers between devices with their start and end apart: 12 -> 6, of which waited for: 3 -> 2; matrix products, arithmetic and copies ran while one was open for 16% -> 5% of each run, Pallas kernels for 23% -> 44%
where the time goes in v3:
time: 785 us; the launch traced here: 779 us
  Pallas kernels  647 us (82%)
  waiting for transfers between devices  37.4 us (5%)
  local copies, waits for them, and re-layouts  31.1 us (4%)
  matrix products  24.9 us (3%)
  other arithmetic  19.4 us (2%)
  between operations  16.8 us (2%)
    pallas_call x1, Pallas kernels, run_reduce(): pl.pallas_call(functools.partial(reduce_kernel, chips, depth, embed), in_...  287 us
    pallas_call x1, Pallas kernels, run_gather(): pl.pallas_call(functools.partial(gather_kernel, chips, shared), in_specs=...  121 us
    pallas_call x1, Pallas kernels, run_backward(): pl.pallas_call(functools.partial(backward_kernel, steps), grid=(steps,),...  113 us
    pallas_call x1, Pallas kernels, run_forward(): pl.pallas_call(functools.partial(forward_kernel, steps), grid=(steps + 1,...  106 us
    psum x1, waiting for transfers between devices, shards(): dec_sum = lax.psum(dec_sum, 'dp').astype(jnp.float32)  34.6 us
    pallas_call x1, Pallas kernels, run_momentum(): pl.pallas_call(momentum_kernel, grid=(4, 2), in_specs=[pl.BlockSpec(memor...  20 us
  transfers between devices with their start and end apart: 6, of which 2 were waited for; matrix products, arithmetic and copies ran while one was open for 5% of the time, Pallas kernels for 44%

profile of v3, /device:TPU:0, one launch (start us, length us, event | category | flops | bytes accessed | tf_op | source)
XLA Modules:
  0.0 778.9 jit_solution(14048724079948213115)
XLA Ops:
  7.3 1.9 copy.99
  13.7 120.6 %shard_map.306 = (bf16[2176,4096]{1,0:T(8,128)(2,1)}, bf16[4096,2048]{1,0:T(8,128)(2,1)}, f32[48,2048]{1,0:T(8,128)}, f32[48,1024]{1,0:T(8,128)}, bf16[384,1024]{1,0:T(8,128)(2,1)}, /*index=5*/s32[48,128]{1,0:T(8,128)}) custom-call(f32[512,8192]{1,0:T(8,128)} %bitcast.77, bf16[128,2048]{1,0:T(8,128)(2,1)} %maximum_maximum_fusion.inb_ref, ...), custom_call_target="tpu_custom_call" | custom-call | bytes 419430400 | tf_op jit(solution)/shard_map/pallas_call | solution.py:403
  137.8 106.2 %shard_map.307 = (bf16[25,48,2048]{2,1,0:T(8,128)(2,1)}, bf16[24,48,2048]{2,1,0:T(8,128)(2,1)}, f32[24,4,48,1024]{3,2,1,0:T(8,128)}, f32[24,48,1024]{2,1,0:T(8,128)}, f32[24,48,1024]{2,1,0:T(8,128)}) custom-call(bf16[24,48,128]{2,1,0:T(8,128)(2,1)} %maximum_maximum_fusion.1.emb_ref, f32[24,48,128]{2,1,0:T(8,128)} %broadcast_in_dim.32.keep_ref, ...), custom_call_target="tpu_custom_call" | custom-call | flops 20535312384 | bytes 524288000 | tf_op jit(solution)/shard_map/pallas_call | solution.py:572
  244.0 5.2 slice.54
  249.3 1.8 constant_dynamic-slice_fusion.4
  251.1 3.1 convolution_convert_fusion
  254.6 1.6 collective-permute-start
  256.9 2.3 slice.57.in_ref
  259.3 4.0 fusion.17
  263.3 2.7 collective-permute-done
  266.0 1.5 maximum_select_fusion
  267.6 5.4 fusion.6
  273.0 2.6 select_reduce_fusion
  275.6 3.9 fusion.2
  279.8 8.0 %bitcast_add_fusion.outg_ref = f32[24,48,1024]{2,1,0:T(8,128)} fusion(f32[48,1024,24]{1,2,0:T(8,128)} %fusion.17, bf16[24,48,275]{2,1,0:T(8,128)(2,1)S(1)} %get-tuple-element.103, bf16[1,2048,275]{1,2,0:T(8,128)(2,1)S(1)} %copy-done.8, s32[]{:T(128)S(6)} %select_n.53), kind=kOutput, calls=%fused_computation.2 | convolution fusion | flops 649986048 | bytes 10895364 | tf_op jit(solution)/shard_map/tbv,hv->tbh/dot_general | solution.py:1426
  287.7 113.2 %shard_map.308 = (bf16[24,48,4096]{2,1,0:T(8,128)(2,1)}, f32[48,1024]{1,0:T(8,128)}, f32[48,1024]{1,0:T(8,128)}) custom-call(f32[24,48,1024]{2,1,0:T(8,128)} %bitcast_add_fusion.outg_ref, f32[24,4,48,1024]{3,2,1,0:T(8,128)} %get-tuple-element.55.gates_ref, f32[24,48,1024]{2,1,0:T(8,128)} %get-tuple-element.56.cell_ref, ...), custom_call_target="tpu_custom_call" | custom-call | flops 19327352832 | bytes 524288000 | tf_op jit(solution)/shard_map/pallas_call | solution.py:727
  406.1 34.6 %all-reduce.4.cloned.1.call-done = bf16[512,275]{0,1:T(8,128)(2,1)} async-done(((bf16[512,275]{0,1:T(8,128)(2,1)}), bf16[512,275]{0,1:T(8,128)(2,1)}) %all-reduce.4.cloned.1.call-update) | async-done | bytes 281616 | tf_op jit(solution)/shard_map/psum | solution.py:1478
  440.7 1.7 fusion.19
  443.7 286.8 %shard_map.309 = (bf16[2,512,4096]{2,1,0:T(8,128)(2,1)}, bf16[112,2048]{1,0:T(8,128)(2,1)}, f32[288,128]{1,0:T(8,128)}, f32[8,128]{1,0:T(8,128)}) custom-call(bf16[1152,2048]{1,0:T(8,128)(2,1)} %bitcast.91, bf16[1152,128]{1,0:T(8,128)(2,1)} %bitcast.80, bf16[1152,4096]{1,0:T(8,128)(2,1)} %bitcast.90, bf16[128,4096]{1,0:T(8,128)(2,1)} %slice.57.in_ref, ...), custom_call_target="tpu_custom_call" | custom-call | flops 19327352832 | bytes 734003200 | tf_op jit(solution)/shard_map/pallas_call | solution.py:1250
  737.0 2.0 multiply_add_fusion
  739.0 1.6 fusion.26
  746.9 1.7 copy.74
  748.6 1.7 copy.71
  751.0 20.0 %shard_map.310 = (f32[1,512,8192]{2,1,0:T(8,128)}, f32[1,512,8192]{2,1,0:T(8,128)}) custom-call(f32[8,128]{1,0:T(8,128)S(1)} %copy-done, bf16[2,512,4096]{2,1,0:T(8,128)(2,1)} %get-tuple-element.65.sum_ref, f32[1,512,8192]{2,1,0:T(8,128)} %moment_ref.1), custom_call_target="tpu_custom_call" | custom-call | tf_op jit(solution)/shard_map/pallas_call | solution.py:1314
  (89 shorter events, 27.9 us)
Async XLA Ops:
  7.2 4.7 copy-start.3
  7.2 5.9 copy-start.13
  7.2 5.9 copy-start.12
  7.2 5.8 copy-start.11
  7.2 260.4 %all-gather.3.cloned.1.call-start = ((), (), s32[]{:S(2)}) async-start(), calls=%async_computation.3 | async-start | bytes 1433600 | tf_op jit(solution)/shard_map/all_gather | solution.py:1359
  9.2 395.5 %reduce-scatter.2.cloned.1.call-start = ((), (), s32[]{:S(2)}) async-start(), calls=%async_computation.1 | async-start | bytes 1433600 | tf_op jit(solution)/shard_map/reduce_scatter | solution.py:1475
  251.1 5.1 copy-start.7
  254.2 5.1 copy-start.15
  254.2 5.1 copy-start.5
  254.6 11.4 %collective-permute-start = (bf16[24,4,2048]{2,1,0:T(4,128)(2,1)S(1)}, bf16[24,4,2048]{2,1,0:T(4,128)(2,1)S(1)}, u32[]{:S(2)}, u32[]{:S(2)}) collective-permute-start(bf16[24,4,2048]{2,1,0:T(4,128)(2,1)S(1)} %get-tuple-element.105), channel_id=1, source_target_pairs={{0,16},{16,0},{1,17},{17,1},{2,18},{18,2},{3,19},{19,3},{4,20},{20... | collective-permute-start | bytes 1179656 | tf_op jit(solution)/shard_map/ppermute | solution.py:17
  275.6 4.2 copy-start.8
  279.5 161.1 %all-reduce.4.cloned.1.call-start = ((), (), s32[]{:S(2)}) async-start(), calls=%async_computation.2 | async-start | bytes 573440 | tf_op jit(solution)/shard_map/psum | solution.py:1478
  401.9 2.8 collective-permute-start.2
  402.9 2.5 collective-permute-start.1
  404.6 39.0 %copy-start.9 = (f32[288,128]{1,0:T(8,128)}, f32[288,128]{1,0:T(8,128)S(1)}, u32[]{:S(2)}) copy-start(f32[288,128]{1,0:T(8,128)S(1)} %dynamic_update_slice.7.extra_ref) | copy-start | bytes 442372
  443.6 292.1 %copy-start.16 = (f32[1,275]{1,0:T(1,128)S(1)}, f32[1,275]{1,0:T(1,128)}, u32[]{:S(2)}) copy-start(f32[1,275]{1,0:T(1,128)} %param.39) | copy-start | bytes 3304
  443.6 293.4 %copy-start.14 = (f32[1,2048]{1,0:T(1,128)S(1)}, f32[1,2048]{1,0:T(1,128)}, u32[]{:S(2)}) copy-start(f32[1,2048]{1,0:T(1,128)} %param.37) | copy-start | bytes 24580
  443.6 295.4 %copy-start.10 = (f32[1,275,100]{2,0,1:T(1,128)S(1)}, f32[1,275,100]{2,0,1:T(1,128)}, u32[]{:S(2)}) copy-start(f32[1,275,100]{2,0,1:T(1,128)} %param.34) | copy-start | bytes 330004
  730.5 11.8 %copy-start.1 = (bf16[512,275]{0,1:T(8,128)(2,1)S(1)}, bf16[512,275]{0,1:T(8,128)(2,1)}, u32[]{:S(2)}) copy-start(bf16[512,275]{0,1:T(8,128)(2,1)} %all-reduce.4.cloned.1.call-done) | copy-start | bytes 844804
  730.5 11.8 %copy-start.6 = (f32[1,512,275]{1,0,2:T(1,128)S(1)}, f32[1,512,275]{1,0,2:T(1,128)}, u32[]{:S(2)}) copy-start(f32[1,512,275]{1,0,2:T(1,128)} %param.38) | copy-start | bytes 1689604
  743.0 2.9 copy-start.2
  743.0 2.9 copy-start.4
  746.8 4.1 copy-start
Sparse Core Ops, SparseCore 0:
  10.2 26.1 all-gather.2
  279.7 25.7 reduce-scatter.1
  404.8 35.8 all-reduce.3

commit v4 on v3

--- a/solution.py
+++ b/solution.py
@@ -580,14 +580,14 @@
             pl.BlockSpec(memory_space=pl.ANY),
         ],
         out_specs=[
-            pl.BlockSpec((1, rows, hidden), lambda t: (t, 0, 0)),
+            pl.BlockSpec((1, rows, hidden), lambda t: (jnp.maximum(t - 1, 0), 0, 0)),
             pl.BlockSpec((1, rows, hidden), lambda t: (at(t), 0, 0)),
             pl.BlockSpec((1, 4, rows, units), lambda t: (at(t), 0, 0, 0)),
             pl.BlockSpec((1, rows, units), lambda t: (at(t), 0, 0)),
             pl.BlockSpec((1, rows, units), lambda t: (at(t), 0, 0)),
         ],
         out_shape=[
-            jax.ShapeDtypeStruct((steps + 1, rows, hidden), jnp.bfloat16),
+            jax.ShapeDtypeStruct((steps, rows, hidden), jnp.bfloat16),
             jax.ShapeDtypeStruct((steps, rows, hidden), jnp.bfloat16),
             jax.ShapeDtypeStruct((steps, 4, rows, units), jnp.float32),
             jax.ShapeDtypeStruct((steps, rows, units), jnp.float32),
@@ -779,14 +779,14 @@
     emb_ref,
     clip_ref,
     turned,
+    fetched,
+    fetch_sem,
     inbox,
     outbox,
     partial,
     final,
     in_all,
     in_box,
-    in_mine,
-    in_part,
     in_final,
     in_swap,
     emb_box,
@@ -853,6 +853,7 @@
         step = (slot - 2) // 2 + 1
         return 2 + 2 * (chips - step - 1) + slot % 2
 
+    order = list(range(2, peers)) + [1, 0]
     barrier = pltpu.get_barrier_semaphore()
     for slot in range(1, peers):
         pl.semaphore_signal(barrier, inc=1, device_id=in_group(owner_of(slot)), device_id_type=MESH)
@@ -960,8 +961,8 @@
             "f1": final_send.at[1, unit],
         }
 
-    units = 2 * groups
-    in_sems, emb_sems = line_sems(units), line_sems(units + 1)
+    extra_rows = 4 // chips
+    emb_sems = line_sems(2 * (groups + extra_rows))
 
     def send_block(slot, parity, index, row):
         return remote(
@@ -986,9 +987,26 @@
 
         lax.fori_loop(0, wide // span, columns, 0)
 
-    def block(slot, b, parity):
-        start = owner_of(slot) * rows_out + b * tall
-        turned[...] = jnp.transpose(kept_ref[:, pl.ds(pl.multiple_of(start, tall), tall)])
+    def fetch(turn, b):
+        start = owner_of(order[turn]) * rows_out + b * tall
+        return pltpu.make_async_copy(
+            kept_ref.at[:, pl.ds(pl.multiple_of(start, tall), tall)],
+            fetched.at[turn % 2],
+            fetch_sem.at[turn % 2],
+        )
+
+    def block(turn, b, parity):
+        slot = order[turn]
+        if turn + 1 < peers:
+            fetch(turn + 1, b).start()
+        else:
+
+            @pl.when(b + 1 < batches)
+            def _():
+                fetch(0, b + 1).start()
+
+        fetch(turn, b).wait()
+        turned[...] = jnp.transpose(fetched[turn % 2])
         if slot == 0:
             product(inbox.at[0, pl.ds(b * lot, lot)])
         else:
@@ -1006,20 +1024,40 @@
             send_block(slot, parity, index, row).start()
 
     def take(row):
-        for slot in range(1, peers):
-            remote(
-                outbox.at[slot - 1, 0, 0],
-                inbox.at[slot, row],
-                y_send.at[slot - 1, 0, 0],
-                y_recv.at[slot - 1, row],
-                in_group(owner_of(slot)),
-            ).wait_recv()
+        @pl.when(row < groups)
+        def _():
+            for slot in range(1, peers):
+                remote(
+                    outbox.at[slot - 1, 0, 0],
+                    inbox.at[slot, row],
+                    y_send.at[slot - 1, 0, 0],
+                    y_recv.at[slot - 1, row],
+                    in_group(owner_of(slot)),
+                ).wait_recv()
+            if chips > 1:
+                for part in range(2):
+                    total = inbox[part, row].astype(jnp.float32)
+                    for slot in range(2 + part, peers, 2):
+                        total = total + inbox[slot, row].astype(jnp.float32)
+                    inbox[part, row] = total.astype(jnp.bfloat16)
+
+        @pl.when(row == groups)
+        def _():
+            for step in range(1, chips):
+                in_copy(step).wait_recv()
+
+        @pl.when(row >= groups)
+        def _():
+            for part in range(2):
+                for k in range(chips):
+                    first = (2 * (row - groups) + part) * chips + k
+                    at = pl.ds(pl.multiple_of(first * 16, 16), 16)
+                    total = in_all[at, in_columns(chip)].astype(jnp.float32)
+                    for step in range(1, chips):
+                        total = total + in_box[step - 1, at].astype(jnp.float32)
+                    inbox[part, row, :, pl.ds(k * in_wide, in_wide)] = total.astype(jnp.bfloat16)
+
         for part in range(2):
-            if chips > 1:
-                total = inbox[part, row].astype(jnp.float32)
-                for slot in range(2 + part, peers, 2):
-                    total = total + inbox[slot, row].astype(jnp.float32)
-                inbox[part, row] = total.astype(jnp.bfloat16)
             send_partial(
                 inbox.at[part, row],
                 partial.at[2 * row + part],
@@ -1038,10 +1076,22 @@
     def finish(row):
         for part in range(2):
             pass_final(final.at[2 * row + part], line_sems(2 * row + part))
-            write_out(row, part).start()
+
+            @pl.when(row < groups)
+            def _():
+                write_out(row, part).start()
+
             squares(final[2 * row + part].astype(jnp.float32))
 
-    in_rows, in_wide = in_mine.shape
+    def settle(row):
+        for part in range(2):
+            wait_line(inbox.at[part, row], final.at[2 * row + part], line_sems(2 * row + part))
+
+            @pl.when(row < groups)
+            def _():
+                write_out(row, part).wait()
+
+    in_wide = wide // chips
 
     def in_columns(index):
         return pl.ds(pl.multiple_of(index * in_wide, in_wide), in_wide)
@@ -1072,12 +1122,10 @@
             cols = pl.ds(pl.multiple_of(j * span, span), span)
             in_all[:, cols] = jnp.dot(
                 turned[...], pre_ref[:, cols], preferred_element_type=jnp.float32
-            )[:in_rows].astype(jnp.bfloat16)
+            ).astype(jnp.bfloat16)
             return carry
 
         lax.fori_loop(0, wide // span, columns, 0)
-        for step in range(1, chips):
-            in_copy(step).start()
         into = lax.dot_general(
             pre_ref[...], in_ref[...], (((1,), (1,)), ((), ())), preferred_element_type=jnp.float32
         ).astype(jnp.bfloat16)
@@ -1087,17 +1135,16 @@
         summed = jnp.dot(onehot, into, preferred_element_type=jnp.float32)
         lanes = lax.broadcasted_iota(jnp.int32, summed.shape, 1)
         emb_mine[...] = jnp.where(lanes < embed, summed, 0.0) + extra_ref[...]
+
+    def send_in():
+        for step in range(1, chips):
+            in_copy(step).start()
+
+    def send_emb():
         for slot in range(1, peers):
             emb_copy(slot, group).start()
 
-    def small_partials():
-        for step in range(1, chips):
-            in_copy(step).wait_recv()
-        total = in_all[:, in_columns(chip)].astype(jnp.float32)
-        for step in range(1, chips):
-            total = total + in_box[step - 1].astype(jnp.float32)
-        in_mine[...] = total.astype(jnp.bfloat16)
-        send_partial(in_mine, in_part, in_final, in_sems)
+    def take_emb():
         for slot in range(1, peers):
             emb_copy(slot, owner_of(slot)).wait_recv()
         for slot in range(1, peers):
@@ -1109,18 +1156,43 @@
         emb_mine[...] = total
         send_partial(emb_mine, emb_part, emb_final, emb_sems)
 
-    def small_finals():
-        pass_final(in_final, in_sems)
-        squares(in_final[...].astype(jnp.float32))
-        pass_final(emb_final, emb_sems)
-
-    order = list(range(2, peers)) + [1, 0]
     lead = (peers - 2) * per_pass
-    y_lag, hop_lag = 3, 4
+    y_lag, hop_lag, settle_lag = 3, 4, 6
     hops = jnp.where(low, middle - z, z - middle)
     most_hops = max(middle, depth - 1 - middle)
-    steps = groups + y_lag + hop_lag * most_hops + lead
-    rounds = max(-(-steps // lot), 3 + most_hops)
+    before = groups // 2
+    places = groups + extra_rows + 1
+    steps = places + y_lag + hop_lag * most_hops + settle_lag + lead
+    rounds = -(-steps // lot)
+
+    def row_at(place):
+        is_in = jnp.logical_and(place >= before, place < before + extra_rows)
+        return jnp.where(
+            is_in,
+            groups + place - before,
+            jnp.where(place < before, place, place - extra_rows - 1),
+        )
+
+    def visit(place, rows, emb):
+        is_emb = place == before + extra_rows
+        inside = jnp.logical_and(place >= 0, place < places)
+
+        @pl.when(jnp.logical_and(inside, jnp.logical_not(is_emb)))
+        def _():
+            rows(row_at(place))
+
+        @pl.when(is_emb)
+        def _():
+            emb()
+
+    def send_any(row):
+        @pl.when(row < groups)
+        def _():
+            send(row)
+
+        @pl.when(row == groups)
+        def _():
+            send_in()
 
     def round_of(b, carry):
         parity = lax.rem(b, 2)
@@ -1129,44 +1201,38 @@
         def _():
             small_products()
 
-        for turn, slot in enumerate(order):
+        for turn in range(peers):
 
             @pl.when(b < batches)
             def _():
-                block(slot, b, parity)
+                block(turn, b, parity)
 
             def step(j, inner):
-                row = b * lot + turn * per_pass + j - lead
-                arrived = row - y_lag
+                sent = b * lot + turn * per_pass + j - lead
+                arrived = sent - y_lag
                 summed = arrived - hop_lag * hops
-
-                @pl.when(jnp.logical_and(row >= 0, row < groups))
-                def _():
-                    send(row)
-
-                @pl.when(jnp.logical_and(arrived >= 0, arrived < groups))
-                def _():
-                    take(arrived)
-
-                @pl.when(jnp.logical_and(summed >= 0, summed < groups))
-                def _():
-                    finish(summed)
-
+                visit(sent, send_any, send_emb)
+                visit(arrived, take, take_emb)
+                visit(summed, finish, lambda: pass_final(emb_final, emb_sems))
+                visit(
+                    summed - settle_lag,
+                    settle,
+                    lambda: wait_line(emb_mine, emb_final, emb_sems),
+                )
                 return inner
 
             lax.fori_loop(0, per_pass, step, 0)
 
-        @pl.when(b == 2)
-        def _():
-            small_partials()
-
-        @pl.when(b == 2 + hops)
-        def _():
-            small_finals()
-
         return carry
 
+    fetch(0, 0).start()
     lax.fori_loop(0, rounds, round_of, 0)
+    for u in range(2 * extra_rows):
+        for k in range(chips):
+            first = (u * chips + k) * 16
+            in_final[first : first + 16] = final[
+                2 * groups + u, :, k * in_wide : (k + 1) * in_wide
+            ]
 
     keep_cols = in_wide // 2
     if in_wide > wide // 4:
@@ -1213,22 +1279,10 @@
 
     for step in range(1, chips):
         in_copy(step).wait_send()
-    wait_line(in_mine, in_final, in_sems)
-    wait_line(emb_mine, emb_final, emb_sems)
     for slot in range(1, peers):
         for parity in range(min(2, batches)):
             for index in range(lot):
                 send_block(slot, parity, index, 0).wait_send()
-
-    def settle(row, carry):
-        for part in range(2):
-            wait_line(
-                inbox.at[part, row], final.at[2 * row + part], line_sems(2 * row + part)
-            )
-            write_out(row, part).wait()
-        return carry
-
-    lax.fori_loop(0, groups, settle, 0)
 
 
 def run_reduce(chips, depth, embed, kept, aug, pre, in_own, chars, extra, dec_sq):
@@ -1239,8 +1293,9 @@
     tall = 128
     lot = tall // 16
     groups = rows_out // 16
-    units = 2 * groups
-    in_rows = -(-(embed + 1) // 16) * 16
+    extra_rows = 4 // chips
+    units = 2 * (groups + extra_rows)
+    in_rows = aug.shape[1]
     in_wide = wide // chips
     in_cols = 2 * wide // peers
     vmem = pl.BlockSpec(memory_space=pltpu.VMEM)
@@ -1249,7 +1304,7 @@
     dma = pltpu.SemaphoreType.DMA
     return pl.pallas_call(
         functools.partial(reduce_kernel, chips, depth, embed),
-        in_specs=[vmem] * 7,
+        in_specs=[pl.BlockSpec(memory_space=pl.ANY)] + [vmem] * 6,
         out_specs=[pl.BlockSpec(memory_space=pl.ANY), vmem, vmem, vmem],
         out_shape=[
             jax.ShapeDtypeStruct((2, rows_out, wide), bf16),
@@ -1259,14 +1314,14 @@
         ],
         scratch_shapes=[
             pltpu.VMEM((tall, count), bf16),
-            pltpu.VMEM((peers, groups, 16, wide), bf16),
+            pltpu.VMEM((2, count, tall), bf16),
+            dma((2,)),
+            pltpu.VMEM((peers, groups + extra_rows, 16, wide), bf16),
             pltpu.VMEM((peers - 1, 2, lot, 16, wide), bf16),
             pltpu.VMEM((units, 16, wide), bf16),
             pltpu.VMEM((units, 16, wide), bf16),
             pltpu.VMEM((in_rows, wide), bf16),
             pltpu.VMEM((max(chips - 1, 1), in_rows, in_wide), bf16),
-            pltpu.VMEM((in_rows, in_wide), bf16),
-            pltpu.VMEM((in_rows, in_wide), bf16),
             pltpu.VMEM((in_rows, in_wide), bf16),
             pltpu.VMEM((in_rows, in_wide // 2), bf16),
             pltpu.VMEM((peers,) + small, f32),
@@ -1277,10 +1332,10 @@
             pltpu.VMEM((peers, 16, 128), f32),
             dma((peers - 1, 2, lot)),
             dma((peers - 1, groups)),
-            dma((units + 2,)),
-            dma((units + 2,)),
-            dma((units + 2,)),
-            dma((2, units + 2)),
+            dma((units + 1,)),
+            dma((units + 1,)),
+            dma((units + 1,)),
+            dma((2, units + 1)),
             dma((units,)),
             dma((max(chips - 1, 1),)),
             dma((max(chips - 1, 1),)),
@@ -1300,29 +1355,203 @@
     )(kept, aug, pre, in_own, chars, extra, dec_sq)
 
 
-def momentum_kernel(clip_ref, sum_ref, moment_ref, grad_ref, next_ref):
+def middle_kernel(
+    vocab,
+    seg_len,
+    out_ref,
+    target_ref,
+    dec_ref,
+    bias_ref,
+    slot_row_ref,
+    slot_col_ref,
+    wg_ref,
+    outg_ref,
+    decg_ref,
+    stat_ref,
+    picked_ref,
+    dec_acc,
+    pick_acc,
+):
+    i = pl.program_id(0)
+    last = pl.num_programs(0) - 1
+    core = lax.rem(lax.axis_index("group"), 2)
+    span, pair, hidden = out_ref.shape
+    count = span * pair
+    units = hidden // 2
+    seg = pair // 2
+    slots = wg_ref.shape[0] // pair
+    wide = dec_ref.shape[1]
+    bf16, f32, i32 = jnp.bfloat16, jnp.float32, jnp.int32
+    out = out_ref[...].reshape(count, hidden)
+
+    @pl.when(i == 0)
+    def _():
+        dec_acc[...] = jnp.zeros_like(dec_acc)
+        pick_acc[...] = jnp.zeros_like(pick_acc)
+        stat_ref[...] = jnp.zeros_like(stat_ref)
+
+    logits = jnp.dot(out, dec_ref[...], preferred_element_type=f32) + bias_ref[...]
+    top = jnp.max(logits, axis=1, keepdims=True)
+    powers = jnp.exp(logits - top)
+    total = jnp.sum(powers, axis=1, keepdims=True)
+    lanes = lax.broadcasted_iota(i32, (count, wide), 1)
+    hit = lanes == target_ref[...]
+    rows = lax.broadcasted_iota(i32, (count, 1), 0)
+    segment = lax.rem(rows, pair)
+    mine = jnp.logical_and(segment >= core * seg, segment < (core + 1) * seg)
+    loss = top + jnp.log(total) - jnp.sum(jnp.where(hit, logits, 0.0), axis=1, keepdims=True)
+    loss = jnp.sum(jnp.where(mine, loss, 0.0))
+    grad = (powers / total - jnp.where(hit, 1.0, 0.0)) * (1.0 / seg_len)
+    grad_b = grad.astype(bf16)
+    own_b = jnp.where(mine, grad_b.astype(f32), 0.0)
+    stat_ref[0:1] += jnp.sum(own_b, axis=0, keepdims=True)
+    stat_ref[1:2] += jnp.full((1, wide), loss, f32)
+    dec_acc[...] += jnp.dot(
+        jnp.transpose(own_b.astype(bf16)), out, preferred_element_type=f32
+    )
+
+    step = rows // pair + i * span
+    slot_count = wg_ref.shape[0]
+    col = lax.broadcasted_iota(i32, (count, slot_count), 1)
+    at_word = jnp.logical_and(slot_row_ref[...] == step, col // slots == segment)
+    words = jnp.where(at_word, 1.0, 0.0).astype(bf16)
+    half = pl.ds(pl.multiple_of(core * units, units), units)
+    outg_ref[...] = lax.dot_general(
+        grad_b, dec_ref[half], (((1,), (1,)), ((), ())), preferred_element_type=f32
+    ) + jnp.dot(words, wg_ref[...], preferred_element_type=f32)
+
+    own_slots = seg * slots
+    across = lax.broadcasted_iota(i32, (own_slots, count), 1)
+    slot_segment = lax.broadcasted_iota(i32, (own_slots, 1), 0) // slots + core * seg
+    picks = jnp.logical_and(
+        slot_col_ref[...] == across // pair + i * span, lax.rem(across, pair) == slot_segment
+    )
+    pick_acc[...] += jnp.dot(
+        jnp.where(picks, 1.0, 0.0).astype(bf16), out, preferred_element_type=f32
+    )
+
+    @pl.when(i == last)
+    def _():
+        decg_ref[...] = dec_acc[: decg_ref.shape[0]].astype(bf16)
+        picked_ref[...] = pick_acc[...].astype(bf16)
+
+
+def run_middle(vocab, out_all, targets, decoder, bias, slot_row, slot_col, wg_pair):
+    steps, pair, hidden = out_all.shape
+    span = 4 if steps % 4 == 0 else 1
+    count = span * pair
+    units = hidden // 2
+    wide = decoder.shape[1]
+    vocab_rows = -(-vocab // 32) * 32
+    own_slots = slot_col.shape[0]
+    bf16, f32 = jnp.bfloat16, jnp.float32
+
+    def fixed(shape):
+        return pl.BlockSpec(shape, lambda i: (0,) * len(shape))
+
+    return pl.pallas_call(
+        functools.partial(middle_kernel, vocab, steps),
+        grid=(steps // span,),
+        in_specs=[
+            pl.BlockSpec((span, pair, hidden), lambda i: (i, 0, 0)),
+            pl.BlockSpec((count, 1), lambda i: (i, 0)),
+            fixed(decoder.shape),
+            fixed(bias.shape),
+            fixed(slot_row.shape),
+            fixed(slot_col.shape),
+            fixed(wg_pair.shape),
+        ],
+        out_specs=[
+            pl.BlockSpec((count, units), lambda i: (i, 0)),
+            fixed((vocab_rows, hidden)),
+            fixed((8, wide)),
+            fixed((own_slots, hidden)),
+        ],
+        out_shape=[
+            jax.ShapeDtypeStruct((steps * pair, units), f32),
+            jax.ShapeDtypeStruct((vocab_rows, hidden), bf16),
+            jax.ShapeDtypeStruct((8, wide), f32),
+            jax.ShapeDtypeStruct((own_slots, hidden), bf16),
+        ],
+        scratch_shapes=[
+            pltpu.VMEM((wide, hidden), f32),
+            pltpu.VMEM((own_slots, hidden), f32),
+        ],
+        compiler_params=pltpu.CompilerParams(vmem_limit_bytes=48 << 20),
+    )(out_all, targets, decoder, bias, slot_row, slot_col, wg_pair)
+
+
+def update_kernel(
+    count,
+    clip_ref,
+    sum_ref,
+    moment_ref,
+    in_ref,
+    emb_ref,
+    dec_ref,
+    mom_in_ref,
+    mom_bias_ref,
+    mom_dec_ref,
+    mom_emb_ref,
+    mom_dbias_ref,
+    grad_ref,
+    next_ref,
+    *small,
+):
+    clip = clip_ref[0, 0]
     gradient = sum_ref[0].astype(jnp.float32)
     grad_ref[0] = gradient
-    next_ref[0] = momentum_step(moment_ref[0], gradient, clip_ref[0, 0])
-
-
-def run_momentum(clip, sums, moment):
+    next_ref[0] = momentum_step(moment_ref[0], gradient, clip)
+
+    @pl.when(jnp.logical_and(pl.program_id(0) == 0, pl.program_id(1) == 0))
+    def _():
+        embed = mom_in_ref.shape[1]
+        vocab = mom_emb_ref.shape[1]
+        emb = emb_ref[...]
+        turned = jnp.transpose(emb)
+        dec = jnp.transpose(dec_ref[...].astype(jnp.float32))
+        small[0][...] = turned[embed + 1 : embed + 2, :128] / count
+        results = [
+            (in_ref[:embed].astype(jnp.float32), mom_in_ref[0]),
+            (in_ref[embed : embed + 1].astype(jnp.float32), mom_bias_ref[...]),
+            (dec[:, :vocab], mom_dec_ref[0]),
+            (emb[:vocab, :embed], mom_emb_ref[0]),
+            (turned[embed : embed + 1, :vocab], mom_dbias_ref[...]),
+        ]
+        for k, (value, moment) in enumerate(results):
+            shape = small[1 + 2 * k].shape
+            small[1 + 2 * k][...] = value.reshape(shape)
+            small[2 + 2 * k][...] = momentum_step(moment, value, clip).reshape(shape)
+
+
+def run_update(count, clip, sums, in_sum, emb_sum, dec_sum, moments):
+    mom_rec, mom_in, mom_bias, mom_dec, mom_emb, mom_dbias = moments
     halves, rows, wide = sums.shape
     span = wide // 4
     block = pl.BlockSpec((1, rows, span), lambda q, s: (0, 0, 2 * q + s))
-    shape = jax.ShapeDtypeStruct(moment.shape, jnp.float32)
+    f32 = jnp.float32
+
+    def fixed(shape):
+        return pl.BlockSpec(shape, lambda q, s: (0,) * len(shape))
+
+    rec_shape = jax.ShapeDtypeStruct(mom_rec.shape, f32)
+    small = [mom_in, mom_bias, mom_dec, mom_emb, mom_dbias]
+    shapes = [(1, 128)]
+    for moment in small:
+        shapes += [moment.shape, moment.shape]
     return pl.pallas_call(
-        momentum_kernel,
+        functools.partial(update_kernel, count),
         grid=(4, 2),
         in_specs=[
             pl.BlockSpec(memory_space=pltpu.SMEM),
             pl.BlockSpec((1, rows, span), lambda q, s: (s, 0, q)),
             block,
-        ],
-        out_specs=[block, block],
-        out_shape=[shape, shape],
-        compiler_params=pltpu.CompilerParams(vmem_limit_bytes=48 << 20),
-    )(clip, sums, moment)
+        ]
+        + [fixed(x.shape) for x in (in_sum, emb_sum, dec_sum, *small)],
+        out_specs=[block, block] + [fixed(shape) for shape in shapes],
+        out_shape=[rec_shape, rec_shape] + [jax.ShapeDtypeStruct(shape, f32) for shape in shapes],
+        compiler_params=pltpu.CompilerParams(vmem_limit_bytes=56 << 20),
+    )(clip, sums, mom_rec, in_sum, emb_sum, dec_sum, *small)
 
 
 def shards(
@@ -1356,6 +1585,8 @@
     first = core == 0
 
     depth = 128
+    vocab_lanes = -(-vocab_size // 128) * 128
+    vocab_rows = -(-vocab_size // 32) * 32
     dec_full = lax.all_gather(w_dec[0].astype(jnp.bfloat16), "group", axis=0, tiled=True)
     in_bias = jnp.concatenate(
         [w_in[0], b_rec, jnp.zeros((depth - embed_size - 1, w_in.shape[2]), jnp.float32)]
@@ -1382,7 +1613,6 @@
         word_grad.reshape(batch_size * word_slots, hidden_size),
         ids,
     )
-    wg_pair = wg_pair.reshape(2 * batch_size, word_slots, units)
     chars2 = packed[:, :seg_len]
     targets2 = packed[:, seg_len : 2 * seg_len]
     resets2 = packed[:, 2 * seg_len : 3 * seg_len]
@@ -1410,38 +1640,22 @@
         (1 - jnp.transpose(resets2)).astype(jnp.float32)[:, :, None],
         (seg_len, 2 * batch_size, 128),
     )
-    hidden_all, kept_all, gate_all, cell_all, cellkept_all = run_forward(
+    out_all, kept_all, gate_all, cell_all, cellkept_all = run_forward(
         embedded_one, keep_major, h_pair, c_pair, weights
     )
-    out_all = hidden_all[1:]
-    logits = (
-        jnp.einsum("tbh,hv->tbv", out_all, dec_full, preferred_element_type=jnp.float32) + b_dec[0]
-    )
-    log_probs = jax.nn.log_softmax(logits, axis=-1)
-    target_onehot = (
-        jnp.transpose(targets2)[:, :, None] == jnp.arange(vocab_size, dtype=jnp.int32)
-    ).astype(jnp.float32)
-    loss_part = -0.5 * jnp.sum(log_probs * target_onehot)
-    logit_grad = ((jnp.exp(log_probs) - target_onehot) / seg_len).astype(jnp.bfloat16)
-    from_output = jnp.einsum(
-        "tbv,hv->tbh",
-        logit_grad,
-        lax.dynamic_slice_in_dim(dec_full, core * units, units, 0),
-        preferred_element_type=jnp.float32,
-    )
-    pos_onehot2 = (word_pos2[:, :, None] == jnp.arange(seg_len, dtype=jnp.int32)).astype(
-        jnp.bfloat16
-    )
-    from_words = jnp.einsum(
-        "bkt,bkh->tbh", pos_onehot2, wg_pair, preferred_element_type=jnp.float32
-    )
-    out_own = lax.dynamic_slice_in_dim(out_all, core * batch_size, batch_size, 1)
-    pos_onehot = (word_pos[0][:, :, None] == jnp.arange(seg_len, dtype=jnp.int32)).astype(
-        jnp.bfloat16
-    )
-    picked = jnp.einsum(
-        "bkt,tbh->bkh", pos_onehot, out_own, preferred_element_type=jnp.float32
-    ).astype(jnp.bfloat16)
+    positions = seg_len * 2 * batch_size
+    out_grad, dec_grad, stats, picked = run_middle(
+        vocab_size,
+        out_all,
+        jnp.transpose(targets2).reshape(positions, 1),
+        jnp.pad(dec_full, ((0, 0), (0, vocab_lanes - vocab_size))),
+        jnp.pad(b_dec, ((0, 0), (0, vocab_lanes - vocab_size)), constant_values=-1e30),
+        word_pos2.reshape(1, 2 * batch_size * word_slots),
+        word_pos[0].reshape(batch_size * word_slots, 1),
+        wg_pair,
+    )
+    dec_sum = lax.psum(dec_grad, ("group", "dp"))
+    picked = picked.reshape(batch_size, word_slots, hidden_size)
     half_slots = picked.shape[1] // 2
     model_index = lax.axis_index("dir")
     own_slots = lax.dynamic_slice_in_dim(picked, model_index * half_slots, half_slots, 1)
@@ -1454,7 +1668,7 @@
         jnp.concatenate([partner_half, own_slots], axis=-1),
     )
     pre_all, gh_pair, gc_pair = run_backward(
-        from_output + from_words, gate_all, cell_all, cellkept_all, keep_major, weights_t
+        out_grad.reshape(seg_len, 2 * batch_size, units), gate_all, cell_all, cellkept_all, keep_major, weights_t
     )
 
     def own_rows(value):
@@ -1469,19 +1683,21 @@
 
     grad_hidden0 = own_rows(gh_pair)
     grad_cell0 = own_rows(gc_pair)
-    lg_own = lax.dynamic_slice_in_dim(logit_grad, core * batch_size, batch_size, 1)
-    dec_grad = jnp.einsum("tbh,tbv->hv", out_own, lg_own, preferred_element_type=jnp.float32)
-    dbias_grad = jnp.sum(lg_own, axis=(0, 1), dtype=jnp.float32)
-    dec_sum = lax.psum_scatter(
-        dec_grad.astype(jnp.bfloat16), "group", scatter_dimension=0, tiled=True
-    )
-    dec_sum = lax.psum(dec_sum, "dp").astype(jnp.float32)
-    vocab_rows = -(-vocab_size // 32) * 32
-    extra = jnp.zeros((vocab_rows, depth), jnp.float32)
-    extra = lax.dynamic_update_slice(extra, dbias_grad[:, None], (0, embed_size))
-    extra = lax.dynamic_update_slice(extra, loss_part.reshape(1, 1), (0, embed_size + 1))
-    dec_sq = jnp.zeros((16, 128), jnp.float32).at[0, 0].set(jnp.sum(dec_sum * dec_sum))
-    positions = seg_len * 2 * batch_size
+    rows_own = w_dec.shape[1]
+    dec_sum = lax.dynamic_slice_in_dim(
+        dec_sum, lax.axis_index("group") * rows_own, rows_own, 1
+    )
+    dec_wide = dec_sum.astype(jnp.float32)
+    extra = jnp.concatenate(
+        [
+            jnp.zeros((vocab_rows, embed_size), jnp.float32),
+            stats[0, :vocab_rows, None],
+            jnp.broadcast_to(stats[1, 0], (vocab_rows, 1)),
+            jnp.zeros((vocab_rows, depth - embed_size - 2), jnp.float32),
+        ],
+        axis=1,
+    )
+    dec_sq = jnp.broadcast_to(jnp.sum(dec_wide * dec_wide) * (1.0 / 2048.0), (16, 128))
     rec_sum, in_out, emb_out, clip = run_reduce(
         lax.axis_size("group") // 2,
         lax.axis_size("dp"),
@@ -1494,37 +1710,35 @@
         extra,
         dec_sq,
     )
-    rec_grad, mom_rec_next = run_momentum(clip, rec_sum, mom_rec)
-    clip_scale = clip[0, 0]
-    in_sum = in_out[:embed_size].astype(jnp.float32)
-    bias_sum = in_out[embed_size].astype(jnp.float32)
-    emb_sum = emb_out[:vocab_size, :embed_size]
-    dbias_sum = emb_out[:vocab_size, embed_size]
-    loss_sum = emb_out[0, embed_size + 1].reshape(1)
-    mom_in_next = momentum_step(mom_in[0], in_sum, clip_scale)
-    mom_bias_next = momentum_step(mom_bias[0], bias_sum, clip_scale)
-    mom_dec_next = momentum_step(mom_dec[0], dec_sum, clip_scale)
-    mom_emb_next = momentum_step(mom_emb[0], emb_sum, clip_scale)
-    mom_dbias_next = momentum_step(mom_dbias[0], dbias_sum, clip_scale)
     token_count = seg_len * batch_size * lax.axis_size("group") * lax.axis_size("dp")
-    losses = loss_sum / token_count
+    grad_rec, next_rec, losses, *small = run_update(
+        token_count,
+        clip,
+        rec_sum,
+        in_out,
+        emb_out,
+        dec_sum,
+        (mom_rec, mom_in, mom_bias, mom_dec, mom_emb, mom_dbias),
+    )
+    grad_in, next_in, grad_bias, next_bias, grad_dec, next_dec = small[:6]
+    grad_emb, next_emb, grad_dbias, next_dbias = small[6:]
     return (
-        losses,
+        losses[0, :1],
         word_vectors,
         grad_hidden0[None],
         grad_cell0[None],
-        emb_sum[None],
-        in_sum[None],
-        rec_grad,
-        bias_sum[None],
-        dec_sum[None],
-        dbias_sum[None],
-        mom_emb_next[None],
-        mom_in_next[None],
-        mom_rec_next,
-        mom_bias_next[None],
-        mom_dec_next[None],
-        mom_dbias_next[None],
+        grad_emb,
+        grad_in,
+        grad_rec,
+        grad_bias,
+        grad_dec,
+        grad_dbias,
+        next_emb,
+        next_in,
+        next_rec,
+        next_bias,
+        next_dec,
+        next_dbias,
     )
 
 

time: 785 us -> 713 us (0.908)
  waiting for transfers between devices: 37.4 us -> 7.77 us
  matrix products: 24.9 us -> 0.51 us
  other arithmetic: 19.4 us -> 9.54 us
    psum x1, waiting for transfers between devices: 34.6 us -> 0.01 us  [shards(): dec_sum = lax.psum(dec_grad, ('group', 'dp'))]
    pallas_call x1, Pallas kernels: 287 us -> 263 us  [run_reduce(): pl.pallas_call(functools.partial(reduce_kernel, chips, depth, embed), in_...]
    dot_general x4 -> x0, matrix products: 19 us -> none  [the longest x1 7.97 us: shards(): jnp.einsum('tbv,hv->tbh', logit_grad, lax.dynamic_slice_in_dim(dec_full,...]
    pallas_call x1 -> x2, Pallas kernels: 20 us -> 38.4 us  [the longest x1 22.5 us: run_update(): pl.pallas_call(functools.partial(update_kernel, count), grid=(4, 2), in_s...]
    slice x4 -> x1, local copies, waits for them, and re-layouts: 8.89 us -> 0.51 us  [shards(): stats[1, 0]]
    unnamed x43 -> x26, local copies, waits for them, and re-layouts: 10.8 us -> 18.6 us
  transfers between devices with their start and end apart: 6 -> 5, of which waited for: 2 -> 1; matrix products, arithmetic and copies ran while one was open for 5% -> 3% of each run, Pallas kernels for 44% -> 48%
where the time goes in v4:
time: 713 us; the launch traced here: 712 us
  Pallas kernels  644 us (90%)
  local copies, waits for them, and re-layouts  32.6 us (5%)
  between operations  14.9 us (2%)
  other arithmetic  9.54 us (1%)
  waiting for transfers between devices  7.77 us (1%)
    pallas_call x1, Pallas kernels, run_reduce(): pl.pallas_call(functools.partial(reduce_kernel, chips, depth, embed), in_...  263 us
    pallas_call x1, Pallas kernels, run_gather(): pl.pallas_call(functools.partial(gather_kernel, chips, shared), in_specs=...  123 us
    pallas_call x1, Pallas kernels, run_backward(): pl.pallas_call(functools.partial(backward_kernel, steps), grid=(steps,),...  113 us
    pallas_call x1, Pallas kernels, run_forward(): pl.pallas_call(functools.partial(forward_kernel, steps), grid=(steps + 1,...  106 us
    pallas_call x1, Pallas kernels, run_update(): pl.pallas_call(functools.partial(update_kernel, count), grid=(4, 2), in_s...  22.5 us
    unnamed x26, local copies, waits for them, and re-layouts  18.6 us
    pallas_call x1, Pallas kernels, run_middle(): pl.pallas_call(functools.partial(middle_kernel, vocab, steps), grid=(step...  15.9 us
  transfers between devices with their start and end apart: 5, of which 1 were waited for; matrix products, arithmetic and copies ran while one was open for 3% of the time, Pallas kernels for 48%

profile of v4, /device:TPU:0, one launch (start us, length us, event | category | flops | bytes accessed | tf_op | source)
XLA Modules:
  0.0 711.5 jit_solution(2040794740976044187)
XLA Ops:
  7.2 1.1 copy.102
  10.9 1.4 copy.103
  13.3 1.4 concatenate.68.ids_ref
  14.7 123.0 %shard_map.306 = (bf16[2176,4096]{1,0:T(8,128)(2,1)}, bf16[4096,2048]{1,0:T(8,128)(2,1)}, f32[48,2048]{1,0:T(8,128)}, f32[48,1024]{1,0:T(8,128)}, bf16[384,1024]{1,0:T(8,128)(2,1)}, /*index=5*/s32[48,128]{1,0:T(8,128)}) custom-call(f32[512,8192]{1,0:T(8,128)} %bitcast.41, bf16[128,2048]{1,0:T(8,128)(2,1)} %maximum_maximum_fusion.inb_ref, ...), custom_call_target="tpu_custom_call" | custom-call | bytes 419430400 | tf_op jit(solution)/shard_map/pallas_call | solution.py:403
  140.4 1.3 copy.85.mom_dec_ref
  141.7 1.2 copy.84.mom_in_ref
  144.7 2.3 slice.28.in_ref
  147.8 1.0 broadcast_in_dim.38.keep_ref
  148.9 105.8 %shard_map.307 = (bf16[24,48,2048]{2,1,0:T(8,128)(2,1)}, bf16[24,48,2048]{2,1,0:T(8,128)(2,1)}, f32[24,4,48,1024]{3,2,1,0:T(8,128)}, f32[24,48,1024]{2,1,0:T(8,128)}, f32[24,48,1024]{2,1,0:T(8,128)}) custom-call(bf16[24,48,128]{2,1,0:T(8,128)(2,1)} %maximum_maximum_fusion.1.emb_ref, f32[24,48,128]{2,1,0:T(8,128)} %broadcast_in_dim.38.keep_ref, ...), custom_call_target="tpu_custom_call" | custom-call | flops 20535312384 | bytes 524288000 | tf_op jit(solution)/shard_map/pallas_call | solution.py:572
  254.8 1.6 pad.8.dec_ref
  256.3 15.9 %shard_map.308 = (f32[1152,1024]{1,0:T(8,128)}, bf16[288,2048]{1,0:T(8,128)(2,1)}, f32[8,384]{1,0:T(8,128)S(1)}, bf16[192,2048]{1,0:T(8,128)(2,1)S(1)}) custom-call(bf16[24,48,2048]{2,1,0:T(8,128)(2,1)} %get-tuple-element.56.out_ref, s32[1152,1]{1,0:T(8,128)S(1)} %reshape.185.target_ref, bf16[2048,384]{1,0:T(8,128)(2,1)S(1)} %pad.8.dec_ref, ...), custom_call_target="tpu_custom_call" | custom-call | tf_op jit(solution)/shard_map/pallas_call | solution.py:1452
  273.7 113.5 %shard_map.309 = (bf16[24,48,4096]{2,1,0:T(8,128)(2,1)}, f32[48,1024]{1,0:T(8,128)}, f32[48,1024]{1,0:T(8,128)}) custom-call(f32[24,48,1024]{2,1,0:T(8,128)} %bitcast.54, f32[24,4,48,1024]{3,2,1,0:T(8,128)} %get-tuple-element.59.gates_ref, f32[24,48,1024]{2,1,0:T(8,128)} %get-tuple-element.60.cell_ref, f32[24,48,1024]{2,1,0:T(8,128)} %get-tuple-element.61.ckept_ref, ...), custom_call_target="tpu_custom_call" | custom-call | flops 19327352832 | bytes 524288000 | tf_op jit(solution)/shard_map/pallas_call | solution.py:727
  390.1 1.5 collective-permute-start
  393.8 7.7 %collective-permute-done = bf16[24,4,2048]{2,1,0:T(4,128)(2,1)S(1)} collective-permute-done((bf16[24,4,2048]{2,1,0:T(4,128)(2,1)S(1)}, bf16[24,4,2048]{2,1,0:T(4,128)(2,1)S(1)}, u32[]{:S(2)}, u32[]{:S(2)}) %collective-permute-start) | collective-permute-done | bytes 393248 | tf_op jit(solution)/shard_map/ppermute | solution.py:17
  401.5 1.5 maximum_select_fusion
  403.1 2.3 multiply_reduce_fusion
  406.7 263.3 %shard_map.310 = (bf16[2,512,4096]{2,1,0:T(8,128)(2,1)}, bf16[128,2048]{1,0:T(8,128)(2,1)}, f32[288,128]{1,0:T(8,128)}, f32[8,128]{1,0:T(8,128)}) custom-call(bf16[1152,2048]{1,0:T(8,128)(2,1)} %bitcast.57, bf16[1152,128]{1,0:T(8,128)(2,1)} %bitcast.45, bf16[1152,4096]{1,0:T(8,128)(2,1)} %bitcast.56, bf16[128,4096]{1,0:T(8,128)(2,1)} %slice.28.in_ref, ...), custom_call_target="tpu_custom_call" | custom-call | flops 19327352832 | bytes 734003200 | tf_op jit(solution)/shard_map/pallas_call | solution.py:1305
  670.0 22.5 %shard_map.311 = (f32[1,512,8192]{2,1,0:T(8,128)}, f32[1,512,8192]{2,1,0:T(8,128)}, f32[1,128]{1,0:T(1,128)}, f32[1,100,2048]{2,1,0:T(8,128)}, f32[1,100,2048]{2...) custom-call(f32[8,128]{1,0:T(8,128)} %get-tuple-element.66.clip_ref,, ...), custom_call_target="tpu_custom_call" | custom-call | tf_op jit(solution)/shard_map/pallas_call | solution.py:1542
  692.5 1.8 copy.87
  694.3 1.7 copy.90
  696.0 2.0 copy.89
  698.0 2.0 copy.92
  700.1 2.9 copy.88
  703.0 1.7 copy.91
  (61 shorter events, 16.0 us)
Async XLA Ops:
  7.2 247.6 %all-gather.3.cloned.1.call-start = ((), (), s32[]{:S(2)}) async-start(), calls=%async_computation.1 | async-start | bytes 1966080 | tf_op jit(solution)/shard_map/all_gather | solution.py:1590
  9.3 393.8 %all-reduce.4.cloned.1.call-start = ((), (), s32[]{:S(2)}) async-start(), calls=%async_computation | async-start | bytes 2359296 | tf_op jit(solution)/shard_map/psum | solution.py:1657
  14.7 124.9 %copy-start.4 = (f32[1,275,100]{2,0,1:T(1,128)S(1)}, f32[1,275,100]{2,0,1:T(1,128)}, u32[]{:S(2)}) copy-start(f32[1,275,100]{2,0,1:T(1,128)} %param.26) | copy-start | bytes 330004
  14.7 125.0 %copy-start.5 = (f32[1,275,100]{2,0,1:T(1,128)S(1)}, f32[1,275,100]{2,0,1:T(1,128)}, u32[]{:S(2)}) copy-start(f32[1,275,100]{2,0,1:T(1,128)} %param.32) | copy-start | bytes 330004
  14.7 125.7 %copy-start.3 = (f32[1,512,275]{1,0,2:T(1,128)S(1)}, f32[1,512,275]{1,0,2:T(1,128)}, u32[]{:S(2)}) copy-start(f32[1,512,275]{1,0,2:T(1,128)} %param.36) | copy-start | bytes 1689604
  14.7 127.0 %copy-start.2 = (f32[1,100,2048]{2,0,1:T(1,128)S(1)}, f32[1,100,2048]{2,0,1:T(1,128)}, u32[]{:S(2)}) copy-start(f32[1,100,2048]{2,0,1:T(1,128)} %param.33) | copy-start | bytes 2457604
  137.7 9.3 %copy-start.6 = (f32[1,275]{1,0:T(1,128)S(1)}, f32[1,275]{1,0:T(1,128)}, u32[]{:S(2)}) copy-start(f32[1,275]{1,0:T(1,128)} %param.31) | copy-start | bytes 3304
  148.9 107.5 %copy-start = (bf16[384,1024]{1,0:T(8,128)(2,1)S(1)}, bf16[384,1024]{1,0:T(8,128)(2,1)}, u32[]{:S(2)}) copy-start(bf16[384,1024]{1,0:T(8,128)(2,1)} %get-tuple-element.57.wg_ref) | copy-start | bytes 2359300
  389.1 3.3 collective-permute-start.1
  389.5 3.6 collective-permute-start.2
  390.1 11.4 %collective-permute-start = (bf16[24,4,2048]{2,1,0:T(4,128)(2,1)S(1)}, bf16[24,4,2048]{2,1,0:T(4,128)(2,1)S(1)}, u32[]{:S(2)}, u32[]{:S(2)}) collective-permute-start(bf16[24,4,2048]{2,1,0:T(4,128)(2,1)S(1)} %get-tuple-element.137), channel_id=1, source_target_pairs={{0,16},{16,0},{1,17},{17,1},{2,18},{18,2},{3,19},{19,3},{4,20},{20... | collective-permute-start | bytes 1179656 | tf_op jit(solution)/shard_map/ppermute | solution.py:17
  692.5 10.5 %copy-start.1 = (f32[1,100,2048]{2,1,0:T(8,128)S(1)}, f32[1,100,2048]{2,1,0:T(8,128)}, u32[]{:S(2)}) copy-start(f32[1,100,2048]{2,1,0:T(8,128)} %get-tuple-element.129) | copy-start | bytes 2457604
Sparse Core Ops, SparseCore 0:
  10.1 30.7 all-gather.2
  273.6 94.4 all-reduce.3

commit v5 on v4

--- a/solution.py
+++ b/solution.py
@@ -53,6 +53,7 @@
     c_out,
     wg_out,
     ids_out,
+    in_out,
     w_ref,
     wt_ref,
     stage,
@@ -266,9 +267,11 @@
 
     def turn(row0):
         at = pl.ds(pl.multiple_of(row0, tall), tall)
-        for q in range(4):
-            local = pl.ds(q * units, units)
-            wt_ref[local, at] = jnp.transpose(w_ref[at, local])
+        for u in range(units // CHUNK):
+            for q in range(4):
+                local = pl.ds(q * units + u * CHUNK, CHUNK)
+                turned = pl.ds((4 * u + q) * CHUNK, CHUNK)
+                wt_ref[turned, at] = jnp.transpose(w_ref[at, local])
 
     def store(row0):
         at = pl.ds(pl.multiple_of(row0, tall), tall)
@@ -351,6 +354,7 @@
         w_ref.at[pl.ds(hidden, deep)], w_hbm.at[pl.ds(hidden, deep)], load_sem.at[0]
     )
     tail.start()
+    in_out[...] = w_ref[hidden:]
 
     for copy in segment_copies:
         copy.wait()
@@ -403,7 +407,7 @@
     return pl.pallas_call(
         functools.partial(gather_kernel, chips, shared),
         in_specs=[anywhere] + [vmem] * 5,
-        out_specs=[anywhere, anywhere] + [vmem] * 4,
+        out_specs=[anywhere, anywhere] + [vmem] * 5,
         out_shape=[
             jax.ShapeDtypeStruct((hidden + deep, wide), bf16),
             jax.ShapeDtypeStruct((wide, hidden), bf16),
@@ -411,6 +415,7 @@
             jax.ShapeDtypeStruct((2 * seg, units), f32),
             jax.ShapeDtypeStruct((2 * word_grad.shape[0], units), bf16),
             jax.ShapeDtypeStruct((2 * seg, ids.shape[1]), jnp.int32),
+            jax.ShapeDtypeStruct((deep, wide), bf16),
         ],
         scratch_shapes=[
             pltpu.VMEM((hidden + deep, wide), bf16),
@@ -636,6 +641,9 @@
     w_sem,
     send_sem,
     recv_sem,
+    swap_send,
+    swap_recv,
+    swapped,
 ):
     i = pl.program_id(0)
     slot = lax.rem(i, 2)
@@ -673,6 +681,7 @@
             dh[:, span] = dh[:, span] + inbox[1 - slot, u]
 
     keep = keep_ref[0][:, :1]
+    block = 4 * CHUNK
     for u in range(chunks):
         span = pl.ds(u * CHUNK, CHUNK)
         gate_in = gates_ref[0, 0, :, span]
@@ -690,15 +699,17 @@
         ]
         for q in range(4):
             grad = grads[q].astype(jnp.bfloat16)
-            pg[:, pl.ds(q * units + u * CHUNK, CHUNK)] = grad
+            pg[:, pl.ds(u * block + q * CHUNK, CHUNK)] = grad
             pre_ref[0, :, pl.ds(q * units + u * CHUNK, CHUNK)] = grad
         dc[:, span] = total_cell * gate_forget * keep
-    for u in range(chunks):
-        cols = pl.ds(pl.multiple_of(par0 + u * CHUNK, CHUNK), CHUNK)
-        outbox[slot, u] = (
-            jnp.dot(pg[...], w_ref[:, cols], preferred_element_type=jnp.float32) * keep
-        )
-        exchange(slot, u).start()
+        part = pl.ds(u * block, block)
+        for n in range(chunks):
+            cols = pl.ds(pl.multiple_of(par0 + n * CHUNK, CHUNK), CHUNK)
+            product = jnp.dot(pg[:, part], w_ref[part, cols], preferred_element_type=jnp.float32)
+            outbox[slot, n] = product if u == 0 else outbox[slot, n] + product
+    for n in range(chunks):
+        outbox[slot, n] = outbox[slot, n] * keep
+        exchange(slot, n).start()
     for u in range(chunks):
         cols = pl.ds(pl.multiple_of(own0 + u * CHUNK, CHUNK), CHUNK)
         dh[:, pl.ds(u * CHUNK, CHUNK)] = (
@@ -711,8 +722,27 @@
             exchange(slot, u).wait()
         for u in range(chunks):
             span = pl.ds(u * CHUNK, CHUNK)
-            gh_ref[:, span] = dh[:, span] + inbox[slot, u]
-        gc_ref[...] = dc[...]
+            dh[:, span] = dh[:, span] + inbox[slot, u]
+        seg = gh_ref.shape[0]
+        rows_own = pl.ds(pl.multiple_of(core * seg, 8), seg)
+        rows_par = pl.ds(pl.multiple_of((1 - core) * seg, 8), seg)
+        swaps = []
+        for k, (held, result) in enumerate(((dh, gh_ref), (dc, gc_ref))):
+            swaps.append(
+                pltpu.make_async_remote_copy(
+                    src_ref=held.at[rows_par],
+                    dst_ref=swapped.at[k],
+                    send_sem=swap_send.at[k],
+                    recv_sem=swap_recv.at[k],
+                    device_id=peer,
+                    device_id_type=MESH,
+                )
+            )
+            swaps[k].start()
+            result[:, pl.ds(own0, units)] = held[rows_own]
+        for k, result in enumerate((gh_ref, gc_ref)):
+            swaps[k].wait()
+            result[:, pl.ds(par0, units)] = swapped[k]
 
 
 def run_backward(out_grad, gates, cells, cells_kept, keep, weights_t):
@@ -738,8 +768,8 @@
         out_specs=[pl.BlockSpec((1, rows, 4 * units), back), whole, whole],
         out_shape=[
             jax.ShapeDtypeStruct((steps, rows, 4 * units), jnp.bfloat16),
-            jax.ShapeDtypeStruct((rows, units), jnp.float32),
-            jax.ShapeDtypeStruct((rows, units), jnp.float32),
+            jax.ShapeDtypeStruct((rows // 2, 2 * units), jnp.float32),
+            jax.ShapeDtypeStruct((rows // 2, 2 * units), jnp.float32),
         ],
         scratch_shapes=[
             pltpu.VMEM(weights_t.shape, jnp.bfloat16),
@@ -751,6 +781,9 @@
             pltpu.SemaphoreType.DMA,
             pltpu.SemaphoreType.DMA((2, chunks)),
             pltpu.SemaphoreType.DMA((2, chunks)),
+            pltpu.SemaphoreType.DMA((2,)),
+            pltpu.SemaphoreType.DMA((2,)),
+            pltpu.VMEM((2, rows // 2, units), jnp.float32),
         ],
         compiler_params=pltpu.CompilerParams(
             collective_id=2, has_side_effects=True, vmem_limit_bytes=56 << 20
@@ -773,7 +806,7 @@
     in_ref,
     chars_ref,
     extra_ref,
-    decsq_ref,
+    dec_ref,
     rec_hbm,
     inout_ref,
     emb_ref,
@@ -1157,7 +1190,7 @@
         send_partial(emb_mine, emb_part, emb_final, emb_sems)
 
     lead = (peers - 2) * per_pass
-    y_lag, hop_lag, settle_lag = 3, 4, 6
+    y_lag, hop_lag, settle_lag = 3, 2, 6
     hops = jnp.where(low, middle - z, z - middle)
     most_hops = max(middle, depth - 1 - middle)
     before = groups // 2
@@ -1249,7 +1282,7 @@
         inout_ref[...] = in_final[...]
     emb_ref[...] = emb_final[...]
 
-    ssq[...] = ssq[...] + decsq_ref[...]
+    squares(dec_ref[...].astype(jnp.float32))
     norm_box[group] = ssq[...]
 
     def norm_copy(slot, source):
@@ -1285,7 +1318,7 @@
                 send_block(slot, parity, index, 0).wait_send()
 
 
-def run_reduce(chips, depth, embed, kept, aug, pre, in_own, chars, extra, dec_sq):
+def run_reduce(chips, depth, embed, kept, aug, pre, in_own, chars, extra, dec_sum):
     hidden = kept.shape[1]
     count, wide = pre.shape
     peers = 2 * chips
@@ -1352,7 +1385,7 @@
         cost_estimate=pl.CostEstimate(
             flops=2 * count * hidden * wide, bytes_accessed=700 << 20, transcendentals=0
         ),
-    )(kept, aug, pre, in_own, chars, extra, dec_sq)
+    )(kept, aug, pre, in_own, chars, extra, dec_sum)
 
 
 def middle_kernel(
@@ -1603,7 +1636,7 @@
         ],
         axis=1,
     )
-    weights, weights_t, h_pair, c_pair, wg_pair, packed = run_gather(
+    weights, weights_t, h_pair, c_pair, wg_pair, packed, in_own = run_gather(
         lax.axis_size("group") // 2,
         lax.axis_size("dp"),
         w_rec[0],
@@ -1667,27 +1700,14 @@
         jnp.concatenate([own_slots, partner_half], axis=-1),
         jnp.concatenate([partner_half, own_slots], axis=-1),
     )
-    pre_all, gh_pair, gc_pair = run_backward(
+    pre_all, grad_hidden0, grad_cell0 = run_backward(
         out_grad.reshape(seg_len, 2 * batch_size, units), gate_all, cell_all, cellkept_all, keep_major, weights_t
     )
 
-    def own_rows(value):
-        mine = lax.dynamic_slice_in_dim(value, core * batch_size, batch_size, 0)
-        theirs = lax.dynamic_slice_in_dim(value, (1 - core) * batch_size, batch_size, 0)
-        other = partner(theirs, "group", 0)
-        return jnp.where(
-            first,
-            jnp.concatenate([mine, other], axis=1),
-            jnp.concatenate([other, mine], axis=1),
-        )
-
-    grad_hidden0 = own_rows(gh_pair)
-    grad_cell0 = own_rows(gc_pair)
     rows_own = w_dec.shape[1]
     dec_sum = lax.dynamic_slice_in_dim(
         dec_sum, lax.axis_index("group") * rows_own, rows_own, 1
     )
-    dec_wide = dec_sum.astype(jnp.float32)
     extra = jnp.concatenate(
         [
             jnp.zeros((vocab_rows, embed_size), jnp.float32),
@@ -1697,7 +1717,6 @@
         ],
         axis=1,
     )
-    dec_sq = jnp.broadcast_to(jnp.sum(dec_wide * dec_wide) * (1.0 / 2048.0), (16, 128))
     rec_sum, in_out, emb_out, clip = run_reduce(
         lax.axis_size("group") // 2,
         lax.axis_size("dp"),
@@ -1705,10 +1724,10 @@
         kept_all.reshape(positions, hidden_size),
         embedded_one.reshape(positions, depth),
         pre_all.reshape(positions, 4 * units),
-        weights[hidden_size:],
+        in_own,
         char_major.reshape(1, positions),
         extra,
-        dec_sq,
+        dec_sum,
     )
     token_count = seg_len * batch_size * lax.axis_size("group") * lax.axis_size("dp")
     grad_rec, next_rec, losses, *small = run_update(

time: 713 us -> 666 us (0.934)
  Pallas kernels: 644 us -> 614 us
  waiting for transfers between devices: 7.77 us -> 0.07 us
    pallas_call x1, Pallas kernels: 113 us -> 91.5 us  [run_backward(): pl.pallas_call(functools.partial(backward_kernel, steps), grid=(steps,),...]
    pallas_call x1, Pallas kernels: 263 us -> 255 us  [run_reduce(): pl.pallas_call(functools.partial(reduce_kernel, chips, depth, embed), in_...]
    ppermute x3 -> x1, waiting for transfers between devices: 7.72 us -> 0.01 us  [partner(): return lax.ppermute(value, axis, pairs)]
    unnamed x26 -> x36, local copies, waits for them, and re-layouts: 18.6 us -> 18.5 us
  transfers between devices with their start and end apart: 5 -> 3, of which waited for: 1 -> 0; matrix products, arithmetic and copies ran while one was open for 3% -> 3% of each run, Pallas kernels for 48% -> 48%
where the time goes in v5:
time: 666 us; the launch traced here: 665 us
  Pallas kernels  614 us (92%)
  local copies, waits for them, and re-layouts  29.4 us (4%)
  between operations  14.3 us (2%)
    pallas_call x1, Pallas kernels, run_reduce(): pl.pallas_call(functools.partial(reduce_kernel, chips, depth, embed), in_...  255 us
    pallas_call x1, Pallas kernels, run_gather(): pl.pallas_call(functools.partial(gather_kernel, chips, shared), in_specs=...  123 us
    pallas_call x1, Pallas kernels, run_forward(): pl.pallas_call(functools.partial(forward_kernel, steps), grid=(steps + 1,...  106 us
    pallas_call x1, Pallas kernels, run_backward(): pl.pallas_call(functools.partial(backward_kernel, steps), grid=(steps,),...  91.5 us
    pallas_call x1, Pallas kernels, run_update(): pl.pallas_call(functools.partial(update_kernel, count), grid=(4, 2), in_s...  22.5 us
    unnamed x36, local copies, waits for them, and re-layouts  18.5 us
    pallas_call x1, Pallas kernels, run_middle(): pl.pallas_call(functools.partial(middle_kernel, vocab, steps), grid=(step...  15.9 us
  transfers between devices with their start and end apart: 3, of which 0 were waited for; matrix products, arithmetic and copies ran while one was open for 3% of the time, Pallas kernels for 48%

profile of v5, /device:TPU:0, one launch (start us, length us, event | category | flops | bytes accessed | tf_op | source)
XLA Modules:
  0.0 665.4 jit_solution(17009526369279309211)
XLA Ops:
  7.2 1.1 copy.102
  8.3 0.9 copy.78
  9.3 1.4 copy.103
  12.2 0.9 maximum_maximum_fusion.inb_ref
  13.2 1.4 concatenate.20.ids_ref
  14.6 123.3 %shard_map.306 = (bf16[2176,4096]{1,0:T(8,128)(2,1)}, bf16[4096,2048]{1,0:T(8,128)(2,1)}, f32[48,2048]{1,0:T(8,128)}, f32[48,1024]{1,0:T(8,128)}, bf16[384,1024]...) custom-call(f32[512,8192]{1,0:T(8,128)} %bitcast.37, bf16[128,2048]{1,0:T(8,128)(2,1)} %maximum_maximum_fusion.inb_ref, ...), custom_call_target="tpu_custom_call" | custom-call | bytes 419430400 | tf_op jit(solution)/shard_map/pallas_call | solution.py:407
  137.9 0.9 slice_bitcast_fusion
  138.8 0.8 slice.24
  141.8 1.2 copy.84.mom_in_ref
  143.0 1.3 copy.85.mom_dec_ref
  145.8 1.0 broadcast_in_dim.39.keep_ref
  146.9 105.9 %shard_map.307 = (bf16[24,48,2048]{2,1,0:T(8,128)(2,1)}, bf16[24,48,2048]{2,1,0:T(8,128)(2,1)}, f32[24,4,48,1024]{3,2,1,0:T(8,128)}, f32[24,48,1024]{2,1,0:T(8,128)}, f32[24,48,1024]{2,1,0:T(8,128)}) custom-call(bf16[24,48,128]{2,1,0:T(8,128)(2,1)} %maximum_maximum_fusion.1.emb_ref, f32[24,48,128]{2,1,0:T(8,128)} %broadcast_in_dim.39.keep_ref, ...), custom_call_target="tpu_custom_call" | custom-call | flops 20535312384 | bytes 524288000 | tf_op jit(solution)/shard_map/pallas_call | solution.py:577
  252.8 1.6 pad.8.dec_ref
  254.4 15.9 %shard_map.308 = (f32[1152,1024]{1,0:T(8,128)}, bf16[288,2048]{1,0:T(8,128)(2,1)}, f32[8,384]{1,0:T(8,128)S(1)}, bf16[192,2048]{1,0:T(8,128)(2,1)S(1)}) custom-call(bf16[24,48,2048]{2,1,0:T(8,128)(2,1)} %get-tuple-element.57.out_ref, s32[1152,1]{1,0:T(8,128)S(1)} %reshape.75.target_ref, bf16[2048,384]{1,0:T(8,128)(2,1)S(1)} %pad.8.dec_ref, ...), custom_call_target="tpu_custom_call" | custom-call | tf_op jit(solution)/shard_map/pallas_call | solution.py:1485
  271.3 1.6 collective-permute-start
  273.8 91.5 %shard_map.309 = (bf16[24,48,4096]{2,1,0:T(8,128)(2,1)}, f32[24,2048]{1,0:T(8,128)}, f32[24,2048]{1,0:T(8,128)}) custom-call(f32[24,48,1024]{2,1,0:T(8,128)} %bitcast.50, f32[24,4,48,1024]{3,2,1,0:T(8,128)} %get-tuple-element.60.gates_ref, f32[24,48,1024]{2,1,0:T(8,128)} %get-tuple-element.61.cell_ref, f32[24,48,1024]{2,1,0:T(8,128)} %get-tuple-element.62.ckept_ref, ...), custom_call_target="tpu_custom_call" | custom-call | flops 19327352832 | bytes 524288000 | tf_op jit(solution)/shard_map/pallas_call | solution.py:757
  366.0 1.5 maximum_select_fusion
  367.6 1.7 constant_dynamic-slice_fusion.2.dec_ref
  369.3 254.7 %shard_map.310 = (bf16[2,512,4096]{2,1,0:T(8,128)(2,1)}, bf16[128,2048]{1,0:T(8,128)(2,1)}, f32[288,128]{1,0:T(8,128)}, f32[8,128]{1,0:T(8,128)}) custom-call(bf16[1152,2048]{1,0:T(8,128)(2,1)} %bitcast.53, bf16[1152,128]{1,0:T(8,128)(2,1)} %bitcast.41, bf16[1152,4096]{1,0:T(8,128)(2,1)} %bitcast.52, bf16[128,4096]{1,0:T(8,128)(2,1)} %get-tuple-element.65.in_ref, ...), custom_call_target="tpu_custom_call" | custom-call | flops 19327352832 | bytes 734003200 | tf_op jit(solution)/shard_map/pallas_call | solution.py:1338
  624.0 22.5 %shard_map.311 = (f32[1,512,8192]{2,1,0:T(8,128)}, f32[1,512,8192]{2,1,0:T(8,128)}, f32[1,128]{1,0:T(1,128)}, f32[1,100,2048]{2,1,0:T(8,128)}, f32[1,100,2048]{2...) custom-call(f32[8,128]{1,0:T(8,128)} %get-tuple-element.68.clip_ref,, ...), custom_call_target="tpu_custom_call" | custom-call | tf_op jit(solution)/shard_map/pallas_call | solution.py:1575
  646.6 3.0 copy.88
  649.6 2.9 copy.91
  652.5 2.0 copy.89
  654.5 1.1 copy.92
  (61 shorter events, 10.9 us)
Async XLA Ops:
  7.2 245.6 %all-gather.3.cloned.1.call-start = ((), (), s32[]{:S(2)}) async-start(), calls=%async_computation.1 | async-start | bytes 1966080 | tf_op jit(solution)/shard_map/all_gather | solution.py:1623
  9.3 358.3 %all-reduce.4.cloned.1.call-start = ((), (), s32[]{:S(2)}) async-start(), calls=%async_computation | async-start | bytes 2359296 | tf_op jit(solution)/shard_map/psum | solution.py:1690
  14.6 125.2 %copy-start.8 = (f32[1,275,100]{2,0,1:T(1,128)S(1)}, f32[1,275,100]{2,0,1:T(1,128)}, u32[]{:S(2)}) copy-start(f32[1,275,100]{2,0,1:T(1,128)} %param.26) | copy-start | bytes 330004
  14.6 127.2 %copy-start.1 = (f32[1,100,2048]{2,0,1:T(1,128)S(1)}, f32[1,100,2048]{2,0,1:T(1,128)}, u32[]{:S(2)}) copy-start(f32[1,100,2048]{2,0,1:T(1,128)} %param.33) | copy-start | bytes 2457604
  14.6 128.4 %copy-start.3 = (f32[1,512,275]{1,0,2:T(1,128)S(1)}, f32[1,512,275]{1,0,2:T(1,128)}, u32[]{:S(2)}) copy-start(f32[1,512,275]{1,0,2:T(1,128)} %param.36) | copy-start | bytes 1689604
  137.9 6.5 copy-start.9
  137.9 7.9 %copy-start.10 = (f32[1,275]{1,0:T(1,128)S(1)}, f32[1,275]{1,0:T(1,128)}, u32[]{:S(2)}) copy-start(f32[1,275]{1,0:T(1,128)} %param.31) | copy-start | bytes 3304
  146.9 107.5 %copy-start = (bf16[384,1024]{1,0:T(8,128)(2,1)S(1)}, bf16[384,1024]{1,0:T(8,128)(2,1)}, u32[]{:S(2)}) copy-start(bf16[384,1024]{1,0:T(8,128)(2,1)} %get-tuple-element.58.wg_ref) | copy-start | bytes 2359300
  271.3 94.7 %collective-permute-start = (bf16[24,4,2048]{2,1,0:T(4,128)(2,1)S(1)}, bf16[24,4,2048]{2,1,0:T(4,128)(2,1)S(1)}, u32[]{:S(2)}, u32[]{:S(2)}) collective-permute-start(bf16[24,4,2048]{2,1,0:T(4,128)(2,1)S(1)} %get-tuple-element.137), channel_id=1, source_target_pairs={{0,16},{16,0},{1,17},{17,1},{2,18},{18,2},{3,19},{19,3},{4,20},{20... | collective-permute-start | bytes 1179656 | tf_op jit(solution)/shard_map/ppermute | solution.py:17
  646.5 8.0 %copy-start.2 = (f32[1,512,275]{2,1,0:T(8,128)S(1)}, f32[1,512,275]{2,1,0:T(8,128)}, u32[]{:S(2)}) copy-start(f32[1,512,275]{2,1,0:T(8,128)} %get-tuple-element.134) | copy-start | bytes 1689604
  646.5 9.1 %copy-start.7 = (f32[1,275,100]{2,1,0:T(8,128)S(1)}, f32[1,275,100]{2,1,0:T(8,128)}, u32[]{:S(2)}) copy-start(f32[1,275,100]{2,1,0:T(8,128)} %get-tuple-element.124) | copy-start | bytes 330004
  646.5 9.9 %copy-start.6 = (f32[1,275,100]{2,1,0:T(8,128)S(1)}, f32[1,275,100]{2,1,0:T(8,128)}, u32[]{:S(2)}) copy-start(f32[1,275,100]{2,1,0:T(8,128)} %get-tuple-element.130) | copy-start | bytes 330004
  646.6 10.7 %copy-start.5 = (f32[24,2048]{1,0:T(8,128)S(1)}, f32[24,2048]{1,0:T(8,128)}, u32[]{:S(2)}) copy-start(f32[24,2048]{1,0:T(8,128)} %get-tuple-element.74) | copy-start | bytes 589828
  646.6 11.3 %copy-start.4 = (f32[24,2048]{1,0:T(8,128)S(1)}, f32[24,2048]{1,0:T(8,128)}, u32[]{:S(2)}) copy-start(f32[24,2048]{1,0:T(8,128)} %get-tuple-element.75) | copy-start | bytes 589828
Sparse Core Ops, SparseCore 0:
  10.1 30.7 all-gather.2
  273.9 93.6 all-reduce.3

commit v6 on v5

--- a/solution.py
+++ b/solution.py
@@ -1053,7 +1053,13 @@
 
     def send(row):
         parity, index = lax.rem(row // lot, 2), lax.rem(row, lot)
-        for slot in list(range(2, peers)) + [1]:
+        if chips > 1:
+
+            @pl.when(row > 0)
+            def _():
+                send_block(2, parity, index, row).start()
+
+        for slot in list(range(3, peers)) + [1]:
             send_block(slot, parity, index, row).start()
 
     def take(row):
@@ -1239,6 +1245,12 @@
             @pl.when(b < batches)
             def _():
                 block(turn, b, parity)
+
+            if turn == 0 and chips > 1:
+
+                @pl.when(b == 0)
+                def _():
+                    send_block(2, 0, 0, 0).start()
 
             def step(j, inner):
                 sent = b * lot + turn * per_pass + j - lead
@@ -1536,36 +1548,47 @@
     grad_ref[0] = gradient
     next_ref[0] = momentum_step(moment_ref[0], gradient, clip)
 
-    @pl.when(jnp.logical_and(pl.program_id(0) == 0, pl.program_id(1) == 0))
+    index = (pl.program_id(0) * pl.num_programs(1) + pl.program_id(1)) * pl.num_programs(2)
+    index = index + pl.program_id(2)
+    embed = mom_in_ref.shape[0]
+    vocab = mom_emb_ref.shape[0]
+
+    def turned():
+        return jnp.transpose(emb_ref[...])
+
+    results = [
+        (lambda: in_ref[...].astype(jnp.float32)[:embed], mom_in_ref),
+        (lambda: in_ref[...].astype(jnp.float32)[embed : embed + 1], mom_bias_ref),
+        (lambda: dec_ref[...].astype(jnp.float32)[:vocab], mom_dec_ref),
+        (lambda: emb_ref[:vocab, :embed], mom_emb_ref),
+        (lambda: turned()[embed : embed + 1, :vocab], mom_dbias_ref),
+    ]
+
+    @pl.when(index == 0)
     def _():
-        embed = mom_in_ref.shape[1]
-        vocab = mom_emb_ref.shape[1]
-        emb = emb_ref[...]
-        turned = jnp.transpose(emb)
-        dec = jnp.transpose(dec_ref[...].astype(jnp.float32))
-        small[0][...] = turned[embed + 1 : embed + 2, :128] / count
-        results = [
-            (in_ref[:embed].astype(jnp.float32), mom_in_ref[0]),
-            (in_ref[embed : embed + 1].astype(jnp.float32), mom_bias_ref[...]),
-            (dec[:, :vocab], mom_dec_ref[0]),
-            (emb[:vocab, :embed], mom_emb_ref[0]),
-            (turned[embed : embed + 1, :vocab], mom_dbias_ref[...]),
-        ]
-        for k, (value, moment) in enumerate(results):
-            shape = small[1 + 2 * k].shape
-            small[1 + 2 * k][...] = value.reshape(shape)
-            small[2 + 2 * k][...] = momentum_step(moment, value, clip).reshape(shape)
+        small[0][...] = turned()[embed + 1 : embed + 2, :128] / count
+
+    def one(k, value_of, moment):
+        @pl.when(index == k + 1)
+        def _():
+            value = value_of().reshape(moment.shape)
+            small[1 + 2 * k][...] = value
+            small[2 + 2 * k][...] = momentum_step(moment[...], value, clip)
+
+    for k, (value_of, moment) in enumerate(results):
+        one(k, value_of, moment)
 
 
 def run_update(count, clip, sums, in_sum, emb_sum, dec_sum, moments):
     mom_rec, mom_in, mom_bias, mom_dec, mom_emb, mom_dbias = moments
     halves, rows, wide = sums.shape
     span = wide // 4
-    block = pl.BlockSpec((1, rows, span), lambda q, s: (0, 0, 2 * q + s))
+    tall = rows
+    block = pl.BlockSpec((1, tall, span), lambda q, s, r: (0, r, 2 * q + s))
     f32 = jnp.float32
 
     def fixed(shape):
-        return pl.BlockSpec(shape, lambda q, s: (0,) * len(shape))
+        return pl.BlockSpec(shape, lambda q, s, r: (0,) * len(shape))
 
     rec_shape = jax.ShapeDtypeStruct(mom_rec.shape, f32)
     small = [mom_in, mom_bias, mom_dec, mom_emb, mom_dbias]
@@ -1574,10 +1597,10 @@
         shapes += [moment.shape, moment.shape]
     return pl.pallas_call(
         functools.partial(update_kernel, count),
-        grid=(4, 2),
+        grid=(4, 2, 1),
         in_specs=[
             pl.BlockSpec(memory_space=pltpu.SMEM),
-            pl.BlockSpec((1, rows, span), lambda q, s: (s, 0, q)),
+            pl.BlockSpec((1, tall, span), lambda q, s, r: (s, r, q)),
             block,
         ]
         + [fixed(x.shape) for x in (in_sum, emb_sum, dec_sum, *small)],
@@ -1737,7 +1760,14 @@
         in_out,
         emb_out,
         dec_sum,
-        (mom_rec, mom_in, mom_bias, mom_dec, mom_emb, mom_dbias),
+        (
+            mom_rec,
+            jnp.transpose(mom_in, (1, 0, 2)),
+            mom_bias,
+            jnp.transpose(mom_dec, (2, 0, 1)),
+            jnp.transpose(mom_emb, (1, 0, 2)),
+            mom_dbias,
+        ),
     )
     grad_in, next_in, grad_bias, next_bias, grad_dec, next_dec = small[:6]
     grad_emb, next_emb, grad_dbias, next_dbias = small[6:]
@@ -1746,17 +1776,17 @@
         word_vectors,
         grad_hidden0[None],
         grad_cell0[None],
-        grad_emb,
-        grad_in,
+        jnp.transpose(grad_emb, (1, 0, 2)),
+        jnp.transpose(grad_in, (1, 0, 2)),
         grad_rec,
         grad_bias,
-        grad_dec,
+        jnp.transpose(grad_dec, (1, 2, 0)),
         grad_dbias,
-        next_emb,
-        next_in,
+        jnp.transpose(next_emb, (1, 0, 2)),
+        jnp.transpose(next_in, (1, 0, 2)),
         next_rec,
         next_bias,
-        next_dec,
+        jnp.transpose(next_dec, (1, 2, 0)),
         next_dbias,
     )
 

time: 666 us -> 649 us (0.974)
  local copies, waits for them, and re-layouts: 29.4 us -> 15.5 us
    unnamed x36 -> x15, local copies, waits for them, and re-layouts: 18.5 us -> 4.61 us
  transfers between devices with their start and end apart: 3 -> 3, of which waited for: 0 -> 0; matrix products, arithmetic and copies ran while one was open for 3% -> 2% of each run, Pallas kernels for 48% -> 49%
where the time goes in v6:
time: 649 us; the launch traced here: 648 us
  Pallas kernels  611 us (94%)
  local copies, waits for them, and re-layouts  15.5 us (2%)
  between operations  14.2 us (2%)
    pallas_call x1, Pallas kernels, run_reduce(): pl.pallas_call(functools.partial(reduce_kernel, chips, depth, embed), in_...  252 us
    pallas_call x1, Pallas kernels, run_gather(): pl.pallas_call(functools.partial(gather_kernel, chips, shared), in_specs=...  123 us
    pallas_call x1, Pallas kernels, run_forward(): pl.pallas_call(functools.partial(forward_kernel, steps), grid=(steps + 1,...  106 us
    pallas_call x1, Pallas kernels, run_backward(): pl.pallas_call(functools.partial(backward_kernel, steps), grid=(steps,),...  91.5 us
    pallas_call x1, Pallas kernels, run_update(): pl.pallas_call(functools.partial(update_kernel, count), grid=(4, 2, 1), i...  22.1 us
    pallas_call x1, Pallas kernels, run_middle(): pl.pallas_call(functools.partial(middle_kernel, vocab, steps), grid=(step...  15.9 us
  transfers between devices with their start and end apart: 3, of which 0 were waited for; matrix products, arithmetic and copies ran while one was open for 2% of the time, Pallas kernels for 49%

profile of v6, /device:TPU:0, one launch (start us, length us, event | category | flops | bytes accessed | tf_op | source)
XLA Modules:
  0.0 648.4 jit_solution(464663659009134555)
XLA Ops:
  7.2 1.1 copy.75
  8.3 0.9 copy.60
  9.3 1.4 copy.76
  10.7 0.7 convert.10
  11.4 0.8 copy.55
  12.2 0.9 maximum_maximum_fusion.inb_ref
  13.2 1.4 concatenate.20.ids_ref
  14.6 123.2 %shard_map.306 = (bf16[2176,4096]{1,0:T(8,128)(2,1)}, bf16[4096,2048]{1,0:T(8,128)(2,1)}, f32[48,2048]{1,0:T(8,128)}, f32[48,1024]{1,0:T(8,128)}, bf16[384,1024]...) custom-call(f32[512,8192]{1,0:T(8,128)} %bitcast.46, bf16[128,2048]{1,0:T(8,128)(2,1)} %maximum_maximum_fusion.inb_ref, ...), custom_call_target="tpu_custom_call" | custom-call | bytes 419430400 | tf_op jit(solution)/shard_map/pallas_call | solution.py:407
  137.8 0.9 slice_bitcast_fusion
  138.7 0.8 slice.24
  141.7 0.8 maximum_maximum_fusion.1.emb_ref
  142.5 1.0 broadcast_in_dim.39.keep_ref
  143.6 105.8 %shard_map.307 = (bf16[24,48,2048]{2,1,0:T(8,128)(2,1)}, bf16[24,48,2048]{2,1,0:T(8,128)(2,1)}, f32[24,4,48,1024]{3,2,1,0:T(8,128)}, f32[24,48,1024]{2,1,0:T(8,128)}, f32[24,48,1024]{2,1,0:T(8,128)}) custom-call(bf16[24,48,128]{2,1,0:T(8,128)(2,1)} %maximum_maximum_fusion.1.emb_ref, f32[24,48,128]{2,1,0:T(8,128)} %broadcast_in_dim.39.keep_ref, ...), custom_call_target="tpu_custom_call" | custom-call | flops 20535312384 | bytes 524288000 | tf_op jit(solution)/shard_map/pallas_call | solution.py:577
  249.4 1.6 pad.8.dec_ref
  251.0 15.9 %shard_map.308 = (f32[1152,1024]{1,0:T(8,128)}, bf16[288,2048]{1,0:T(8,128)(2,1)}, f32[8,384]{1,0:T(8,128)S(1)}, bf16[192,2048]{1,0:T(8,128)(2,1)S(1)}) custom-call(bf16[24,48,2048]{2,1,0:T(8,128)(2,1)} %get-tuple-element.57.out_ref, s32[1152,1]{1,0:T(8,128)S(1)} %reshape.75.target_ref, bf16[2048,384]{1,0:T(8,128)(2,1)S(1)} %pad.8.dec_ref, ...), custom_call_target="tpu_custom_call" | custom-call | tf_op jit(solution)/shard_map/pallas_call | solution.py:1497
  268.0 1.6 collective-permute-start
  269.7 0.7 pad.16.clone
  270.4 91.5 %shard_map.309 = (bf16[24,48,4096]{2,1,0:T(8,128)(2,1)}, f32[24,2048]{1,0:T(8,128)}, f32[24,2048]{1,0:T(8,128)}) custom-call(f32[24,48,1024]{2,1,0:T(8,128)} %bitcast.62, f32[24,4,48,1024]{3,2,1,0:T(8,128)} %get-tuple-element.60.gates_ref, f32[24,48,1024]{2,1,0:T(8,128)} %get-tuple-element.61.cell_ref, f32[24,48,1024]{2,1,0:T(8,128)} %get-tuple-element.62.ckept_ref, ...), custom_call_target="tpu_custom_call" | custom-call | flops 19327352832 | bytes 524288000 | tf_op jit(solution)/shard_map/pallas_call | solution.py:757
  361.9 0.8 maximum_maximum_fusion.2.extra_ref
  362.7 1.5 maximum_select_fusion
  364.2 1.7 constant_dynamic-slice_fusion.2.dec_ref
  365.9 252.1 %shard_map.310 = (bf16[2,512,4096]{2,1,0:T(8,128)(2,1)}, bf16[128,2048]{1,0:T(8,128)(2,1)}, f32[288,128]{1,0:T(8,128)}, f32[8,128]{1,0:T(8,128)}) custom-call(bf16[1152,2048]{1,0:T(8,128)(2,1)} %bitcast.71, bf16[1152,128]{1,0:T(8,128)(2,1)} %bitcast.52, bf16[1152,4096]{1,0:T(8,128)(2,1)} %bitcast.70, bf16[128,4096]{1,0:T(8,128)(2,1)} %get-tuple-element.65.in_ref, ...), custom_call_target="tpu_custom_call" | custom-call | flops 19327352832 | bytes 734003200 | tf_op jit(solution)/shard_map/pallas_call | solution.py:1350
  618.0 22.1 %shard_map.311 = (f32[1,512,8192]{2,1,0:T(8,128)}, f32[1,512,8192]{2,1,0:T(8,128)}, f32[1,128]{1,0:T(1,128)}, f32[100,1,2048]{2,1,0:T(1,128)}, f32[100,1,2048]{2...) custom-call(f32[8,128]{1,0:T(8,128)} %get-tuple-element.68.clip_ref,, ...), custom_call_target="tpu_custom_call" | custom-call | tf_op jit(solution)/shard_map/pallas_call | solution.py:1598
  640.2 0.7 copy.80
  (40 shorter events, 4.2 us)
Async XLA Ops:
  7.2 242.3 %all-gather.3.cloned.1.call-start = ((), (), s32[]{:S(2)}) async-start(), calls=%async_computation.1 | async-start | bytes 1966080 | tf_op jit(solution)/shard_map/all_gather | solution.py:1646
  9.3 354.9 %all-reduce.4.cloned.1.call-start = ((), (), s32[]{:S(2)}) async-start(), calls=%async_computation | async-start | bytes 2359296 | tf_op jit(solution)/shard_map/psum | solution.py:1713
  14.6 125.1 %copy-start.3 = (f32[1,275,100]{2,0,1:T(1,128)S(1)}, f32[1,275,100]{2,0,1:T(1,128)}, u32[]{:S(2)}) copy-start(f32[1,275,100]{2,0,1:T(1,128)} %param.26) | copy-start | bytes 330004
  14.6 127.9 %copy-start.4 = (f32[1,275]{1,0:T(1,128)S(1)}, f32[1,275]{1,0:T(1,128)}, u32[]{:S(2)}) copy-start(f32[1,275]{1,0:T(1,128)} %param.31) | copy-start | bytes 3304
  143.6 107.5 %copy-start = (bf16[384,1024]{1,0:T(8,128)(2,1)S(1)}, bf16[384,1024]{1,0:T(8,128)(2,1)}, u32[]{:S(2)}) copy-start(bf16[384,1024]{1,0:T(8,128)(2,1)} %get-tuple-element.58.wg_ref) | copy-start | bytes 2359300
  268.0 94.7 %collective-permute-start = (bf16[24,4,2048]{2,1,0:T(4,128)(2,1)S(1)}, bf16[24,4,2048]{2,1,0:T(4,128)(2,1)S(1)}, u32[]{:S(2)}, u32[]{:S(2)}) collective-permute-start(bf16[24,4,2048]{2,1,0:T(4,128)(2,1)S(1)} %get-tuple-element.89), channel_id=1, source_target_pairs={{0,16},{16,0},{1,17},{17,1},{2,18},{18,2},{3,19},{19,3},{4,20},{20... | collective-permute-start | bytes 1179656 | tf_op jit(solution)/shard_map/ppermute | solution.py:17
  618.0 22.2 %copy-start.2 = (f32[24,2048]{1,0:T(8,128)S(1)}, f32[24,2048]{1,0:T(8,128)}, u32[]{:S(2)}) copy-start(f32[24,2048]{1,0:T(8,128)} %get-tuple-element.74) | copy-start | bytes 589828
  618.0 22.8 %copy-start.1 = (f32[24,2048]{1,0:T(8,128)S(1)}, f32[24,2048]{1,0:T(8,128)}, u32[]{:S(2)}) copy-start(f32[24,2048]{1,0:T(8,128)} %get-tuple-element.75) | copy-start | bytes 589828
Sparse Core Ops, SparseCore 0:
  10.1 30.7 all-gather.2
  270.5 93.5 all-reduce.3

commit v7 on v6

--- a/solution.py
+++ b/solution.py
@@ -1196,7 +1196,7 @@
         send_partial(emb_mine, emb_part, emb_final, emb_sems)
 
     lead = (peers - 2) * per_pass
-    y_lag, hop_lag, settle_lag = 3, 2, 6
+    y_lag, hop_lag, settle_lag = 3, 1, 6
     hops = jnp.where(low, middle - z, z - middle)
     most_hops = max(middle, depth - 1 - middle)
     before = groups // 2
@@ -1643,7 +1643,8 @@
     depth = 128
     vocab_lanes = -(-vocab_size // 128) * 128
     vocab_rows = -(-vocab_size // 32) * 32
-    dec_full = lax.all_gather(w_dec[0].astype(jnp.bfloat16), "group", axis=0, tiled=True)
+    dec_own = jnp.pad(w_dec[0].astype(jnp.bfloat16), ((0, 0), (0, vocab_lanes - vocab_size)))
+    dec_full = lax.all_gather(dec_own, "group", axis=0, tiled=True)
     in_bias = jnp.concatenate(
         [w_in[0], b_rec, jnp.zeros((depth - embed_size - 1, w_in.shape[2]), jnp.float32)]
     ).astype(jnp.bfloat16)
@@ -1704,7 +1705,7 @@
         vocab_size,
         out_all,
         jnp.transpose(targets2).reshape(positions, 1),
-        jnp.pad(dec_full, ((0, 0), (0, vocab_lanes - vocab_size))),
+        dec_full,
         jnp.pad(b_dec, ((0, 0), (0, vocab_lanes - vocab_size)), constant_values=-1e30),
         word_pos2.reshape(1, 2 * batch_size * word_slots),
         word_pos[0].reshape(batch_size * word_slots, 1),

time: 649 us -> 709 us (1.092)
  Pallas kernels: 611 us -> 670 us
    pallas_call x1, Pallas kernels: 252 us -> 312 us  [run_reduce(): pl.pallas_call(functools.partial(reduce_kernel, chips, depth, embed), in_...]
  transfers between devices with their start and end apart: 3 -> 3, of which waited for: 0 -> 0; matrix products, arithmetic and copies ran while one was open for 2% -> 2% of each run, Pallas kernels for 49% -> 45%
where the time goes in v7:
time: 709 us; the launch traced here: 708 us
  Pallas kernels  670 us (94%)
  local copies, waits for them, and re-layouts  15.4 us (2%)
  between operations  14.2 us (2%)
    pallas_call x1, Pallas kernels, run_reduce(): pl.pallas_call(functools.partial(reduce_kernel, chips, depth, embed), in_...  312 us
    pallas_call x1, Pallas kernels, run_gather(): pl.pallas_call(functools.partial(gather_kernel, chips, shared), in_specs=...  123 us
    pallas_call x1, Pallas kernels, run_forward(): pl.pallas_call(functools.partial(forward_kernel, steps), grid=(steps + 1,...  106 us
    pallas_call x1, Pallas kernels, run_backward(): pl.pallas_call(functools.partial(backward_kernel, steps), grid=(steps,),...  91.5 us
    pallas_call x1, Pallas kernels, run_update(): pl.pallas_call(functools.partial(update_kernel, count), grid=(4, 2, 1), i...  22.1 us
    pallas_call x1, Pallas kernels, run_middle(): pl.pallas_call(functools.partial(middle_kernel, vocab, steps), grid=(step...  15.9 us
  transfers between devices with their start and end apart: 3, of which 0 were waited for; matrix products, arithmetic and copies ran while one was open for 2% of the time, Pallas kernels for 45%

profile of v7, /device:TPU:0, one launch (start us, length us, event | category | flops | bytes accessed | tf_op | source)
XLA Modules:
  0.0 707.9 jit_solution(5554364042009832422)
XLA Ops:
  7.2 1.3 copy.48
  8.6 0.8 pad.8
  9.4 1.4 copy.62
  10.8 0.7 convert.10
  11.5 0.8 copy.44
  12.4 0.9 maximum_maximum_fusion.inb_ref
  13.3 1.4 concatenate.20.ids_ref
  14.7 123.2 %shard_map.306 = (bf16[2176,4096]{1,0:T(8,128)(2,1)}, bf16[4096,2048]{1,0:T(8,128)(2,1)}, f32[48,2048]{1,0:T(8,128)}, f32[48,1024]{1,0:T(8,128)}, bf16[384,1024]...) custom-call(f32[512,8192]{1,0:T(8,128)} %bitcast.48, bf16[128,2048]{1,0:T(8,128)(2,1)} %maximum_maximum_fusion.inb_ref, ...), custom_call_target="tpu_custom_call" | custom-call | bytes 419430400 | tf_op jit(solution)/shard_map/pallas_call | solution.py:407
  137.9 0.9 slice_bitcast_fusion
  138.8 0.8 slice.24
  141.8 0.8 maximum_maximum_fusion.1.emb_ref
  142.6 1.0 broadcast_in_dim.39.keep_ref
  143.7 105.8 %shard_map.307 = (bf16[24,48,2048]{2,1,0:T(8,128)(2,1)}, bf16[24,48,2048]{2,1,0:T(8,128)(2,1)}, f32[24,4,48,1024]{3,2,1,0:T(8,128)}, f32[24,48,1024]{2,1,0:T(8,128)}, f32[24,48,1024]{2,1,0:T(8,128)}) custom-call(bf16[24,48,128]{2,1,0:T(8,128)(2,1)} %maximum_maximum_fusion.1.emb_ref, f32[24,48,128]{2,1,0:T(8,128)} %broadcast_in_dim.39.keep_ref, ...), custom_call_target="tpu_custom_call" | custom-call | flops 20535312384 | bytes 524288000 | tf_op jit(solution)/shard_map/pallas_call | solution.py:577
  249.6 1.4 copy-done
  251.0 15.9 %shard_map.308 = (f32[1152,1024]{1,0:T(8,128)}, bf16[288,2048]{1,0:T(8,128)(2,1)}, f32[8,384]{1,0:T(8,128)S(1)}, bf16[192,2048]{1,0:T(8,128)(2,1)S(1)}) custom-call(bf16[24,48,2048]{2,1,0:T(8,128)(2,1)} %get-tuple-element.57.out_ref, s32[1152,1]{1,0:T(8,128)S(1)} %reshape.74.target_ref, bf16[2048,384]{1,0:T(8,128)(2,1)S(1)} %copy-done, ...), custom_call_target="tpu_custom_call" | custom-call | tf_op jit(solution)/shard_map/pallas_call | solution.py:1497
  267.9 1.6 collective-permute-start
  269.6 0.7 pad.16.clone
  270.3 91.5 %shard_map.309 = (bf16[24,48,4096]{2,1,0:T(8,128)(2,1)}, f32[24,2048]{1,0:T(8,128)}, f32[24,2048]{1,0:T(8,128)}) custom-call(f32[24,48,1024]{2,1,0:T(8,128)} %bitcast.64, f32[24,4,48,1024]{3,2,1,0:T(8,128)} %get-tuple-element.60.gates_ref, f32[24,48,1024]{2,1,0:T(8,128)} %get-tuple-element.61.cell_ref, f32[24,48,1024]{2,1,0:T(8,128)} %get-tuple-element.62.ckept_ref, ...), custom_call_target="tpu_custom_call" | custom-call | flops 19327352832 | bytes 524288000 | tf_op jit(solution)/shard_map/pallas_call | solution.py:757
  361.8 0.8 maximum_maximum_fusion.2.extra_ref
  362.6 1.5 maximum_select_fusion
  364.1 1.7 constant_dynamic-slice_fusion.2.dec_ref
  365.8 311.7 %shard_map.310 = (bf16[2,512,4096]{2,1,0:T(8,128)(2,1)}, bf16[128,2048]{1,0:T(8,128)(2,1)}, f32[288,128]{1,0:T(8,128)}, f32[8,128]{1,0:T(8,128)}) custom-call(bf16[1152,2048]{1,0:T(8,128)(2,1)} %bitcast.73, bf16[1152,128]{1,0:T(8,128)(2,1)} %bitcast.54, bf16[1152,4096]{1,0:T(8,128)(2,1)} %bitcast.72, bf16[128,4096]{1,0:T(8,128)(2,1)} %get-tuple-element.65.in_ref, ...), custom_call_target="tpu_custom_call" | custom-call | flops 19327352832 | bytes 734003200 | tf_op jit(solution)/shard_map/pallas_call | solution.py:1350
  677.6 22.1 %shard_map.311 = (f32[1,512,8192]{2,1,0:T(8,128)}, f32[1,512,8192]{2,1,0:T(8,128)}, f32[1,128]{1,0:T(1,128)}, f32[100,1,2048]{2,1,0:T(1,128)}, f32[100,1,2048]{2...) custom-call(f32[8,128]{1,0:T(8,128)} %get-tuple-element.68.clip_ref,, ...), custom_call_target="tpu_custom_call" | custom-call | tf_op jit(solution)/shard_map/pallas_call | solution.py:1598
  699.7 0.7 copy.66
  (41 shorter events, 4.2 us)
Async XLA Ops:
  7.2 242.4 %all-gather.2.cloned.1.call-start = ((), (), s32[]{:S(2)}) async-start(), calls=%async_computation | async-start | bytes 1966080 | tf_op jit(solution)/shard_map/all_gather | solution.py:1647
  9.4 354.8 %all-reduce.4.cloned.1.call-start = ((), (), s32[]{:S(2)}) async-start(), calls=%async_computation.1 | async-start | bytes 2359296 | tf_op jit(solution)/shard_map/psum | solution.py:1714
  14.7 125.1 %copy-start.4 = (f32[1,275,100]{2,0,1:T(1,128)S(1)}, f32[1,275,100]{2,0,1:T(1,128)}, u32[]{:S(2)}) copy-start(f32[1,275,100]{2,0,1:T(1,128)} %param.26) | copy-start | bytes 330004
  14.7 126.6 %copy-start.5 = (f32[1,275]{1,0:T(1,128)S(1)}, f32[1,275]{1,0:T(1,128)}, u32[]{:S(2)}) copy-start(f32[1,275]{1,0:T(1,128)} %param.31) | copy-start | bytes 3304
  143.7 105.9 %copy-start.1 = (bf16[384,1024]{1,0:T(8,128)(2,1)S(1)}, bf16[384,1024]{1,0:T(8,128)(2,1)}, u32[]{:S(2)}) copy-start(bf16[384,1024]{1,0:T(8,128)(2,1)} %get-tuple-element.58.wg_ref) | copy-start | bytes 2359300
  249.6 1.4 copy-start
  267.9 94.7 %collective-permute-start = (bf16[24,4,2048]{2,1,0:T(4,128)(2,1)S(1)}, bf16[24,4,2048]{2,1,0:T(4,128)(2,1)S(1)}, u32[]{:S(2)}, u32[]{:S(2)}) collective-permute-start(bf16[24,4,2048]{2,1,0:T(4,128)(2,1)S(1)} %get-tuple-element.89), channel_id=1, source_target_pairs={{0,16},{16,0},{1,17},{17,1},{2,18},{18,2},{3,19},{19,3},{4,20},{20... | collective-permute-start | bytes 1179656 | tf_op jit(solution)/shard_map/ppermute | solution.py:17
  677.6 22.2 %copy-start.3 = (f32[24,2048]{1,0:T(8,128)S(1)}, f32[24,2048]{1,0:T(8,128)}, u32[]{:S(2)}) copy-start(f32[24,2048]{1,0:T(8,128)} %get-tuple-element.74) | copy-start | bytes 589828
  677.6 22.8 %copy-start.2 = (f32[24,2048]{1,0:T(8,128)S(1)}, f32[24,2048]{1,0:T(8,128)}, u32[]{:S(2)}) copy-start(f32[24,2048]{1,0:T(8,128)} %get-tuple-element.75) | copy-start | bytes 589828
Sparse Core Ops, SparseCore 0:
  10.1 30.7 all-gather.1
  270.5 93.5 all-reduce.3
